TPU v7x, 32 devices: a whole 2x2x4 slice. The times are simulated.
32 devices in a mesh: tm: 4 (over z), lon: 8 (over y, x, core).
Axes of the slice: x: 2, y: 2, z: 4, core: 2. Of those that a mesh axis runs over, the one named last changes fastest.
Arguments:
- noise: bfloat16 [2, 256, 1024, 512], P(None, 'tm', 'lon'), may hold values from -6 to 6
- observed: float32 [256, 256, 1024], P('tm', 'lon'), may hold values from -6 to 6
- mask: int32 [256, 256, 1024], P('tm', 'lon'), may hold values from 0 to 1, as said below
- lat_factor: bfloat16 [256, 256], replicated, as said below
- lon_factor: bfloat16 [1024, 1024], P('lon'), as said below
- spectrum: float32 [257], replicated, may hold values from 0.1 to 4
Outputs:
- posterior: float32 [2, 256, 256, 1024], P(None, 'tm', 'lon')
- residual_next: float32 [2, 256, 256, 1024], P(None, 'tm', 'lon')
Inputs may be any that keep to these rules, and one draw needn't show every extreme that they name: `mask`: 1 where the cell is observed, 0 elsewhere. `lat_factor`: lower triangular with a positive diagonal. `lon_factor`: lower triangular with a positive diagonal.
All inputs are finite; a program needn't handle non-finite values.
Results may differ from a plain program's by a relative error of at most 0.0026.
Values may be sent and summed in bfloat16 or wider, within the bound.
No kernel may reach another device: no remote copies, remote signals or barrier semaphores. Data moves between devices by JAX's collectives and lax.ppermute only.
A program may use at most 192 MiB of HBM per device.

v0:
```python
import jax
import jax.numpy as jnp
from jax import lax
from jax.sharding import PartitionSpec as P

PRECISE = lax.Precision.HIGHEST
NOISE_VAR = 0.25


def angle_tables(row_count, col_count, period):
    row_index = lax.broadcasted_iota(jnp.int32, (row_count, col_count), 0)
    col_index = lax.broadcasted_iota(jnp.int32, (row_count, col_count), 1)
    phase = (row_index * col_index % period).astype(jnp.float32) * (2.0 * jnp.pi / period)
    return (jnp.cos(phase), jnp.sin(phase))


def over_hours(tensor_in):
    return lax.all_to_all(tensor_in, "tm", split_axis=2, concat_axis=0, tiled=True)


def over_columns(tensor_in):
    return lax.all_to_all(tensor_in, "lon", split_axis=2, concat_axis=0, tiled=True)


def finish(hourly, lat_whole, lon_forward):
    samples, hours, lat_local, lon_local = hourly.shape
    arrived = over_hours(hourly.reshape(1, samples, hours, lat_local * lon_local))
    lat_parts = arrived.shape[0]
    hour_local = arrived.shape[2]
    arrived = arrived.reshape(lat_parts, samples, hour_local, lat_local, lon_local)
    lat_split = lat_whole.reshape(lat_whole.shape[0], lat_parts, lat_local)
    spread = jnp.einsum("acy,cstyx->satx", lat_split, arrived, precision=PRECISE)
    lat_count = spread.shape[1]
    arrived = over_columns(spread.reshape(1, samples, lat_count, hour_local * lon_local))
    lon_parts = arrived.shape[0]
    lat_rows = arrived.shape[2]
    arrived = arrived.reshape(lon_parts, samples, lat_rows, hour_local, lon_local)
    return lon_forward(arrived)


def shards(noise, observed, mask, lat_factor, lon_factor, spectrum):
    periods = noise.shape[3]
    hours = periods // 2
    powers = jnp.concatenate([spectrum, spectrum[1:-1][::-1]])
    amplitude = jnp.sqrt(powers / periods)
    cosine_tab, sine_tab = angle_tables(hours, periods, periods)
    table_cos = (cosine_tab * amplitude).astype(jnp.bfloat16)
    table_sin = (sine_tab * amplitude).astype(jnp.bfloat16)
    tables = jnp.stack([jnp.stack([table_cos, table_sin]), jnp.stack([-table_sin, table_cos])])
    hourly = jnp.einsum("cyxk,scjk->sjyx", noise, tables, preferred_element_type=jnp.float32)
    scaled = powers / periods
    hour_kernel = jnp.dot(cosine_tab * scaled, cosine_tab.T, precision=PRECISE) + jnp.dot(
        sine_tab * scaled, sine_tab.T, precision=PRECISE
    )
    lat_whole = lat_factor.astype(jnp.float32)

    def lon_forward(arrived):
        lon_parts = arrived.shape[0]
        lon_local = arrived.shape[4]
        factor_rows = lax.all_gather(lon_factor, "lon", axis=0, tiled=True)
        split_rows = factor_rows.astype(jnp.float32).reshape(
            factor_rows.shape[0], lon_parts, lon_local
        )
        return jnp.einsum("odx,dsltx->stlo", split_rows, arrived, precision=PRECISE)

    prior_draw = finish(hourly, lat_whole, lon_forward)
    observed_mask = mask.astype(jnp.float32)
    residual = observed_mask * (observed[None] - prior_draw)
    local_norm = jnp.sum(residual * residual, axis=(1, 2, 3))
    norm_sq = lax.psum(local_norm, ("tm", "lon"))
    backed = jnp.einsum(
        "ij,stli->sjtl",
        lax.all_gather(lon_factor, "lon", axis=0, tiled=True).astype(jnp.float32),
        residual,
        precision=PRECISE,
    )
    samples = backed.shape[0]
    lon_count = backed.shape[1]
    hour_local = backed.shape[2]
    lat_rows = backed.shape[3]
    arrived = over_columns(backed.reshape(1, samples, lon_count, hour_local * lat_rows))
    lat_parts = arrived.shape[0]
    lon_local = arrived.shape[2]
    arrived = arrived.reshape(lat_parts, samples, lon_local, hour_local, lat_rows)
    lat_split = lat_whole.reshape(lat_parts, lat_rows, lat_whole.shape[1])
    spread = jnp.einsum("clj,csxtl->sjxt", lat_split, arrived, precision=PRECISE)
    lat_count = spread.shape[1]
    arrived = over_hours(spread.reshape(1, samples, lat_count, lon_local * hour_local))
    hour_parts = arrived.shape[0]
    lat_local = arrived.shape[2]
    arrived = arrived.reshape(hour_parts, samples, lat_local, lon_local, hour_local)
    kernel_split = hour_kernel.reshape(hour_kernel.shape[0], hour_parts, hour_local)
    hourly_back = jnp.einsum("jdt,dsyxt->sjyx", kernel_split, arrived, precision=PRECISE)
    applied = finish(hourly_back, lat_whole, lon_forward)
    operated = observed_mask * applied + NOISE_VAR * residual
    local_bend = jnp.sum(residual * operated, axis=(1, 2, 3))
    bending = lax.psum(local_bend, ("tm", "lon"))
    step_size = (norm_sq / bending)[:, None, None, None]
    return (prior_draw + step_size * applied, residual - step_size * operated)


def solution(mesh):
    return jax.shard_map(
        shards,
        mesh=mesh,
        in_specs=(
            P(None, "tm", "lon", None),
            P("tm", "lon", None),
            P("tm", "lon", None),
            P(),
            P("lon", None),
            P(),
        ),
        out_specs=(P(None, "tm", "lon", None), P(None, "tm", "lon", None)),
        check_vma=False,
    )
```

profile of v0, /device:TPU:0, one launch (start us, length us, event | category | flops | bytes accessed | tf_op | source)
XLA Modules:
  0.0 2386.3 jit_solution(8307541084280037643)
XLA Ops:
  29.8 25.3 %copy.97 = f32[1,2,256,8192]{3,1,0,2:T(2,128)} copy(f32[1,2,256,8192]{2,3,1,0:T(8,128)} %bitcast.185) | data formatting | bytes 33554432 | tf_op jit(solution)/shard_map/reshape | solution.py:27
  62.7 364.4 %all-to-all-done = f32[1,2,256,8192]{3,1,0,2:T(2,128)} async-done(((f32[1,2,256,8192]{3,1,0,2:T(2,128)}), f32[1,2,256,8192]{3,1,0,2:T(2,128)}, u32[]{:S(2)}, u32[]{:S(2)}) %all-to-all-start) | async-done | bytes 16777248 | tf_op jit(solution)/shard_map/all_to_all | solution.py:18
  449.3 20.2 fusion.45
  469.6 25.3 %copy.101 = f32[1,2,256,8192]{3,1,0,2:T(2,128)} copy(f32[1,2,256,8192]{2,3,1,0:T(8,128)} %bitcast.174) | data formatting | bytes 33554432 | tf_op jit(solution)/shard_map/reshape | solution.py:34
  525.3 85.1 %all-gather.2.cloned.1.call-done = bf16[1024,1024]{1,0:T(8,128)(2,1)} async-done(((bf16[128,1024]{1,0:T(8,128)(2,1)}), bf16[1024,1024]{1,0:T(8,128)(2,1)}) %all-gather.2.cloned.1.call-update) | async-done | bytes 2097168 | tf_op jit(solution)/shard_map/all_gather | solution.py:60
  613.4 79.5 %all-to-all-done.1 = f32[1,2,256,8192]{3,1,0,2:T(2,128)} async-done(((f32[1,2,256,8192]{3,1,0,2:T(2,128)}), f32[1,2,256,8192]{3,1,0,2:T(2,128)}, u32[]{:S(2)}, u32[]{:S(2)}) %all-to-all-start.1) | async-done | bytes 16777248 | tf_op jit(solution)/shard_map/all_to_all | solution.py:22
  715.3 35.0 %fusion.4 = (f32[2,64,32,1024]{3,1,2,0:T(8,128)}, f32[2,32,64,1024,1]{3,2,1,4,0:T(8,128)}) fusion(f32[64,32,1024]{2,0,1:T(8,128)} %copy.107, f32[64,32,1024]{2,0,1:T(8,128)S(1)} %bitcast.165, f32[8,2,32,64,128]{4,3,2,0,1:T(8,128)} %bitcast.182, bf16[1024,8,128,1,1]{0,2,4,1,3:T(8,128)(2,1)S(1)} %bitcast.183), kind=kOutput, calls=%fused_computation.7 | convolution fusion | flops 51547996160 | bytes 69206016 | tf_op jit(solution)/shard_map/odx,dsltx->stlo/dot_general | solution.py:64
  750.2 41.9 %fusion.7 = f32[2,64,32,1024]{3,2,1,0:T(8,128)} fusion(f32[2,64,32,1024]{3,1,2,0:T(8,128)} %get-tuple-element.24, bf16[1024,1024]{1,0:T(8,128)(2,1)} %all-gather.2.cloned.1.call-done), kind=kOutput, calls=%fused_computation.10 | convolution fusion | flops 51539607552 | bytes 35651584 | tf_op jit(solution)/shard_map/ij,stli->sjtl/dot_general | solution.py:71
  792.1 25.4 %copy.109 = f32[1,2,1024,2048]{3,1,0,2:T(2,128)} copy(f32[1,2,1024,2048]{2,3,1,0:T(8,128)} %bitcast.186) | data formatting | bytes 33554432 | tf_op jit(solution)/shard_map/reshape | solution.py:81
  817.5 188.2 %all_to_all.90 = f32[1,2,1024,2048]{3,1,0,2:T(2,128)S(1)} all-to-all(f32[1,2,1024,2048]{3,1,0,2:T(2,128)} %copy.109), channel_id=1, replica_groups=mesh['tm'=4,'lon'=8] {'lon'}, dimensions={2} | all-to-all | bytes 33554432 | tf_op jit(solution)/shard_map/all_to_all | solution.py:22
  1005.7 19.9 copy.110
  1042.0 20.2 convolution_bitcast_fusion
  1080.2 25.3 %copy.114 = f32[1,2,256,8192]{3,1,0,2:T(2,128)} copy(f32[1,2,256,8192]{2,3,1,0:T(8,128)} %bitcast.178) | data formatting | bytes 33554432 | tf_op jit(solution)/shard_map/reshape | solution.py:88
  1117.7 357.3 %all-to-all-done.3 = f32[1,2,256,8192]{3,1,0,2:T(2,128)} async-done(((f32[1,2,256,8192]{3,1,0,2:T(2,128)}), f32[1,2,256,8192]{3,1,0,2:T(2,128)}, u32[]{:S(2)}, u32[]{:S(2)}) %all-to-all-start.3) | async-done | bytes 16777248 | tf_op jit(solution)/shard_map/all_to_all | solution.py:18
  1492.8 27.0 %reshape.258 = f32[4,2,64,128,64]{4,3,2,0,1:T(8,128)} reshape(f32[4,1,2,64,8192]{4,3,0,2,1:T(8,128)} %bitcast.169) | data formatting | bytes 33554432 | tf_op jit(solution)/shard_map/reshape | solution.py:91
  1519.8 34.0 %fusion = f32[2,64,128,256,1]{3,2,0,1,4:T(8,128)S(1)} fusion(f32[256,4,64,1,1]{0,2,3,4,1:T(8,128)S(1)} %bitcast.190, f32[4,2,64,128,64]{4,3,2,0,1:T(8,128)} %reshape.258), kind=kOutput, calls=%fused_computation | convolution fusion | flops 12884901888 | bytes 33816576 | tf_op jit(solution)/shard_map/jdt,dsyxt->sjyx/dot_general | solution.py:93
  1560.0 25.4 %copy.118 = f32[1,2,256,8192]{3,1,0,2:T(2,128)} copy(f32[1,2,256,8192]{2,3,1,0:T(8,128)} %bitcast.179) | data formatting | bytes 33554432 | tf_op jit(solution)/shard_map/reshape | solution.py:27
  1585.4 367.9 %all_to_all.91 = f32[1,2,256,8192]{3,1,0,2:T(2,128)S(1)} all-to-all(f32[1,2,256,8192]{3,1,0,2:T(2,128)} %copy.118), channel_id=1, replica_groups=mesh['tm'=4,'lon'=8] {'tm'}, dimensions={2} | all-to-all | bytes 33554432 | tf_op jit(solution)/shard_map/all_to_all | solution.py:18
  1970.8 20.0 fusion.46
  1990.8 25.3 %copy.121 = f32[1,2,256,8192]{3,1,0,2:T(2,128)} copy(f32[1,2,256,8192]{2,3,1,0:T(8,128)} %bitcast.171) | data formatting | bytes 33554432 | tf_op jit(solution)/shard_map/reshape | solution.py:34
  2016.1 188.3 %all_to_all.92 = f32[1,2,256,8192]{3,1,0,2:T(2,128)S(1)} all-to-all(f32[1,2,256,8192]{3,1,0,2:T(2,128)} %copy.121), channel_id=1, replica_groups=mesh['tm'=4,'lon'=8] {'lon'}, dimensions={2} | all-to-all | bytes 33554432 | tf_op jit(solution)/shard_map/all_to_all | solution.py:22
  2236.3 35.5 %multiply_reduce_fusion = (f32[2]{0:T(128)S(1)}, f32[2]{0:T(128)S(1)}, f32[2,32,64,1024,1]{3,2,1,4,0:T(8,128)}) fusion(f32[2,64,32,1024]{3,1,2,0:T(8,128)} %get-tuple-element.24, f32[64,32,1024]{2,0,1:T(8,128)S(1)} %bitcast.167, f32[8,2,32,64,128]{4,3,2,0,1:T(8,128)} %bitcast.168, bf16[1024,8,128,1,1]{0,2,4,1,3:T(8,128)(2,1)S(1)} %bitcast.184), kind=kOutput, calls=%fused_computation.14 | convolution fusion | flops 51568967680 | bytes 60817424 | tf_op jit(solution)/shard_map/odx,dsltx->stlo/dot_general | solution.py:64
  2271.8 38.2 %all-reduce = (f32[2]{0:T(128)S(1)}, f32[2]{0:T(128)S(1)}) all-reduce(f32[2]{0:T(128)S(1)} %get-tuple-element.13, f32[2]{0:T(128)S(1)} %get-tuple-element.12), channel_id=1, replica_groups=mesh['tm'=4,'lon'=8] {'tm','lon'}, use_global_device_ids=true, to_apply=%region_1.2 | all-reduce | flops 4 | bytes 32 | tf_op jit(solution)/shard_map/psum | solution.py:70
  2309.9 30.2 %multiply_subtract_fusion = (f32[2,64,32,1024]{3,1,2,0:T(8,128)}, f32[2,64,32,1024]{3,1,2,0:T(8,128)}) fusion(f32[2,64,32,1024]{3,1,2,0:T(8,128)} %get-tuple-element.24, f32[2,32,64,1024,1]{3,2,1,4,0:T(8,128)} %get-tuple-element.26, f32[2]{0:T(128)S(1)} %div.8, f32[64,32,1024]{2,0,1:T(8,128)} %copy.106, f32[2,32,64,1024,1]{3,2,1,4,0:T(8,128)} %get-tuple-element.25), kind=kLoop, calls=%fused_computation.13 | loop fusion | flops 29360128 | bytes 92274696 | tf_op jit(solution)/shard_map/sub | solution.py:99
  (61 shorter events, 266.9 us)
Async XLA Ops:
  55.0 7.6 copy-start.5
  55.0 372.1 %all-to-all-start = ((f32[1,2,256,8192]{3,1,0,2:T(2,128)}), f32[1,2,256,8192]{3,1,0,2:T(2,128)}, u32[]{:S(2)}, u32[]{:S(2)}) async-start(f32[1,2,256,8192]{3,1,0,2:T(2,128)} %copy.97), calls=%async_computation | async-start | bytes 33554432 | tf_op jit(solution)/shard_map/all_to_all | solution.py:18
  62.7 386.6 %copy-start.3 = (bf16[256,256]{0,1:T(8,128)(2,1)}, bf16[256,256]{0,1:T(8,128)(2,1)S(1)}, u32[]{:S(2)}) copy-start(bf16[256,256]{0,1:T(8,128)(2,1)S(1)} %copy.100) | copy-start | bytes 393220
  494.8 198.1 %all-to-all-start.1 = ((f32[1,2,256,8192]{3,1,0,2:T(2,128)}), f32[1,2,256,8192]{3,1,0,2:T(2,128)}, u32[]{:S(2)}, u32[]{:S(2)}) async-start(f32[1,2,256,8192]{3,1,0,2:T(2,128)} %copy.101), calls=%async_computation.1 | async-start | bytes 33554432 | tf_op jit(solution)/shard_map/all_to_all | solution.py:22
  500.6 109.8 %all-gather.2.cloned.1.call-start = ((), (), s32[]{:S(2)}) async-start(), calls=%async_computation.6 | async-start | bytes 2359296 | tf_op jit(solution)/shard_map/all_gather | solution.py:60
  613.4 101.8 %copy-start.1 = (bf16[1024,1024]{0,1:T(8,128)(2,1)}, bf16[1024,1024]{0,1:T(8,128)(2,1)S(1)}, u32[]{:S(2)}) copy-start(bf16[1024,1024]{0,1:T(8,128)(2,1)S(1)} %copy.104) | copy-start | bytes 6291460
  692.9 22.3 slice-start
  708.3 6.9 slice-start.1
  1025.6 16.4 copy-start.6
  1105.4 7.1 copy-start.7
  1105.4 369.6 %all-to-all-start.3 = ((f32[1,2,256,8192]{3,1,0,2:T(2,128)}), f32[1,2,256,8192]{3,1,0,2:T(2,128)}, u32[]{:S(2)}, u32[]{:S(2)}) async-start(f32[1,2,256,8192]{3,1,0,2:T(2,128)} %copy.114), calls=%async_computation.3 | async-start | bytes 33554432 | tf_op jit(solution)/shard_map/all_to_all | solution.py:18
  1963.8 6.9 copy-start.4
  2204.3 31.9 %slice-start.2 = ((s8[8388608]{0:T(1024)(128)(4,1)}), s8[4194304]{0:T(1024)(128)(4,1)S(1)}, s32[]{:S(2)}) async-start(s8[8388608]{0:T(1024)(128)(4,1)} %bitcast.166), calls=%async_computation.9 | async-start | bytes 8388608
  2221.7 14.6 slice-start.3
  2221.7 14.6 copy-start.2
  2340.1 19.3 copy-start
Sparse Core Ops, SparseCore 0:
  503.3 107.0 all-gather.1
where the time goes:
time: 2400 us; the launch traced here: 2390 us
  waiting for transfers between devices  887 us (37%)
  blocking collectives  783 us (33%)
  local copies, waits for them, and re-layouts  413 us (17%)
  matrix products  228 us (10%)
  other arithmetic  40.2 us (2%)
    all_to_all x2, waiting for transfers between devices, over_hours(): lax.all_to_all(tensor_in, 'tm', split_axis=2, concat_axis=0, tiled=True)  722 us
    all_to_all x2, blocking collectives, over_columns(): lax.all_to_all(tensor_in, 'lon', split_axis=2, concat_axis=0, tiled=True)  376 us
    all_to_all x1, blocking collectives, over_hours(): lax.all_to_all(tensor_in, 'tm', split_axis=2, concat_axis=0, tiled=True)  368 us
    unnamed x34, local copies, waits for them, and re-layouts  86 us
    all_gather x1, waiting for transfers between devices, lon_forward(): factor_rows = lax.all_gather(lon_factor, 'lon', axis=0, tiled=True)  85.1 us
    all_to_all x1, waiting for transfers between devices, over_columns(): lax.all_to_all(tensor_in, 'lon', split_axis=2, concat_axis=0, tiled=True)  79.5 us
    dot_general x2, matrix products, lon_forward(): return jnp.einsum('odx,dsltx->stlo', split_rows, arrived, precision=PRECISE)  70.4 us
    all_to_all x4, local copies, waits for them, and re-layouts, over_columns(): lax.all_to_all(tensor_in, 'lon', split_axis=2, concat_axis=0, tiled=True)  69 us
  transfers between devices with their start and end apart: 4, of which 4 were waited for; matrix products, arithmetic and copies ran while one was open for 1% of the time, Pallas kernels for 0%

commit v1 on v0

v1 whole, which is shorter than its diff:
```python
import functools
import jax
import jax.numpy as jnp
from jax import lax
from jax.experimental import pallas as pl
from jax.experimental.pallas import tpu as pltpu
from jax.sharding import PartitionSpec as P

F32, BF16, I16, I32 = jnp.float32, jnp.bfloat16, jnp.int16, jnp.int32
EXACT, HIGH = lax.Precision.HIGHEST, lax.Precision.HIGH
NOISE_VAR = 0.25
SPECTRUM_MAX = 4.0
HOURLY_MAX = 400.0
STEPS = 1024.0
LEAST = -18.0
CODE_MAX = 2.0**13.5
GROUP = 16
VMEM = 52 * 1024 * 1024


def angle_tables(row_count, col_count, period):
    row_index = lax.broadcasted_iota(I32, (row_count, col_count), 0)
    col_index = lax.broadcasted_iota(I32, (row_count, col_count), 1)
    phase = (row_index * col_index % period).astype(F32) * (2.0 * jnp.pi / period)
    return (jnp.cos(phase), jnp.sin(phase))


def encode(x):
    size = jnp.maximum(jnp.abs(x), 2.0**LEAST)
    code = (jnp.log(size) * (STEPS / 0.6931471805599453) + (0.5 - STEPS * LEAST)).astype(I32)
    return jnp.where(x < 0, -code, code).astype(I16)


def decode(code):
    wide = code.astype(I32)
    size = jnp.exp2(jnp.abs(wide).astype(F32) * (1.0 / STEPS) + LEAST)
    size = jnp.where(wide == 0, 0.0, size)
    return jnp.where(wide < 0, -size, size)


def dot(a, b):
    return jnp.dot(a, b, preferred_element_type=F32)


def dot_rows(a, b):
    return lax.dot_general(a, b, (((1,), (1,)), ((), ())), preferred_element_type=F32)


def two_part_dot(a, b):
    top = a.astype(BF16)
    rest = (a - top.astype(F32)).astype(BF16)
    return dot(top, b) + dot(rest, b)


def fold(x):
    rows, cols = x.shape
    x = jnp.sum(x.reshape(rows // 8, 8, cols), axis=0)
    total = x[:, :128]
    for start in range(128, cols, 128):
        total = total + x[:, start : start + 128]
    return total


def call(body, name, grid, out_shape, in_specs, out_specs, flops, moved, scratch=(), aliases={}):
    return pl.pallas_call(
        body,
        name=name,
        grid=(grid,),
        out_shape=out_shape,
        in_specs=in_specs,
        out_specs=out_specs,
        scratch_shapes=list(scratch),
        input_output_aliases=aliases,
        compiler_params=pltpu.CompilerParams(vmem_limit_bytes=VMEM),
        cost_estimate=pl.CostEstimate(flops=flops, bytes_accessed=moved, transcendentals=0),
    )


def whole_spec(shape):
    return pl.BlockSpec(shape, lambda i: (0,) * len(shape))


SCALARS = pl.BlockSpec(memory_space=pltpu.SMEM)


def struct(shape, kind):
    return jax.ShapeDtypeStruct(shape, kind)


class Kernels:
    def __init__(self, zs, qs, hour_local, lat_local, lat_rows, lon_local):
        self.zs, self.qs = zs, qs
        self.hl, self.al, self.lr, self.ol = hour_local, lat_local, lat_rows, lon_local
        self.hours, self.lats, self.lons = zs * hour_local, zs * lat_local, qs * lon_local
        self.cells = hour_local * lat_rows * self.lons

    def parts_specs(self):
        return [pl.BlockSpec((GROUP, self.lr, self.ol), lambda i: (i, 0, 0))] * self.qs

    def parts_shape(self, kind):
        return [struct((self.hl, self.lr, self.ol), kind)] * self.qs

    def grid_spec(self):
        return pl.BlockSpec((GROUP, self.lr, self.lons), lambda i: (i, 0, 0))

    def hourly(self, noise, tables):
        zs, hl, al, ol, hours = self.zs, self.hl, self.al, self.ol, self.hours
        periods = noise.shape[3]

        def body(noise_ref, table_ref, out_ref, turned):
            for start in range(0, GROUP, 4):
                part = noise_ref[:, start : start + 4].reshape(2, 4 * ol, periods)
                total = dot_rows(table_ref[0], part[0]) + dot_rows(table_ref[1], part[1])
                for k in range(4):
                    turned[pl.ds(start + k, hours, stride=GROUP), :] = total[:, k * ol : (k + 1) * ol]
            out_ref[...] = turned[...].reshape(zs, hl, GROUP, ol).astype(BF16)

        return call(
            body, "hourly", al // GROUP, struct((zs, hl, al, ol), BF16),
            [pl.BlockSpec((2, GROUP, ol, periods), lambda i: (0, i, 0, 0)), whole_spec(tables.shape)],
            pl.BlockSpec((zs, hl, GROUP, ol), lambda i: (0, 0, i, 0)),
            4 * hours * periods * al * ol, 2 * noise.size + 2 * hours * al * ol,
            [pltpu.VMEM((hours * GROUP, ol), F32)],
        )(noise, tables)

    def lat_up(self, g, lat, gain):
        zs, qs, hl, lr, ol, lats = self.zs, self.qs, self.hl, self.lr, self.ol, self.lats

        def body(gain_ref, g_ref, lat_ref, *outs):
            for start in range(0, GROUP, 4):
                part = [g_ref[:, start + k].reshape(lats, ol) for k in range(4)]
                total = dot(lat_ref[...], jnp.concatenate(part, axis=1))
                code = encode(total * gain_ref[0])
                for k in range(4):
                    for d in range(qs):
                        outs[d][start + k] = code[d * lr : (d + 1) * lr, k * ol : (k + 1) * ol]

        return call(
            body, "lat_up", hl // GROUP, self.parts_shape(I16),
            [SCALARS, pl.BlockSpec((zs, GROUP, self.al, ol), lambda i: (0, i, 0, 0)), whole_spec(lat.shape)],
            self.parts_specs(), 2 * self.cells * lats, 4 * self.cells,
        )(gain.reshape(1), g, lat)

    def residual(self, parts, back, lon_up, lon_down, observed, mask):
        qs, hl, lr, ol, lons = self.qs, self.hl, self.lr, self.ol, self.lons
        rows = GROUP * lr

        def body(back_ref, *refs):
            codes, (up_ref, down_ref, observed_ref, mask_ref), outs = refs[:qs], refs[qs : qs + 4], refs[qs + 4 :]
            prior_ref, norm_ref, sent = outs[0], outs[1], outs[2:]
            x = jnp.concatenate([decode(c[...].reshape(rows, ol)) for c in codes], axis=1)
            prior = two_part_dot(x, up_ref[...]) * back_ref[0]
            prior_ref[...] = prior.reshape(GROUP, lr, lons)
            seen = mask_ref[...].reshape(rows, lons).astype(F32)
            resid = seen * (observed_ref[...].reshape(rows, lons) - prior)

            @pl.when(pl.program_id(0) == 0)
            def _():
                norm_ref[...] = jnp.zeros_like(norm_ref)

            norm_ref[...] += fold(resid * resid)
            v = two_part_dot(resid, down_ref[...]).astype(BF16)
            for d in range(qs):
                sent[d][...] = v[:, d * ol : (d + 1) * ol].reshape(GROUP, lr, ol)

        out = call(
            body, "residual", hl // GROUP,
            [struct((hl, lr, lons), F32), struct((8, 128), F32)] + self.parts_shape(BF16),
            [SCALARS] + self.parts_specs() + [whole_spec(lon_up.shape)] * 2 + [self.grid_spec()] * 2,
            [self.grid_spec(), whole_spec((8, 128))] + self.parts_specs(),
            8 * self.cells * lons, 16 * self.cells,
        )(back.reshape(1), *parts, lon_up, lon_down, observed, mask)
        return out[0], jnp.sum(out[1]), out[2:]

    def lat_down(self, parts, lat_t):
        zs, qs, hl, al, lr, ol, lats = self.zs, self.qs, self.hl, self.al, self.lr, self.ol, self.lats

        def body(*refs):
            sent, (lat_ref, out_ref, turned) = refs[:qs], refs[qs:]
            for start in range(0, GROUP, 4):
                part = [jnp.concatenate([s[start + k] for s in sent], axis=0) for k in range(4)]
                total = dot(lat_ref[...], jnp.concatenate(part, axis=1))
                for k in range(4):
                    turned[pl.ds(start + k, lats, stride=GROUP), :] = total[:, k * ol : (k + 1) * ol]
            out_ref[...] = turned[...].reshape(zs, al, GROUP, ol).astype(BF16)

        return call(
            body, "lat_down", hl // GROUP, struct((zs, al, hl, ol), BF16),
            self.parts_specs() + [whole_spec(lat_t.shape)],
            pl.BlockSpec((zs, al, GROUP, ol), lambda i: (0, 0, i, 0)),
            2 * self.cells * lats, 4 * self.cells,
            [pltpu.VMEM((lats * GROUP, ol), F32)],
        )(*parts, lat_t)

    def over_hours(self, x, kern):
        zs, hl, al, ol, hours = self.zs, self.hl, self.al, self.ol, self.hours

        def body(x_ref, kern_ref, out_ref, bend_ref, turned):
            @pl.when(pl.program_id(0) == 0)
            def _():
                bend_ref[...] = jnp.zeros_like(bend_ref)

            for start in range(0, GROUP, 4):
                part = [x_ref[:, start + k].reshape(hours, ol) for k in range(4)]
                part = jnp.concatenate(part, axis=1)
                total = dot(kern_ref[0], part) + dot(kern_ref[1], part)
                bend_ref[...] += fold(total * part.astype(F32))
                for k in range(4):
                    turned[pl.ds(start + k, hours, stride=GROUP), :] = total[:, k * ol : (k + 1) * ol]
            out_ref[...] = turned[...].reshape(zs, hl, GROUP, ol).astype(BF16)

        out = call(
            body, "over_hours", al // GROUP, [struct((zs, hl, al, ol), BF16), struct((8, 128), F32)],
            [pl.BlockSpec((zs, GROUP, hl, ol), lambda i: (0, i, 0, 0)), whole_spec(kern.shape)],
            [pl.BlockSpec((zs, hl, GROUP, ol), lambda i: (0, 0, i, 0)), whole_spec((8, 128))],
            4 * self.cells * hours, 4 * self.cells,
            [pltpu.VMEM((hours * GROUP, ol), F32)],
        )(x, kern)
        return out[0], jnp.sum(out[1])

    def finish(self, s, parts, back, step, lon_up, prior, observed, mask, earlier):
        qs, hl, lr, ol, lons = self.qs, self.hl, self.lr, self.ol, self.lons
        rows = GROUP * lr

        def body(scalar_ref, *refs):
            codes, (up_ref, prior_ref, observed_ref, mask_ref) = refs[:qs], refs[qs : qs + 4]
            posterior_ref, next_ref = refs[-2:]
            x = jnp.concatenate([decode(c[...].reshape(rows, ol)) for c in codes], axis=1)
            scaled = two_part_dot(x, up_ref[...]) * scalar_ref[0]
            prior = prior_ref[...].reshape(rows, lons)
            seen = mask_ref[...].reshape(rows, lons).astype(F32)
            resid = seen * (observed_ref[...].reshape(rows, lons) - prior)
            shape = (1, GROUP, lr, lons)
            posterior_ref[...] = (prior + scaled).reshape(shape)
            next_ref[...] = (resid - seen * scaled - scalar_ref[1] * resid).reshape(shape)

        full = struct((2, hl, lr, lons), F32)
        out_spec = pl.BlockSpec((1, GROUP, lr, lons), lambda i: (s, i, 0, 0))
        count = 1 + qs + 4
        return call(
            body, "finish", hl // GROUP, [full, full],
            [SCALARS] + self.parts_specs() + [whole_spec(lon_up.shape)] + [self.grid_spec()] * 3
            + [pl.BlockSpec(memory_space=pl.ANY)] * len(earlier),
            [out_spec, out_spec], 4 * self.cells * lons, 22 * self.cells,
            aliases={count + i: i for i in range(len(earlier))},
        )(jnp.stack([back * step, NOISE_VAR * step]), *parts, lon_up, prior, observed, mask, *earlier)


class Plain(Kernels):
    def hourly(self, noise, tables):
        h = jnp.einsum("cyxk,cjk->jyx", noise, tables, preferred_element_type=F32)
        return h.reshape(self.zs, self.hl, self.al, self.ol).astype(BF16)

    def lat_up(self, g, lat, gain):
        split = lat.reshape(self.qs, self.lr, self.zs, self.al)
        x = jnp.einsum("qlzy,zhyx->qhlx", split, g, preferred_element_type=F32)
        code = encode(x * gain)
        return [code[d] for d in range(self.qs)]

    def up(self, parts, lon_up):
        x = jnp.concatenate([decode(c) for c in parts], axis=2)
        return jnp.einsum("hlx,xo->hlo", x, lon_up.astype(F32), precision=HIGH)

    def residual(self, parts, back, lon_up, lon_down, observed, mask):
        prior = self.up(parts, lon_up) * back
        resid = mask.astype(F32) * (observed - prior)
        v = jnp.einsum("hlo,op->hlp", resid, lon_down.astype(F32), precision=HIGH).astype(BF16)
        return prior, jnp.sum(resid * resid), jnp.split(v, self.qs, axis=2)

    def lat_down(self, parts, lat_t):
        split = lat_t.reshape(self.zs, self.al, self.qs, self.lr)
        x = jnp.einsum("zyql,qhlx->zyhx", split, jnp.stack(parts), preferred_element_type=F32)
        return x.astype(BF16)

    def over_hours(self, x, kern):
        split = kern.astype(F32).sum(0).reshape(self.zs, self.hl, self.zs, self.hl)
        x = x.astype(F32)
        y = jnp.einsum("ghzk,zykx->ghyx", split, x, precision=HIGH)
        return y.astype(BF16), jnp.einsum("ghyx,gyhx->", y, x)

    def finish(self, s, parts, back, step, lon_up, prior, observed, mask, earlier):
        scaled = self.up(parts, lon_up) * (back * step)
        seen = mask.astype(F32)
        resid = seen * (observed - prior)
        pair = (prior + scaled, resid - seen * scaled - NOISE_VAR * step * resid)
        if not earlier:
            return pair
        return tuple(jnp.stack([a, b]) for a, b in zip(earlier, pair))


def swap_tm(x):
    return lax.all_to_all(x, "tm", split_axis=0, concat_axis=0, tiled=True)


def swap_lon(parts):
    count = len(parts)
    return [parts[0]] + [
        lax.ppermute(parts[d], "lon", [(i, i ^ d) for i in range(count)]) for d in range(1, count)
    ]


def largest_norm(factor, axis):
    return jnp.sqrt(jnp.max(jnp.sum(jnp.square(factor.astype(F32)), axis=axis)))


def shards(noise, observed, mask, lat_factor, lon_factor, spectrum):
    _, lat_local, lon_local, periods = noise.shape
    hour_local, lat_rows, lon_count = observed.shape
    hours = periods // 2
    zs, qs = hours // hour_local, lon_count // lon_local
    lat_count = zs * lat_local
    fits = lon_local % 128 == 0 and lat_rows % 16 == 0
    fits = fits and lat_local % GROUP == 0 and hour_local % GROUP == 0
    stages = (Kernels if fits else Plain)(zs, qs, hour_local, lat_local, lat_rows, lon_local)

    powers = jnp.concatenate([spectrum, spectrum[1:-1][::-1]])
    amplitude = jnp.sqrt(powers / periods)
    cosine_tab, sine_tab = angle_tables(hours, periods, periods)
    table_cos = (cosine_tab * amplitude).astype(BF16)
    table_sin = (sine_tab * amplitude).astype(BF16)
    tables = (jnp.stack([table_cos, table_sin]), jnp.stack([-table_sin, table_cos]))

    def hour_kernel():
        scaled = powers / periods
        kern = jnp.dot(cosine_tab * scaled, cosine_tab.T, precision=EXACT) + jnp.dot(
            sine_tab * scaled, sine_tab.T, precision=EXACT
        )
        top = lax.reduce_precision(kern, 8, 7)
        return jnp.stack([top.astype(BF16), (kern - top).astype(BF16)])

    arrived = [swap_tm(stages.hourly(noise, table)) for table in tables]
    kern = hour_kernel()
    order = lax.axis_index("lon") ^ jnp.arange(qs)
    lon = lax.all_gather(lon_factor, "lon", axis=0, tiled=True).reshape(lon_count, qs, lon_local)
    lon_down = jnp.take(lon, order, axis=1).reshape(lon_count, lon_count)
    lon_up = lon_down.T
    lat = jnp.take(lat_factor.reshape(qs, lat_rows, lat_count), order, axis=0)
    lat = lat.reshape(lat_count, lat_count)
    lat_t = lat.T
    lat_row_norm = largest_norm(lat_factor, 1)
    lon_col_norm = largest_norm(lon_down, 0)
    lat_norm = jnp.sqrt(jnp.sum(jnp.square(lat_factor.astype(F32))))
    first_gain = CODE_MAX / jnp.maximum(lat_row_norm * (lat_count**0.5 * HOURLY_MAX), 1e-30)

    earlier = ()
    for s in range(2):
        parts = swap_lon(stages.lat_up(arrived[s], lat, first_gain))
        prior, norm_sq, parts = stages.residual(parts, 1.0 / first_gain, lon_up, lon_down, observed, mask)
        x = swap_tm(stages.lat_down(swap_lon(parts), lat_t))
        y, bending = stages.over_hours(x, kern)
        y = swap_tm(y)
        if s == 1:
            bending, _ = lax.optimization_barrier((bending, step))
        norm_sq, bending = lax.psum((norm_sq, bending), ("tm", "lon"))
        step = norm_sq / (bending + NOISE_VAR * norm_sq)
        bound = SPECTRUM_MAX * lat_row_norm * lat_norm * lon_col_norm * jnp.sqrt(norm_sq)
        gain = CODE_MAX / jnp.maximum(bound, 1e-30)
        parts = swap_lon(stages.lat_up(y, lat, gain))
        earlier = stages.finish(s, parts, 1.0 / gain, step, lon_up, prior, observed, mask, earlier)
    return tuple(earlier)


def solution(mesh):
    return jax.shard_map(
        shards,
        mesh=mesh,
        in_specs=(
            P(None, "tm", "lon", None),
            P("tm", "lon", None),
            P("tm", "lon", None),
            P(),
            P("lon", None),
            P(),
        ),
        out_specs=(P(None, "tm", "lon", None), P(None, "tm", "lon", None)),
        check_vma=False,
    )
```

time: 2400 us -> 927 us (0.39)
  blocking collectives: 783 us -> 160 us
  waiting for transfers between devices: 887 us -> 449 us
  local copies, waits for them, and re-layouts: 413 us -> 21.3 us
  matrix products: 228 us -> 5.08 us
  Pallas kernels: 0 us -> 173 us
  starting transfers between devices: 20.6 us -> 76.1 us
  other arithmetic: 40.2 us -> 13.9 us
    all_to_all x3 -> x0, blocking collectives: 744 us -> none  [the longest x2 376 us: over_columns(): lax.all_to_all(tensor_in, 'lon', split_axis=2, concat_axis=0, tiled=True)]
    all_to_all x3 -> x6, waiting for transfers between devices: 801 us -> 250 us  [swap_tm(): return lax.all_to_all(x, 'tm', split_axis=0, concat_axis=0, tiled=True)]
    dot_general x10 -> x2, matrix products: 228 us -> 5.08 us  [the longest x1 2.55 us: hour_kernel(): jnp.dot(sine_tab * scaled, sine_tab.T, precision=EXACT)]
    ppermute x0 -> x42, waiting for transfers between devices: none -> 200 us  [swap_lon(): lax.ppermute(parts[d], 'lon', [(i, i ^ d) for i in range(count)])]
    reshape x7 -> x1, local copies, waits for them, and re-layouts: 179 us -> 3.9 us  [shards(): lax.all_gather(lon_factor, 'lon', axis=0, tiled=True)]
    pallas_call x0 -> x14, Pallas kernels: none -> 173 us  [the longest x2 54.1 us: residual(): call(body, 'residual', hl // GROUP, [struct((hl, lr, lons), F32), struct(...]
    psum x1 -> x2, blocking collectives: 38.2 us -> 160 us  [shards(): norm_sq, bending = lax.psum((norm_sq, bending), ('tm', 'lon'))]
    all_to_all x7 -> x0, local copies, waits for them, and re-layouts: 112 us -> none  [the longest x4 69 us: over_columns(): lax.all_to_all(tensor_in, 'lon', split_axis=2, concat_axis=0, tiled=True)]
  transfers between devices with their start and end apart: 4 -> 49, of which waited for: 4 -> 17; matrix products, arithmetic and copies ran while one was open for 1% -> 3% of each run, Pallas kernels for 0% -> 15%
where the time goes in v1:
time: 927 us; the launch traced here: 921 us
  waiting for transfers between devices  449 us (48%)
  Pallas kernels  173 us (19%)
  blocking collectives  160 us (17%)
  starting transfers between devices  76.1 us (8%)
  between operations  22.1 us (2%)
  local copies, waits for them, and re-layouts  21.3 us (2%)
  other arithmetic  13.9 us (1%)
    all_to_all x6, waiting for transfers between devices, swap_tm(): return lax.all_to_all(x, 'tm', split_axis=0, concat_axis=0, tiled=True)  250 us
    ppermute x42, waiting for transfers between devices, swap_lon(): lax.ppermute(parts[d], 'lon', [(i, i ^ d) for i in range(count)])  200 us
    psum x2, blocking collectives, shards(): norm_sq, bending = lax.psum((norm_sq, bending), ('tm', 'lon'))  160 us
    pallas_call x2, Pallas kernels, residual(): call(body, 'residual', hl // GROUP, [struct((hl, lr, lons), F32), struct(...  54.1 us
    ppermute x42, starting transfers between devices, swap_lon(): lax.ppermute(parts[d], 'lon', [(i, i ^ d) for i in range(count)])  44.2 us
    pallas_call x2, Pallas kernels, finish(): call(body, 'finish', hl // GROUP, [full, full], [SCALARS] + self.parts_sp...  43.1 us
    all_to_all x6, starting transfers between devices, swap_tm(): return lax.all_to_all(x, 'tm', split_axis=0, concat_axis=0, tiled=True)  31.8 us
    pallas_call x4, Pallas kernels, lat_up(): call(body, 'lat_up', hl // GROUP, self.parts_shape(I16), [SCALARS, pl.Blo...  26.9 us
  transfers between devices with their start and end apart: 49, of which 17 were waited for; matrix products, arithmetic and copies ran while one was open for 3% of the time, Pallas kernels for 15%

profile of v1, /device:TPU:0, one launch (start us, length us, event | category | flops | bytes accessed | tf_op | source)
XLA Modules:
  0.0 921.1 jit_solution(6887468695389373030)
XLA Ops:
  13.2 11.1 %hourly.3 = bf16[4,64,64,128]{3,2,1,0:T(8,128)(2,1)} custom-call(bf16[2,64,128,512]{3,2,1,0:T(8,128)(2,1)} %noise_ref.3, bf16[2,256,512]{2,1,0:T(8,128)(2,1)S(1)} %get-tuple-element.128.table_ref), custom_call_target="tpu_custom_call" | custom-call | flops 4294967296 | bytes 20971520 | tf_op jit(solution)/shard_map/hourly/pallas_call | solution.py:118
  31.7 11.1 %hourly.2 = bf16[4,64,64,128]{3,2,1,0:T(8,128)(2,1)} custom-call(bf16[2,64,128,512]{3,2,1,0:T(8,128)(2,1)} %noise_ref.3, bf16[2,256,512]{2,1,0:T(8,128)(2,1)S(1)} %get-tuple-element.129.table_ref), custom_call_target="tpu_custom_call" | custom-call | flops 4294967296 | bytes 20971520 | tf_op jit(solution)/shard_map/hourly/pallas_call | solution.py:118
  42.8 81.5 %all-to-all-done.2.g_ref = bf16[4,64,64,128]{3,2,1,0:T(8,128)(2,1)} async-done(((bf16[4,64,64,128]{3,2,1,0:T(8,128)(2,1)}), bf16[4,64,64,128]{3,2,1,0:T(8,128)(2,1)}, u32[]{:S(2)}, u32[]{:S(2)}) %all-to-all-start.2) | async-done | bytes 4194336 | tf_op jit(solution)/shard_map/all_to_all | solution.py:292
  146.0 8.7 collective-permute-done.15.refs_2_
  171.2 18.1 %collective-permute-done.18.refs_5_ = s16[64,32,128]{2,1,0:T(8,128)(2,1)} collective-permute-done((s16[64,32,128]{2,1,0:T(8,128)(2,1)}, s16[64,32,128]{2,1,0:T(8,128)(2,1)}, u32[]{:S(2)}, u32[]{:S(2)}) %collective-permute-start.18) | collective-permute-done | bytes 524320 | tf_op jit(solution)/shard_map/ppermute | solution.py:298
  189.3 27.1 %residual.3 = (f32[64,32,1024]{2,1,0:T(8,128)}, f32[8,128]{1,0:T(8,128)S(1)}, bf16[64,32,128]{2,1,0:T(8,128)(2,1)S(1)}, bf16[64,32,128]{2,1,0:T(8,128)(2,1)S(1)}...) custom-call(f32[1]{0:T(128)} %bitcast.3.back_ref, ...), custom_call_target="tpu_custom_call" | custom-call | flops 17179869184 | bytes 33554432 | tf_op jit(solution)/shard_map/residual/pallas_call | solution.py:166
  223.0 8.7 collective-permute-done.22.refs_2_
  232.3 9.8 %collective-permute-done.23.refs_3_ = bf16[64,32,128]{2,1,0:T(8,128)(2,1)S(1)} collective-permute-done((bf16[64,32,128]{2,1,0:T(8,128)(2,1)}, bf16[64,32,128]{2,1,0:T(8,128)(2,1)S(1)}, u32[]{:S(2)}, u32[]{:S(2)}) %collective-permute-start.23) | collective-permute-done | bytes 524320 | tf_op jit(solution)/shard_map/ppermute | solution.py:298
  242.1 24.4 %collective-permute-done.25.refs_5_ = bf16[64,32,128]{2,1,0:T(8,128)(2,1)S(1)} collective-permute-done((bf16[64,32,128]{2,1,0:T(8,128)(2,1)}, bf16[64,32,128]{2,1,0:T(8,128)(2,1)S(1)}, u32[]{:S(2)}, u32[]{:S(2)}) %collective-permute-start.25) | collective-permute-done | bytes 524320 | tf_op jit(solution)/shard_map/ppermute | solution.py:298
  292.5 8.7 collective-permute-done.1.refs_2_
  302.8 8.8 collective-permute-done.2.refs_3_
  311.6 24.0 %collective-permute-done.4.refs_5_ = s16[64,32,128]{2,1,0:T(8,128)(2,1)S(1)} collective-permute-done((s16[64,32,128]{2,1,0:T(8,128)(2,1)}, s16[64,32,128]{2,1,0:T(8,128)(2,1)S(1)}, u32[]{:S(2)}, u32[]{:S(2)}) %collective-permute-start.4) | collective-permute-done | bytes 524320 | tf_op jit(solution)/shard_map/ppermute | solution.py:298
  336.8 27.0 %residual.2 = (f32[64,32,1024]{2,1,0:T(8,128)}, f32[8,128]{1,0:T(8,128)S(1)}, bf16[64,32,128]{2,1,0:T(8,128)(2,1)S(1)}, bf16[64,32,128]{2,1,0:T(8,128)(2,1)S(1)}...) custom-call(f32[1]{0:T(128)} %bitcast.3.back_ref, ...), custom_call_target="tpu_custom_call" | custom-call | flops 17179869184 | bytes 33554432 | tf_op jit(solution)/shard_map/residual/pallas_call | solution.py:166
  370.9 8.7 collective-permute-done.8.refs_2_
  380.1 9.9 %collective-permute-done.9.refs_3_ = bf16[64,32,128]{2,1,0:T(8,128)(2,1)S(1)} collective-permute-done((bf16[64,32,128]{2,1,0:T(8,128)(2,1)}, bf16[64,32,128]{2,1,0:T(8,128)(2,1)S(1)}, u32[]{:S(2)}, u32[]{:S(2)}) %collective-permute-start.9) | collective-permute-done | bytes 524320 | tf_op jit(solution)/shard_map/ppermute | solution.py:298
  390.0 24.3 %collective-permute-done.11.refs_5_ = bf16[64,32,128]{2,1,0:T(8,128)(2,1)S(1)} collective-permute-done((bf16[64,32,128]{2,1,0:T(8,128)(2,1)}, bf16[64,32,128]{2,1,0:T(8,128)(2,1)S(1)}, u32[]{:S(2)}, u32[]{:S(2)}) %collective-permute-start.11) | collective-permute-done | bytes 524320 | tf_op jit(solution)/shard_map/ppermute | solution.py:298
  439.2 82.0 %all-to-all-done.1.x_ref = bf16[4,64,64,128]{3,2,1,0:T(8,128)(2,1)} async-done(((bf16[4,64,64,128]{3,2,1,0:T(8,128)(2,1)}), bf16[4,64,64,128]{3,2,1,0:T(8,128)(2,1)}, u32[]{:S(2)}, u32[]{:S(2)}) %all-to-all-start.1) | async-done | bytes 4194336 | tf_op jit(solution)/shard_map/all_to_all | solution.py:292
  533.2 86.2 %all-to-all-done.5.g_ref = bf16[4,64,64,128]{3,2,1,0:T(8,128)(2,1)} async-done(((bf16[4,64,64,128]{3,2,1,0:T(8,128)(2,1)}), bf16[4,64,64,128]{3,2,1,0:T(8,128)(2,1)}, u32[]{:S(2)}, u32[]{:S(2)}) %all-to-all-start.5) | async-done | bytes 4194336 | tf_op jit(solution)/shard_map/all_to_all | solution.py:292
  629.8 107.6 %all-reduce.1 = (f32[]{:T(128)}, f32[]{:T(128)}) all-reduce(f32[]{:T(128)} %reduce_sum.68, f32[]{:T(128)} %reduce_sum.69), channel_id=1, replica_groups=mesh['tm'=4,'lon'=8] {'tm','lon'}, use_global_device_ids=true, to_apply=%region_9.10 | all-reduce | flops 2 | bytes 16 | tf_op jit(solution)/shard_map/psum | solution.py:354
  752.2 52.3 %all-reduce = (f32[]{:T(128)}, f32[]{:T(128)}) all-reduce(f32[]{:T(128)} %reduce_sum.66, f32[]{:T(128)} %reduce_sum.67), channel_id=1, replica_groups=mesh['tm'=4,'lon'=8] {'tm','lon'}, use_global_device_ids=true, to_apply=%region_6.7 | all-reduce | flops 2 | bytes 16 | tf_op jit(solution)/shard_map/psum | solution.py:354
  819.7 21.5 %collective-permute-done.39.refs_5_ = s16[64,32,128]{2,1,0:T(8,128)(2,1)} collective-permute-done((s16[64,32,128]{2,1,0:T(8,128)(2,1)}, s16[64,32,128]{2,1,0:T(8,128)(2,1)}, u32[]{:S(2)}, u32[]{:S(2)}) %collective-permute-start.39) | collective-permute-done | bytes 524320 | tf_op jit(solution)/shard_map/ppermute | solution.py:298
  851.6 21.5 %finish.2 = (f32[2,64,32,1024]{3,2,1,0:T(8,128)}, f32[2,64,32,1024]{3,2,1,0:T(8,128)}) custom-call(f32[2]{0:T(128)S(1)} %pad_maximum_fusion.4.scalar_ref, s16[64,32,128]{2,1,0:T(8,128)(2,1)S(1)} %get-tuple-element.109.refs_0_, s16[64,32,128]{2,1,0:T(8,128)(2,1)S(1)} %collective-permute-done.35.refs_1_, ...), custom_call_target="tpu_custom_call" | custom-call | flops 8589934592 | bytes 46137344 | tf_op jit(solution)/shard_map/finish/pallas_call | solution.py:240
  873.2 18.0 %collective-permute-done.32.refs_5_ = s16[64,32,128]{2,1,0:T(8,128)(2,1)S(1)} collective-permute-done((s16[64,32,128]{2,1,0:T(8,128)(2,1)}, s16[64,32,128]{2,1,0:T(8,128)(2,1)S(1)}, u32[]{:S(2)}, u32[]{:S(2)}) %collective-permute-start.32) | collective-permute-done | bytes 524320 | tf_op jit(solution)/shard_map/ppermute | solution.py:298
  892.4 21.5 %finish.3 = (f32[2,64,32,1024]{3,2,1,0:T(8,128)}, f32[2,64,32,1024]{3,2,1,0:T(8,128)}) custom-call(f32[2]{0:T(128)S(1)} %pad_maximum_fusion.3.scalar_ref, s16[64,32,128]{2,1,0:T(8,128)(2,1)S(1)} %get-tuple-element.99.refs_0_, s16[64,32,128]{2,1,0:T(8,128)(2,1)S(1)} %collective-permute-done.28.refs_1_, ...), custom_call_target="tpu_custom_call", output_to_operand_aliasing={{0}: (13, {}), {1}: (14, {})} | custom-call | flops 8589934592 | bytes 46137344 | tf_op jit(solution)/shard_map/finish/pallas_call | solution.py:240
  (182 shorter events, 176.2 us)
Async XLA Ops:
  24.3 99.9 %all-to-all-start.2 = ((bf16[4,64,64,128]{3,2,1,0:T(8,128)(2,1)}), bf16[4,64,64,128]{3,2,1,0:T(8,128)(2,1)}, u32[]{:S(2)}, u32[]{:S(2)}) async-start(bf16[4,64,64,128]{3,2,1,0:T(8,128)(2,1)} %hourly.3), calls=%async_computation.2 | async-start | bytes 8388608 | tf_op jit(solution)/shard_map/all_to_all | solution.py:292
  30.8 125.6 %all-gather.2.cloned.1.call-start = ((), (), s32[]{:S(2)}) async-start(), calls=%async_computation.6 | async-start | bytes 2359296 | tf_op jit(solution)/shard_map/all_gather | solution.py:334
  124.2 149.5 %all-to-all-start = ((bf16[4,64,64,128]{3,2,1,0:T(8,128)(2,1)}), bf16[4,64,64,128]{3,2,1,0:T(8,128)(2,1)}, u32[]{:S(2)}, u32[]{:S(2)}) async-start(bf16[4,64,64,128]{3,2,1,0:T(8,128)(2,1)} %hourly.2), calls=%async_computation | async-start | bytes 8388608 | tf_op jit(solution)/shard_map/all_to_all | solution.py:292
  143.4 45.9 %collective-permute-start.18 = (s16[64,32,128]{2,1,0:T(8,128)(2,1)}, s16[64,32,128]{2,1,0:T(8,128)(2,1)}, u32[]{:S(2)}, u32[]{:S(2)}) collective-permute-start(s16[64,32,128]{2,1,0:T(8,128)(2,1)} %get-tuple-element.84), channel_id=1, source_target_pairs={{0,5},{1,4},{2,7},{3,6},{4,1},{5,0},{6,3},{7,2},{8,13},{9,12},{10,... | collective-permute-start | bytes 1572872 | tf_op jit(solution)/shard_map/ppermute | solution.py:298
  143.5 45.8 %collective-permute-start.19 = (s16[64,32,128]{2,1,0:T(8,128)(2,1)}, s16[64,32,128]{2,1,0:T(8,128)(2,1)}, u32[]{:S(2)}, u32[]{:S(2)}) collective-permute-start(s16[64,32,128]{2,1,0:T(8,128)(2,1)} %get-tuple-element.85), channel_id=1, source_target_pairs={{0,6},{1,7},{2,4},{3,5},{4,2},{5,3},{6,0},{7,1},{8,14},{9,15},{10,... | collective-permute-start | bytes 1572872 | tf_op jit(solution)/shard_map/ppermute | solution.py:298
  220.0 46.5 %collective-permute-start.25 = (bf16[64,32,128]{2,1,0:T(8,128)(2,1)}, bf16[64,32,128]{2,1,0:T(8,128)(2,1)S(1)}, u32[]{:S(2)}, u32[]{:S(2)}) collective-permute-start(bf16[64,32,128]{2,1,0:T(8,128)(2,1)} %get-tuple-element.93), channel_id=1, source_target_pairs={{0,5},{1,4},{2,7},{3,6},{4,1},{5,0},{6,3},{7,2},{8,13},{9,12},{10,... | collective-permute-start | bytes 1572872 | tf_op jit(solution)/shard_map/ppermute | solution.py:298
  220.4 46.1 %collective-permute-start.26 = (bf16[64,32,128]{2,1,0:T(8,128)(2,1)}, bf16[64,32,128]{2,1,0:T(8,128)(2,1)}, u32[]{:S(2)}, u32[]{:S(2)}) collective-permute-start(bf16[64,32,128]{2,1,0:T(8,128)(2,1)} %get-tuple-element.94), channel_id=1, source_target_pairs={{0,6},{1,7},{2,4},{3,5},{4,2},{5,3},{6,0},{7,1},{8,14},{9,15},{10,... | collective-permute-start | bytes 1572872 | tf_op jit(solution)/shard_map/ppermute | solution.py:298
  231.7 34.8 %collective-permute-start.27 = (bf16[64,32,128]{2,1,0:T(8,128)(2,1)}, bf16[64,32,128]{2,1,0:T(8,128)(2,1)}, u32[]{:S(2)}, u32[]{:S(2)}) collective-permute-start(bf16[64,32,128]{2,1,0:T(8,128)(2,1)} %get-tuple-element.95), channel_id=1, source_target_pairs={{0,7},{1,6},{2,5},{3,4},{4,3},{5,2},{6,1},{7,0},{8,15},{9,14},{10,... | collective-permute-start | bytes 1572872 | tf_op jit(solution)/shard_map/ppermute | solution.py:298
  273.7 148.2 %all-to-all-start.3 = ((bf16[4,64,64,128]{3,2,1,0:T(8,128)(2,1)}), bf16[4,64,64,128]{3,2,1,0:T(8,128)(2,1)}, u32[]{:S(2)}, u32[]{:S(2)}) async-start(bf16[4,64,64,128]{3,2,1,0:T(8,128)(2,1)} %lat_down.3), calls=%async_computation.3 | async-start | bytes 8388608 | tf_op jit(solution)/shard_map/all_to_all | solution.py:292
  289.8 45.8 %collective-permute-start.4 = (s16[64,32,128]{2,1,0:T(8,128)(2,1)}, s16[64,32,128]{2,1,0:T(8,128)(2,1)S(1)}, u32[]{:S(2)}, u32[]{:S(2)}) collective-permute-start(s16[64,32,128]{2,1,0:T(8,128)(2,1)} %get-tuple-element.66), channel_id=1, source_target_pairs={{0,5},{1,4},{2,7},{3,6},{4,1},{5,0},{6,3},{7,2},{8,13},{9,12},{10,... | collective-permute-start | bytes 1572872 | tf_op jit(solution)/shard_map/ppermute | solution.py:298
  289.9 45.7 %collective-permute-start.5 = (s16[64,32,128]{2,1,0:T(8,128)(2,1)}, s16[64,32,128]{2,1,0:T(8,128)(2,1)S(1)}, u32[]{:S(2)}, u32[]{:S(2)}) collective-permute-start(s16[64,32,128]{2,1,0:T(8,128)(2,1)} %get-tuple-element.67), channel_id=1, source_target_pairs={{0,6},{1,7},{2,4},{3,5},{4,2},{5,3},{6,0},{7,1},{8,14},{9,15},{10,... | collective-permute-start | bytes 1572872 | tf_op jit(solution)/shard_map/ppermute | solution.py:298
  367.9 46.4 %collective-permute-start.11 = (bf16[64,32,128]{2,1,0:T(8,128)(2,1)}, bf16[64,32,128]{2,1,0:T(8,128)(2,1)S(1)}, u32[]{:S(2)}, u32[]{:S(2)}) collective-permute-start(bf16[64,32,128]{2,1,0:T(8,128)(2,1)} %get-tuple-element.75), channel_id=1, source_target_pairs={{0,5},{1,4},{2,7},{3,6},{4,1},{5,0},{6,3},{7,2},{8,13},{9,12},{10,... | collective-permute-start | bytes 1572872 | tf_op jit(solution)/shard_map/ppermute | solution.py:298
  368.3 46.1 %collective-permute-start.12 = (bf16[64,32,128]{2,1,0:T(8,128)(2,1)}, bf16[64,32,128]{2,1,0:T(8,128)(2,1)S(1)}, u32[]{:S(2)}, u32[]{:S(2)}) collective-permute-start(bf16[64,32,128]{2,1,0:T(8,128)(2,1)} %get-tuple-element.76), channel_id=1, source_target_pairs={{0,6},{1,7},{2,4},{3,5},{4,2},{5,3},{6,0},{7,1},{8,14},{9,15},{10,... | collective-permute-start | bytes 1572872 | tf_op jit(solution)/shard_map/ppermute | solution.py:298
  421.9 99.4 %all-to-all-start.1 = ((bf16[4,64,64,128]{3,2,1,0:T(8,128)(2,1)}), bf16[4,64,64,128]{3,2,1,0:T(8,128)(2,1)}, u32[]{:S(2)}, u32[]{:S(2)}) async-start(bf16[4,64,64,128]{3,2,1,0:T(8,128)(2,1)} %lat_down.2), calls=%async_computation.1 | async-start | bytes 8388608 | tf_op jit(solution)/shard_map/all_to_all | solution.py:292
  521.2 98.2 %all-to-all-start.5 = ((bf16[4,64,64,128]{3,2,1,0:T(8,128)(2,1)}), bf16[4,64,64,128]{3,2,1,0:T(8,128)(2,1)}, u32[]{:S(2)}, u32[]{:S(2)}) async-start(bf16[4,64,64,128]{3,2,1,0:T(8,128)(2,1)} %get-tuple-element.108), calls=%async_computation.5 | async-start | bytes 8388608 | tf_op jit(solution)/shard_map/all_to_all | solution.py:292
  619.4 185.9 %all-to-all-start.4 = ((bf16[4,64,64,128]{3,2,1,0:T(8,128)(2,1)}), bf16[4,64,64,128]{3,2,1,0:T(8,128)(2,1)}, u32[]{:S(2)}, u32[]{:S(2)}) async-start(bf16[4,64,64,128]{3,2,1,0:T(8,128)(2,1)} %get-tuple-element.98), calls=%async_computation.4 | async-start | bytes 8388608 | tf_op jit(solution)/shard_map/all_to_all | solution.py:292
  744.8 67.3 %collective-permute-start.35 = (s16[64,32,128]{2,1,0:T(8,128)(2,1)S(1)}, s16[64,32,128]{2,1,0:T(8,128)(2,1)S(1)}, u32[]{:S(2)}, u32[]{:S(2)}) collective-permute-start(s16[64,32,128]{2,1,0:T(8,128)(2,1)S(1)} %get-tuple-element.110), channel_id=1, source_target_pairs={{0,1},{1,0},{2,3},{3,2},{4,5},{5,4},{6,7},{7,6},{8,9},{9,8},{10,11... | collective-permute-start | bytes 1572872 | tf_op jit(solution)/shard_map/ppermute | solution.py:298
  744.8 69.5 %collective-permute-start.36 = (s16[64,32,128]{2,1,0:T(8,128)(2,1)S(1)}, s16[64,32,128]{2,1,0:T(8,128)(2,1)S(1)}, u32[]{:S(2)}, u32[]{:S(2)}) collective-permute-start(s16[64,32,128]{2,1,0:T(8,128)(2,1)S(1)} %get-tuple-element.111), channel_id=1, source_target_pairs={{0,2},{1,3},{2,0},{3,1},{4,6},{5,7},{6,4},{7,5},{8,10},{9,11},{10,... | collective-permute-start | bytes 1572872 | tf_op jit(solution)/shard_map/ppermute | solution.py:298
  747.1 69.9 %collective-permute-start.37 = (s16[64,32,128]{2,1,0:T(8,128)(2,1)}, s16[64,32,128]{2,1,0:T(8,128)(2,1)}, u32[]{:S(2)}, u32[]{:S(2)}) collective-permute-start(s16[64,32,128]{2,1,0:T(8,128)(2,1)} %get-tuple-element.112), channel_id=1, source_target_pairs={{0,3},{1,2},{2,1},{3,0},{4,7},{5,6},{6,5},{7,4},{8,11},{9,10},{10,... | collective-permute-start | bytes 1572872 | tf_op jit(solution)/shard_map/ppermute | solution.py:298
  747.2 69.8 %collective-permute-start.38 = (s16[64,32,128]{2,1,0:T(8,128)(2,1)}, s16[64,32,128]{2,1,0:T(8,128)(2,1)}, u32[]{:S(2)}, u32[]{:S(2)}) collective-permute-start(s16[64,32,128]{2,1,0:T(8,128)(2,1)} %get-tuple-element.113), channel_id=1, source_target_pairs={{0,4},{1,5},{2,6},{3,7},{4,0},{5,1},{6,2},{7,3},{8,12},{9,13},{10,... | collective-permute-start | bytes 1572872 | tf_op jit(solution)/shard_map/ppermute | solution.py:298
  805.2 36.0 %collective-permute-start.39 = (s16[64,32,128]{2,1,0:T(8,128)(2,1)}, s16[64,32,128]{2,1,0:T(8,128)(2,1)}, u32[]{:S(2)}, u32[]{:S(2)}) collective-permute-start(s16[64,32,128]{2,1,0:T(8,128)(2,1)} %get-tuple-element.114), channel_id=1, source_target_pairs={{0,5},{1,4},{2,7},{3,6},{4,1},{5,0},{6,3},{7,2},{8,13},{9,12},{10,... | collective-permute-start | bytes 1572872 | tf_op jit(solution)/shard_map/ppermute | solution.py:298
  844.6 46.7 %collective-permute-start.32 = (s16[64,32,128]{2,1,0:T(8,128)(2,1)}, s16[64,32,128]{2,1,0:T(8,128)(2,1)S(1)}, u32[]{:S(2)}, u32[]{:S(2)}) collective-permute-start(s16[64,32,128]{2,1,0:T(8,128)(2,1)} %get-tuple-element.104), channel_id=1, source_target_pairs={{0,5},{1,4},{2,7},{3,6},{4,1},{5,0},{6,3},{7,2},{8,13},{9,12},{10,... | collective-permute-start | bytes 1572872 | tf_op jit(solution)/shard_map/ppermute | solution.py:298
  845.0 46.3 %collective-permute-start.33 = (s16[64,32,128]{2,1,0:T(8,128)(2,1)}, s16[64,32,128]{2,1,0:T(8,128)(2,1)S(1)}, u32[]{:S(2)}, u32[]{:S(2)}) collective-permute-start(s16[64,32,128]{2,1,0:T(8,128)(2,1)} %get-tuple-element.105), channel_id=1, source_target_pairs={{0,6},{1,7},{2,4},{3,5},{4,2},{5,3},{6,0},{7,1},{8,14},{9,15},{10,... | collective-permute-start | bytes 1572872 | tf_op jit(solution)/shard_map/ppermute | solution.py:298
  851.6 39.6 %collective-permute-start.34 = (s16[64,32,128]{2,1,0:T(8,128)(2,1)}, s16[64,32,128]{2,1,0:T(8,128)(2,1)S(1)}, u32[]{:S(2)}, u32[]{:S(2)}) collective-permute-start(s16[64,32,128]{2,1,0:T(8,128)(2,1)} %get-tuple-element.106), channel_id=1, source_target_pairs={{0,7},{1,6},{2,5},{3,4},{4,3},{5,2},{6,1},{7,0},{8,15},{9,14},{10,... | collective-permute-start | bytes 1572872 | tf_op jit(solution)/shard_map/ppermute | solution.py:298
  (53 other events, 981.3 us)
Sparse Core Ops, SparseCore 0:
  33.5 29.6 all-gather.1

commit v2 on v1

v2 whole, which is shorter than its diff:
```python
import functools
import jax
import jax.numpy as jnp
from jax import lax
from jax.experimental import pallas as pl
from jax.experimental.pallas import tpu as pltpu
from jax.sharding import PartitionSpec as P

F32, BF16, I16, I32 = jnp.float32, jnp.bfloat16, jnp.int16, jnp.int32
EXACT, HIGH = lax.Precision.HIGHEST, lax.Precision.HIGH
NOISE_VAR = 0.25
SPECTRUM_MAX = 4.0
HOURLY_MAX = 400.0
STEPS = 1024.0
LEAST = -18.0
CODE_MAX = 2.0**13.5
GROUP = 16
HALVES = 2
VMEM = 52 * 1024 * 1024


def encode(x):
    size = jnp.maximum(jnp.abs(x), 2.0**LEAST)
    code = (jnp.log(size) * (STEPS / 0.6931471805599453) + (0.5 - STEPS * LEAST)).astype(I32)
    return jnp.where(x < 0, -code, code).astype(I16)


def decode(code):
    wide = code.astype(I32)
    size = jnp.exp2(jnp.abs(wide).astype(F32) * (1.0 / STEPS) + LEAST)
    size = jnp.where(wide == 0, 0.0, size)
    return jnp.where(wide < 0, -size, size)


def dot(a, b):
    return jnp.dot(a, b, preferred_element_type=F32)


def dot_rows(a, b):
    return lax.dot_general(a, b, (((1,), (1,)), ((), ())), preferred_element_type=F32)


def two_part_dot(a, b):
    top = a.astype(BF16)
    rest = (a - top.astype(F32)).astype(BF16)
    both = dot(jnp.concatenate([top, rest], axis=0), b)
    return both[: a.shape[0]] + both[a.shape[0] :]


def fold(x):
    rows, cols = x.shape
    x = jnp.sum(x.reshape(rows // 8, 8, cols), axis=0)
    total = x[:, :128]
    for start in range(128, cols, 128):
        total = total + x[:, start : start + 128]
    return total


def whole_spec(shape):
    return pl.BlockSpec(shape, lambda i: (0,) * len(shape))


SCALARS = pl.BlockSpec(memory_space=pltpu.SMEM)
ANYWHERE = pl.BlockSpec(memory_space=pl.ANY)


def struct(shape, kind):
    return jax.ShapeDtypeStruct(shape, kind)


class Kernels:
    def __init__(self, zs, qs, hour_local, lat_local, lat_rows, lon_local):
        self.zs, self.qs = zs, qs
        self.al, self.lr, self.ol = lat_local, lat_rows, lon_local
        self.hl = hour_local
        self.hp = hour_local // HALVES
        self.hours, self.lats, self.lons = zs * hour_local, zs * lat_local, qs * lon_local
        self.cells = self.hp * lat_rows * self.lons
        self.token = None

    def call(self, body, name, grid, out_shape, in_specs, out_specs, flops, moved, scratch=(), aliases={}):
        tokens = [] if self.token is None else [self.token]

        def run(*args):
            def whole(*refs):
                refs = list(refs)
                del refs[len(args) : len(args) + len(tokens)]
                place = len(args) + len(out_shape)
                token_ref = refs.pop(place)
                token_ref[...] = jnp.zeros_like(token_ref)
                body(*refs)

            out = pl.pallas_call(
                whole,
                name=name,
                grid=(grid,),
                out_shape=list(out_shape) + [struct((8, 128), F32)],
                in_specs=list(in_specs) + [ANYWHERE] * len(tokens),
                out_specs=list(out_specs) + [whole_spec((8, 128))],
                scratch_shapes=list(scratch),
                input_output_aliases=aliases,
                compiler_params=pltpu.CompilerParams(vmem_limit_bytes=VMEM),
                cost_estimate=pl.CostEstimate(flops=flops, bytes_accessed=moved, transcendentals=0),
            )(*args, *tokens)
            self.token = out[-1]
            return out[:-1]

        return run

    def after(self, x):
        return pl.pallas_call(
            lambda x_ref, token_ref, out_ref: None,
            name="after",
            out_shape=struct(x.shape, x.dtype),
            in_specs=[ANYWHERE, ANYWHERE],
            out_specs=ANYWHERE,
            input_output_aliases={0: 0},
            compiler_params=pltpu.CompilerParams(vmem_limit_bytes=VMEM),
            cost_estimate=pl.CostEstimate(flops=0, bytes_accessed=0, transcendentals=0),
        )(x, self.token)

    def parts_specs(self, group):
        return [pl.BlockSpec((group, self.lr, self.ol), lambda i: (i, 0, 0))] * self.qs

    def parts_shape(self, kind):
        return [struct((self.hp, self.lr, self.ol), kind)] * self.qs

    def grid_spec(self, group, c=None):
        start = 0 if c is None else c * (self.hp // group)
        return pl.BlockSpec((group, self.lr, self.lons), lambda i: (i + start, 0, 0))

    def hourly(self, noise, tables):
        zs, hp, al, ol, hours = self.zs, self.hp, self.al, self.ol, self.hours
        periods = noise.shape[3]

        def body(noise_ref, table_ref, *refs):
            outs, turned = refs[:HALVES], refs[HALVES]
            for start in range(0, GROUP, 4):
                part = noise_ref[:, start : start + 4].reshape(2, 4 * ol, periods)
                total = dot_rows(table_ref[0], part[0]) + dot_rows(table_ref[1], part[1])
                for k in range(4):
                    turned[pl.ds(start + k, hours, stride=GROUP), :] = total[:, k * ol : (k + 1) * ol]
            value = turned[...].reshape(HALVES, zs, hp, GROUP, ol).astype(BF16)
            for c in range(HALVES):
                outs[c][...] = value[c]

        return self.call(
            body, "hourly", al // GROUP, [struct((zs, hp, al, ol), BF16)] * HALVES,
            [pl.BlockSpec((2, GROUP, ol, periods), lambda i: (0, i, 0, 0)), whole_spec(tables.shape)],
            [pl.BlockSpec((zs, hp, GROUP, ol), lambda i: (0, 0, i, 0))] * HALVES,
            4 * hours * periods * al * ol, 2 * noise.size + 2 * hours * al * ol,
            [pltpu.VMEM((hours * GROUP, ol), F32)],
        )(noise, tables)

    def lat_up(self, g, lat, gain):
        zs, qs, hp, lr, ol, lats = self.zs, self.qs, self.hp, self.lr, self.ol, self.lats
        group = 8

        def body(gain_ref, g_ref, lat_ref, *outs):
            for start in range(0, group, 4):
                part = [g_ref[:, start + k].reshape(lats, ol) for k in range(4)]
                total = dot(lat_ref[...], jnp.concatenate(part, axis=1))
                code = encode(total * gain_ref[0])
                for k in range(4):
                    for d in range(qs):
                        outs[d][start + k] = code[d * lr : (d + 1) * lr, k * ol : (k + 1) * ol]

        return self.call(
            body, "lat_up", hp // group, self.parts_shape(I16),
            [SCALARS, pl.BlockSpec((zs, group, self.al, ol), lambda i: (0, i, 0, 0)), whole_spec(lat.shape)],
            self.parts_specs(group), 2 * self.cells * self.lats, 4 * self.cells,
        )(gain.reshape(1), g, lat)

    def residual(self, c, codes, back, lon_up, lon_down, observed, mask):
        qs, hp, lr, ol, lons = self.qs, self.hp, self.lr, self.ol, self.lons
        group = 8
        rows = group * lr

        def body(back_ref, *refs):
            arrived, (up_ref, down_ref, observed_ref, mask_ref) = refs[:qs], refs[qs : qs + 4]
            prior_ref, norm_ref, outs = refs[qs + 4], refs[qs + 5], refs[qs + 6 :]
            x = jnp.concatenate([decode(a[...].reshape(rows, ol)) for a in arrived], axis=1)
            prior = two_part_dot(x, up_ref[...]) * back_ref[0]
            prior_ref[...] = prior.reshape(group, lr, lons)
            seen = mask_ref[...].reshape(rows, lons).astype(F32)
            resid = seen * (observed_ref[...].reshape(rows, lons) - prior)

            @pl.when(pl.program_id(0) == 0)
            def _():
                norm_ref[...] = jnp.zeros_like(norm_ref)

            norm_ref[...] += fold(resid * resid)
            v = two_part_dot(resid, down_ref[...]).astype(BF16)
            for d in range(qs):
                outs[d][...] = v[:, d * ol : (d + 1) * ol].reshape(group, lr, ol)

        out = self.call(
            body, "residual", hp // group,
            [struct((hp, lr, lons), F32), struct((8, 128), F32)] + self.parts_shape(BF16),
            [SCALARS] + self.parts_specs(group) + [whole_spec(lon_up.shape)] * 2 + [self.grid_spec(group, c)] * 2,
            [self.grid_spec(group), whole_spec((8, 128))] + self.parts_specs(group),
            8 * self.cells * lons, 16 * self.cells,
        )(back.reshape(1), *codes, lon_up, lon_down, observed, mask)
        return out[0], out[1], out[2:]

    def lat_down(self, v, lat_t):
        zs, qs, hp, al, lr, ol, lats = self.zs, self.qs, self.hp, self.al, self.lr, self.ol, self.lats

        def body(*refs):
            sent, (lat_ref, out_ref, turned) = refs[:qs], refs[qs:]
            for start in range(0, GROUP, 4):
                part = [jnp.concatenate([s[start + k] for s in sent], axis=0) for k in range(4)]
                total = dot(lat_ref[...], jnp.concatenate(part, axis=1))
                for k in range(4):
                    turned[pl.ds(start + k, lats, stride=GROUP), :] = total[:, k * ol : (k + 1) * ol]
            out_ref[...] = turned[...].reshape(zs, al, GROUP, ol).astype(BF16)

        return self.call(
            body, "lat_down", hp // GROUP, [struct((zs, al, hp, ol), BF16)],
            self.parts_specs(GROUP) + [whole_spec(lat_t.shape)],
            [pl.BlockSpec((zs, al, GROUP, ol), lambda i: (0, 0, i, 0))],
            2 * self.cells * lats, 4 * self.cells,
            [pltpu.VMEM((lats * GROUP, ol), F32)],
        )(*v, lat_t)[0]

    def over_hours(self, halves, kern):
        zs, hp, al, ol, hours = self.zs, self.hp, self.al, self.ol, self.hours

        def body(*refs):
            sent, kern_ref, outs = refs[:HALVES], refs[HALVES], refs[HALVES + 1 : 2 * HALVES + 1]
            bend_ref, turned = refs[2 * HALVES + 1 :]

            @pl.when(pl.program_id(0) == 0)
            def _():
                bend_ref[...] = jnp.zeros_like(bend_ref)

            for start in range(0, GROUP, 4):
                part = [
                    jnp.concatenate([x[:, start + k].reshape(zs * hp, ol) for x in sent], axis=0) for k in range(4)
                ]
                part = jnp.concatenate(part, axis=1)
                total = dot(kern_ref[0], part) + dot(kern_ref[1], part)
                bend_ref[...] += fold(total * part.astype(F32))
                for k in range(4):
                    turned[pl.ds(start + k, hours, stride=GROUP), :] = total[:, k * ol : (k + 1) * ol]
            value = turned[...].reshape(HALVES, zs, hp, GROUP, ol).astype(BF16)
            for c in range(HALVES):
                outs[c][...] = value[c]

        out = self.call(
            body, "over_hours", al // GROUP, [struct((zs, hp, al, ol), BF16)] * HALVES + [struct((8, 128), F32)],
            [pl.BlockSpec((zs, GROUP, hp, ol), lambda i: (0, i, 0, 0))] * HALVES + [whole_spec(kern.shape)],
            [pl.BlockSpec((zs, hp, GROUP, ol), lambda i: (0, 0, i, 0))] * HALVES + [whole_spec((8, 128))],
            8 * self.cells * hours, 8 * self.cells,
            [pltpu.VMEM((hours * GROUP, ol), F32)],
        )(*halves, kern)
        return out[:HALVES], out[-1]

    def finish(self, s, c, codes, back, step, lon_up, prior, observed, mask, earlier):
        qs, hp, lr, ol, lons = self.qs, self.hp, self.lr, self.ol, self.lons
        group = 8
        rows = group * lr

        def body(scalar_ref, *refs):
            arrived, (up_ref, prior_ref, observed_ref, mask_ref) = refs[:qs], refs[qs : qs + 4]
            posterior_ref, next_ref = refs[-2:]
            x = jnp.concatenate([decode(a[...].reshape(rows, ol)) for a in arrived], axis=1)
            scaled = two_part_dot(x, up_ref[...]) * scalar_ref[0]
            prior = prior_ref[...].reshape(rows, lons)
            seen = mask_ref[...].reshape(rows, lons).astype(F32)
            resid = seen * (observed_ref[...].reshape(rows, lons) - prior)
            shape = (1, group, lr, lons)
            posterior_ref[...] = (prior + scaled).reshape(shape)
            next_ref[...] = (resid - seen * scaled - scalar_ref[1] * resid).reshape(shape)

        full = struct((2, self.hl, lr, lons), F32)
        start = c * (hp // group)
        out_spec = pl.BlockSpec((1, group, lr, lons), lambda i: (s, i + start, 0, 0))
        count = 1 + qs + 4
        return self.call(
            body, "finish", hp // group, [full, full],
            [SCALARS] + self.parts_specs(group) + [whole_spec(lon_up.shape), self.grid_spec(group)]
            + [self.grid_spec(group, c)] * 2 + [ANYWHERE] * len(earlier),
            [out_spec, out_spec], 4 * self.cells * lons, 22 * self.cells,
            aliases={count + i: i for i in range(len(earlier))},
        )(jnp.stack([back * step, NOISE_VAR * step]), *codes, lon_up, prior, observed, mask, *earlier)

    def joined(self, earlier):
        return tuple(earlier)


class Plain(Kernels):
    def after(self, x):
        return x

    def hourly(self, noise, tables):
        h = jnp.einsum("cyxk,cjk->jyx", noise, tables, preferred_element_type=F32).astype(BF16)
        h = h.reshape(HALVES, self.zs, self.hp, self.al, self.ol)
        return [h[c] for c in range(HALVES)]

    def lat_up(self, g, lat, gain):
        split = lat.reshape(self.qs, self.lr, self.zs, self.al)
        x = encode(jnp.einsum("qlzy,zhyx->qhlx", split, g, preferred_element_type=F32) * gain)
        return [x[d] for d in range(self.qs)]

    def up(self, codes, lon_up):
        x = jnp.concatenate([decode(c) for c in codes], axis=2)
        return jnp.einsum("hlx,xo->hlo", x, lon_up.astype(F32), precision=HIGH)

    def half(self, x, c):
        return x[c * self.hp : (c + 1) * self.hp]

    def residual(self, c, codes, back, lon_up, lon_down, observed, mask):
        prior = self.up(codes, lon_up) * back
        resid = self.half(mask, c).astype(F32) * (self.half(observed, c) - prior)
        v = jnp.einsum("hlo,op->hlp", resid, lon_down.astype(F32), precision=HIGH).astype(BF16)
        return prior, jnp.sum(resid * resid), jnp.split(v, self.qs, axis=2)

    def lat_down(self, v, lat_t):
        split = lat_t.reshape(self.zs, self.al, self.qs, self.lr)
        x = jnp.einsum("zyql,qhlx->zyhx", split, jnp.stack(v), preferred_element_type=F32)
        return x.astype(BF16)

    def over_hours(self, halves, kern):
        x = jnp.concatenate([jnp.swapaxes(h, 0, 1).reshape(self.al, -1, self.ol) for h in halves], axis=1)
        x = x.astype(F32)
        y = jnp.einsum("gk,ykx->gyx", kern.astype(F32).sum(0), x, precision=HIGH)
        bend = jnp.einsum("gyx,ygx->", y, x)
        y = y.astype(BF16).reshape(HALVES, self.zs, self.hp, self.al, self.ol)
        return [y[c] for c in range(HALVES)], bend

    def finish(self, s, c, codes, back, step, lon_up, prior, observed, mask, earlier):
        scaled = self.up(codes, lon_up) * (back * step)
        seen = self.half(mask, c).astype(F32)
        resid = seen * (self.half(observed, c) - prior)
        return tuple(earlier) + ((prior + scaled, resid - seen * scaled - NOISE_VAR * step * resid),)

    def joined(self, earlier):
        whole = []
        for i in range(2):
            samples = [
                jnp.concatenate([pair[i] for pair in earlier[s * HALVES : (s + 1) * HALVES]])
                for s in range(2)
            ]
            whole.append(jnp.stack(samples))
        return tuple(whole)


def swap_tm(x):
    return lax.all_to_all(x, "tm", split_axis=0, concat_axis=0, tiled=True)


def swap_lon(parts):
    count = len(parts)
    return [parts[0]] + [
        lax.ppermute(parts[d], "lon", [(i, i ^ d) for i in range(count)]) for d in range(1, count)
    ]


def largest_norm(factor, axis):
    return jnp.sqrt(jnp.max(jnp.sum(jnp.square(factor.astype(F32)), axis=axis)))


def shards(noise, observed, mask, lat_factor, lon_factor, spectrum):
    _, lat_local, lon_local, periods = noise.shape
    hour_local, lat_rows, lon_count = observed.shape
    hours = periods // 2
    hour_part = hour_local // HALVES
    zs, qs = hours // hour_local, lon_count // lon_local
    lat_count = zs * lat_local
    fits = lon_local % 128 == 0 and lat_rows % 16 == 0
    fits = fits and lat_local % GROUP == 0 and hour_part % GROUP == 0
    stages = (Kernels if fits else Plain)(zs, qs, hour_local, lat_local, lat_rows, lon_local)
    order = lax.axis_index("lon") ^ jnp.arange(qs)

    powers = jnp.concatenate([spectrum, spectrum[1:-1][::-1]])
    amplitude = jnp.sqrt(powers / periods)
    clock = jnp.arange(HALVES)[:, None, None] * hour_part + jnp.arange(zs)[None, :, None] * hour_local
    clock = (clock + jnp.arange(hour_part)).reshape(hours, 1)
    phase = (clock * jnp.arange(periods) % periods).astype(F32) * (2.0 * jnp.pi / periods)
    cosine_tab, sine_tab = jnp.cos(phase), jnp.sin(phase)
    table_cos = (cosine_tab * amplitude).astype(BF16)
    table_sin = (sine_tab * amplitude).astype(BF16)
    tables = (jnp.stack([table_cos, table_sin]), jnp.stack([-table_sin, table_cos]))

    def hour_kernel():
        scaled = powers / periods
        kern = jnp.dot(cosine_tab * scaled, cosine_tab.T, precision=EXACT) + jnp.dot(
            sine_tab * scaled, sine_tab.T, precision=EXACT
        )
        top = lax.reduce_precision(kern, 8, 7)
        return jnp.stack([top.astype(BF16), (kern - top).astype(BF16)])

    lon = lax.all_gather(lon_factor, "lon", axis=0, tiled=True).reshape(lon_count, qs, lon_local)
    units = [(s, c) for s in range(2) for c in range(HALVES)]
    first, second, third, fourth = units
    wait = stages.after
    arrived, waves = {}, {}
    for s in range(2):
        for c, part in enumerate(stages.hourly(noise, tables[s])):
            waves[s, c] = part
    arrived[first] = swap_tm(waves[first])
    arrived[second] = swap_tm(wait(waves[second]))
    kern = hour_kernel()
    lon_down = jnp.take(lon, order, axis=1).reshape(lon_count, lon_count)
    lon_up = lon_down.T
    lat = jnp.take(lat_factor.reshape(qs, lat_rows, lat_count), order, axis=0)
    lat = lat.reshape(lat_count, lat_count)
    lat_t = lat.T
    lat_row_norm = largest_norm(lat_factor, 1)
    lon_col_norm = largest_norm(lon_down, 0)
    lat_norm = jnp.sqrt(jnp.sum(jnp.square(lat_factor.astype(F32))))
    first_gain = CODE_MAX / jnp.maximum(lat_row_norm * (lat_count**0.5 * HOURLY_MAX), 1e-30)
    codes, priors, norms, sent, down = {}, {}, {}, {}, {}

    def up(u):
        codes[u] = swap_lon(stages.lat_up(arrived[u], lat, first_gain))

    def middle(u):
        priors[u], norms[u], v = stages.residual(
            u[1], codes[u], 1.0 / first_gain, lon_up, lon_down, observed, mask
        )
        sent[u] = swap_lon(v)

    def lower(u):
        down[u] = stages.lat_down(sent[u], lat_t)

    up(first)
    middle(first)
    arrived[third] = swap_tm(wait(waves[third]))
    up(second)
    lower(first)
    middle(second)
    arrived[fourth] = swap_tm(wait(waves[fourth]))
    up(third)
    lower(second)
    down[first] = swap_tm(wait(down[first]))
    middle(third)
    up(fourth)
    lower(third)
    down[second] = swap_tm(wait(down[second]))
    middle(fourth)
    down[third] = swap_tm(wait(down[third]))
    lower(fourth)
    down[fourth] = swap_tm(down[fourth])

    sums = []
    for s in range(2):
        mine = [u for u in units if u[0] == s]
        sums.append(sum(jnp.sum(norms[u]) for u in mine))
        halves, bending = stages.over_hours([down[u] for u in mine], kern)
        sums.append(jnp.sum(bending))
        for u in mine:
            waves[u] = halves[u[1]]
    arrived[first] = swap_tm(waves[first])
    arrived[second] = swap_tm(wait(waves[second]))
    sums = lax.psum(jnp.stack(sums), ("tm", "lon"))
    gains, steps = [], []
    for s in range(2):
        norm_sq, bending = sums[2 * s], sums[2 * s + 1]
        bound = SPECTRUM_MAX * lat_row_norm * lat_norm * lon_col_norm * jnp.sqrt(norm_sq)
        gains.append(CODE_MAX / jnp.maximum(bound, 1e-30))
        steps.append(norm_sq / (bending + NOISE_VAR * norm_sq))
    earlier = ()
    for u in units:
        s, c = u
        codes = swap_lon(stages.lat_up(arrived[u], lat, gains[s]))
        later = {first: third, second: fourth}.get(u)
        earlier = stages.finish(s, c, codes, 1.0 / gains[s], steps[s], lon_up, priors[u], observed, mask, earlier)
        if later is not None:
            arrived[later] = swap_tm(wait(waves[later]))
    return stages.joined(earlier)


def solution(mesh):
    return jax.shard_map(
        shards,
        mesh=mesh,
        in_specs=(
            P(None, "tm", "lon", None),
            P("tm", "lon", None),
            P("tm", "lon", None),
            P(),
            P("lon", None),
            P(),
        ),
        out_specs=(P(None, "tm", "lon", None), P(None, "tm", "lon", None)),
        check_vma=False,
    )
```

time: 927 us -> 850 us (0.917)
  blocking collectives: 160 us -> 56.8 us
  waiting for transfers between devices: 449 us -> 368 us
  starting transfers between devices: 76.1 us -> 139 us
  Pallas kernels: 173 us -> 195 us
  local copies, waits for them, and re-layouts: 21.3 us -> 31 us
    psum x2 -> x1, blocking collectives: 160 us -> 56.8 us  [shards(): sums = lax.psum(jnp.stack(sums), ('tm', 'lon'))]
    all_to_all x6 -> x12, waiting for transfers between devices: 250 us -> 158 us  [swap_tm(): return lax.all_to_all(x, 'tm', split_axis=0, concat_axis=0, tiled=True)]
    ppermute x42 -> x84, starting transfers between devices: 44.2 us -> 82.1 us  [swap_lon(): lax.ppermute(parts[d], 'lon', [(i, i ^ d) for i in range(count)])]
    all_to_all x6 -> x12, starting transfers between devices: 31.8 us -> 56.9 us  [swap_tm(): return lax.all_to_all(x, 'tm', split_axis=0, concat_axis=0, tiled=True)]
    pallas_call x14 -> x33, Pallas kernels: 173 us -> 195 us  [the longest x24 195 us: run(): pl.pallas_call(whole, name=name, grid=(grid,), out_shape=list(out_shape)...]
    ppermute x42 -> x84, waiting for transfers between devices: 200 us -> 210 us  [swap_lon(): lax.ppermute(parts[d], 'lon', [(i, i ^ d) for i in range(count)])]
  transfers between devices with their start and end apart: 49 -> 97, of which waited for: 17 -> 42; matrix products, arithmetic and copies ran while one was open for 3% -> 4% of each run, Pallas kernels for 15% -> 20%
where the time goes in v2:
time: 850 us; the launch traced here: 839 us
  waiting for transfers between devices  368 us (43%)
  Pallas kernels  195 us (23%)
  starting transfers between devices  139 us (16%)
  blocking collectives  56.8 us (7%)
  local copies, waits for them, and re-layouts  31 us (4%)
  between operations  25.1 us (3%)
  other arithmetic  15.4 us (2%)
  matrix products  9.05 us (1%)
    ppermute x84, waiting for transfers between devices, swap_lon(): lax.ppermute(parts[d], 'lon', [(i, i ^ d) for i in range(count)])  210 us
    pallas_call x24, Pallas kernels, run(): pl.pallas_call(whole, name=name, grid=(grid,), out_shape=list(out_shape)...  195 us
    all_to_all x12, waiting for transfers between devices, swap_tm(): return lax.all_to_all(x, 'tm', split_axis=0, concat_axis=0, tiled=True)  158 us
    ppermute x84, starting transfers between devices, swap_lon(): lax.ppermute(parts[d], 'lon', [(i, i ^ d) for i in range(count)])  82.1 us
    all_to_all x12, starting transfers between devices, swap_tm(): return lax.all_to_all(x, 'tm', split_axis=0, concat_axis=0, tiled=True)  56.9 us
    psum x1, blocking collectives, shards(): sums = lax.psum(jnp.stack(sums), ('tm', 'lon'))  56.8 us
  transfers between devices with their start and end apart: 97, of which 42 were waited for; matrix products, arithmetic and copies ran while one was open for 4% of the time, Pallas kernels for 20%

profile of v2, /device:TPU:0, one launch (start us, length us, event | category | flops | bytes accessed | tf_op | source)
XLA Modules:
  0.0 839.5 jit_solution(18289820352907779404)
XLA Ops:
  43.5 36.1 %all-to-all-done.refs_1_ = bf16[4,32,64,128]{3,2,1,0:T(8,128)(2,1)S(1)} async-done(((bf16[4,32,64,128]{3,2,1,0:T(8,128)(2,1)}), bf16[4,32,64,128]{3,2,1,0:T(8,128)(2,1)S(1)}, u32[]{:S(2)}, u32[]{:S(2)}) %all-to-all-start) | async-done | bytes 2097184 | tf_op jit(solution)/shard_map/all_to_all | solution.py:350
  124.0 14.9 %residual.4 = (f32[32,32,1024]{2,1,0:T(8,128)}, f32[8,128]{1,0:T(8,128)S(1)}, bf16[32,32,128]{2,1,0:T(8,128)(2,1)S(1)}, bf16[32,32,128]{2,1,0:T(8,128)(2,1)S(1)}...) custom-call(f32[1]{0:T(128)} %bitcast.3.refs_0_, ...), custom_call_target="tpu_custom_call" | custom-call | flops 8589934592 | bytes 16777216 | tf_op jit(solution)/shard_map/residual/pallas_call | solution.py:93
  188.4 16.0 %collective-permute-done.11.refs_6_ = s16[32,32,128]{2,1,0:T(8,128)(2,1)} collective-permute-done((s16[32,32,128]{2,1,0:T(8,128)(2,1)S(1)}, s16[32,32,128]{2,1,0:T(8,128)(2,1)}, u32[]{:S(2)}, u32[]{:S(2)}) %collective-permute-start.11) | collective-permute-done | bytes 262176 | tf_op jit(solution)/shard_map/ppermute | solution.py:356
  205.2 14.8 %residual.5 = (f32[32,32,1024]{2,1,0:T(8,128)}, f32[8,128]{1,0:T(8,128)S(1)}, bf16[32,32,128]{2,1,0:T(8,128)(2,1)S(1)}, bf16[32,32,128]{2,1,0:T(8,128)(2,1)S(1)}...) custom-call(f32[1]{0:T(128)} %bitcast.3.refs_0_, ...), custom_call_target="tpu_custom_call" | custom-call | flops 8589934592 | bytes 16777216 | tf_op jit(solution)/shard_map/residual/pallas_call | solution.py:93
  239.3 12.3 %collective-permute-done.25.refs_5_ = bf16[32,32,128]{2,1,0:T(8,128)(2,1)S(1)} collective-permute-done((bf16[32,32,128]{2,1,0:T(8,128)(2,1)S(1)}, bf16[32,32,128]{2,1,0:T(8,128)(2,1)S(1)}, u32[]{:S(2)}, u32[]{:S(2)}) %collective-permute-start.25) | collective-permute-done | bytes 262176 | tf_op jit(solution)/shard_map/ppermute | solution.py:356
  256.1 17.6 %all-to-all-done.4.refs_1_ = bf16[4,32,64,128]{3,2,1,0:T(8,128)(2,1)} async-done(((bf16[4,32,64,128]{3,2,1,0:T(8,128)(2,1)}), bf16[4,32,64,128]{3,2,1,0:T(8,128)(2,1)}, u32[]{:S(2)}, u32[]{:S(2)}) %all-to-all-start.4) | async-done | bytes 2097184 | tf_op jit(solution)/shard_map/all_to_all | solution.py:350
  292.2 12.8 %collective-permute-done.32.refs_6_ = s16[32,32,128]{2,1,0:T(8,128)(2,1)S(1)} collective-permute-done((s16[32,32,128]{2,1,0:T(8,128)(2,1)S(1)}, s16[32,32,128]{2,1,0:T(8,128)(2,1)S(1)}, u32[]{:S(2)}, u32[]{:S(2)}) %collective-permute-start.32) | collective-permute-done | bytes 262176 | tf_op jit(solution)/shard_map/ppermute | solution.py:356
  305.9 14.7 %residual.6 = (f32[32,32,1024]{2,1,0:T(8,128)}, f32[8,128]{1,0:T(8,128)S(1)}, bf16[32,32,128]{2,1,0:T(8,128)(2,1)S(1)}, bf16[32,32,128]{2,1,0:T(8,128)(2,1)S(1)}...) custom-call(f32[1]{0:T(128)} %bitcast.3.refs_0_, ...), custom_call_target="tpu_custom_call" | custom-call | flops 8589934592 | bytes 16777216 | tf_op jit(solution)/shard_map/residual/pallas_call | solution.py:93
  335.0 13.1 %collective-permute-done.39.refs_5_ = bf16[32,32,128]{2,1,0:T(8,128)(2,1)S(1)} collective-permute-done((bf16[32,32,128]{2,1,0:T(8,128)(2,1)S(1)}, bf16[32,32,128]{2,1,0:T(8,128)(2,1)S(1)}, u32[]{:S(2)}, u32[]{:S(2)}) %collective-permute-start.39) | collective-permute-done | bytes 262176 | tf_op jit(solution)/shard_map/ppermute | solution.py:356
  371.7 12.6 %collective-permute-done.46.refs_6_ = s16[32,32,128]{2,1,0:T(8,128)(2,1)S(1)} collective-permute-done((s16[32,32,128]{2,1,0:T(8,128)(2,1)S(1)}, s16[32,32,128]{2,1,0:T(8,128)(2,1)S(1)}, u32[]{:S(2)}, u32[]{:S(2)}) %collective-permute-start.46) | collective-permute-done | bytes 262176 | tf_op jit(solution)/shard_map/ppermute | solution.py:356
  385.2 14.8 %residual.7 = (f32[32,32,1024]{2,1,0:T(8,128)}, f32[8,128]{1,0:T(8,128)S(1)}, bf16[32,32,128]{2,1,0:T(8,128)(2,1)S(1)}, bf16[32,32,128]{2,1,0:T(8,128)(2,1)S(1)}...) custom-call(f32[1]{0:T(128)} %bitcast.3.refs_0_, ...), custom_call_target="tpu_custom_call" | custom-call | flops 8589934592 | bytes 16777216 | tf_op jit(solution)/shard_map/residual/pallas_call | solution.py:93
  425.0 12.8 %collective-permute-done.53.refs_5_ = bf16[32,32,128]{2,1,0:T(8,128)(2,1)S(1)} collective-permute-done((bf16[32,32,128]{2,1,0:T(8,128)(2,1)S(1)}, bf16[32,32,128]{2,1,0:T(8,128)(2,1)S(1)}, u32[]{:S(2)}, u32[]{:S(2)}) %collective-permute-start.53) | collective-permute-done | bytes 262176 | tf_op jit(solution)/shard_map/ppermute | solution.py:356
  442.1 16.9 %all-to-all-done.6.refs_0_ = bf16[4,64,32,128]{3,2,1,0:T(8,128)(2,1)} async-done(((bf16[4,64,32,128]{3,2,1,0:T(8,128)(2,1)}), bf16[4,64,32,128]{3,2,1,0:T(8,128)(2,1)}, u32[]{:S(2)}, u32[]{:S(2)}) %all-to-all-start.6) | async-done | bytes 2097184 | tf_op jit(solution)/shard_map/all_to_all | solution.py:350
  479.1 31.4 %all-to-all-done.7.refs_1_ = bf16[4,64,32,128]{3,2,1,0:T(8,128)(2,1)S(1)} async-done(((bf16[4,64,32,128]{3,2,1,0:T(8,128)(2,1)}), bf16[4,64,32,128]{3,2,1,0:T(8,128)(2,1)S(1)}, u32[]{:S(2)}, u32[]{:S(2)}) %all-to-all-start.7) | async-done | bytes 2097184 | tf_op jit(solution)/shard_map/all_to_all | solution.py:350
  523.5 40.6 %all-to-all-done.9.refs_1_ = bf16[4,32,64,128]{3,2,1,0:T(8,128)(2,1)} async-done(((bf16[4,32,64,128]{3,2,1,0:T(8,128)(2,1)}), bf16[4,32,64,128]{3,2,1,0:T(8,128)(2,1)}, u32[]{:S(2)}, u32[]{:S(2)}) %all-to-all-start.9) | async-done | bytes 2097184 | tf_op jit(solution)/shard_map/all_to_all | solution.py:350
  579.1 56.8 %psum.7 = f32[4]{0:T(128)S(1)} all-reduce(f32[4]{0:T(128)S(1)} %pad_maximum_fusion.3), channel_id=1, replica_groups=mesh['tm'=4,'lon'=8] {'tm','lon'}, use_global_device_ids=true, to_apply=%region_11.12 | all-reduce | flops 4 | bytes 32 | tf_op jit(solution)/shard_map/psum | solution.py:457
  656.6 12.3 %collective-permute-done.60.refs_6_ = s16[32,32,128]{2,1,0:T(8,128)(2,1)S(1)} collective-permute-done((s16[32,32,128]{2,1,0:T(8,128)(2,1)S(1)}, s16[32,32,128]{2,1,0:T(8,128)(2,1)S(1)}, u32[]{:S(2)}, u32[]{:S(2)}) %collective-permute-start.60) | collective-permute-done | bytes 262176 | tf_op jit(solution)/shard_map/ppermute | solution.py:356
  669.7 11.8 %finish.4 = (f32[2,64,32,1024]{3,2,1,0:T(8,128)}, f32[2,64,32,1024]{3,2,1,0:T(8,128)}, f32[8,128]{1,0:T(8,128)S(1)}) custom-call(f32[2]{0:T(128)S(1)} %pad_maximum_fusion.5.refs_0_, s16[32,32,128]{2,1,0:T(8,128)(2,1)S(1)} %get-tuple-element.248.refs_1_, s16[32,32,128]{2,1,0:T(8,128)(2,1)S(1)} %collective-permute-done.56.refs_2_, ...), custom_call_target="tpu_custom_call" | custom-call | flops 4294967296 | bytes 23068672 | tf_op jit(solution)/shard_map/finish/pallas_call | solution.py:93
  704.5 12.7 %collective-permute-done.67.refs_6_ = s16[32,32,128]{2,1,0:T(8,128)(2,1)S(1)} collective-permute-done((s16[32,32,128]{2,1,0:T(8,128)(2,1)S(1)}, s16[32,32,128]{2,1,0:T(8,128)(2,1)S(1)}, u32[]{:S(2)}, u32[]{:S(2)}) %collective-permute-start.67) | collective-permute-done | bytes 262176 | tf_op jit(solution)/shard_map/ppermute | solution.py:356
  717.9 11.8 %finish.5 = (f32[2,64,32,1024]{3,2,1,0:T(8,128)}, f32[2,64,32,1024]{3,2,1,0:T(8,128)}, f32[8,128]{1,0:T(8,128)S(1)}) custom-call(f32[2]{0:T(128)S(1)} %pad_maximum_fusion.5.refs_0_, s16[32,32,128]{2,1,0:T(8,128)(2,1)S(1)} %get-tuple-element.259.refs_1_, ...), custom_call_target="tpu_custom_call", output_to_operand_aliasing={{0}: (13, {}), {1}: (14, {})} | custom-call | flops 4294967296 | bytes 23068672 | tf_op jit(solution)/shard_map/finish/pallas_call | solution.py:93
  759.5 12.5 %collective-permute-done.74.refs_6_ = s16[32,32,128]{2,1,0:T(8,128)(2,1)S(1)} collective-permute-done((s16[32,32,128]{2,1,0:T(8,128)(2,1)S(1)}, s16[32,32,128]{2,1,0:T(8,128)(2,1)S(1)}, u32[]{:S(2)}, u32[]{:S(2)}) %collective-permute-start.74) | collective-permute-done | bytes 262176 | tf_op jit(solution)/shard_map/ppermute | solution.py:356
  772.7 11.9 %finish.6 = (f32[2,64,32,1024]{3,2,1,0:T(8,128)}, f32[2,64,32,1024]{3,2,1,0:T(8,128)}, f32[8,128]{1,0:T(8,128)S(1)}) custom-call(f32[2]{0:T(128)S(1)} %pad_maximum_fusion.4.refs_0_, s16[32,32,128]{2,1,0:T(8,128)(2,1)S(1)} %get-tuple-element.273.refs_1_, ...), custom_call_target="tpu_custom_call", output_to_operand_aliasing={{0}: (13, {}), {1}: (14, {})} | custom-call | flops 4294967296 | bytes 23068672 | tf_op jit(solution)/shard_map/finish/pallas_call | solution.py:93
  807.2 12.4 %collective-permute-done.81.refs_6_ = s16[32,32,128]{2,1,0:T(8,128)(2,1)S(1)} collective-permute-done((s16[32,32,128]{2,1,0:T(8,128)(2,1)S(1)}, s16[32,32,128]{2,1,0:T(8,128)(2,1)S(1)}, u32[]{:S(2)}, u32[]{:S(2)}) %collective-permute-start.81) | collective-permute-done | bytes 262176 | tf_op jit(solution)/shard_map/ppermute | solution.py:356
  820.3 11.8 %finish.7 = (f32[2,64,32,1024]{3,2,1,0:T(8,128)}, f32[2,64,32,1024]{3,2,1,0:T(8,128)}, f32[8,128]{1,0:T(8,128)}) custom-call(f32[2]{0:T(128)S(1)} %pad_maximum_fusion.4.refs_0_, s16[32,32,128]{2,1,0:T(8,128)(2,1)S(1)} %get-tuple-element.286.refs_1_, ...), custom_call_target="tpu_custom_call", output_to_operand_aliasing={{0}: (13, {}), {1}: (14, {})} | custom-call | flops 4294967296 | bytes 23068672 | tf_op jit(solution)/shard_map/finish/pallas_call | solution.py:93
  (333 shorter events, 378.8 us)
Async XLA Ops:
  25.0 54.6 %all-to-all-start = ((bf16[4,32,64,128]{3,2,1,0:T(8,128)(2,1)}), bf16[4,32,64,128]{3,2,1,0:T(8,128)(2,1)S(1)}, u32[]{:S(2)}, u32[]{:S(2)}) async-start(bf16[4,32,64,128]{3,2,1,0:T(8,128)(2,1)} %get-tuple-element.151), calls=%async_computation | async-start | bytes 4194304 | tf_op jit(solution)/shard_map/all_to_all | solution.py:350
  31.4 66.0 %all-gather.2.cloned.1.call-start = ((), (), s32[]{:S(2)}) async-start(), calls=%async_computation.12 | async-start | bytes 2359296 | tf_op jit(solution)/shard_map/all_gather | solution.py:394
  80.9 57.9 %all-to-all-start.1 = ((bf16[4,32,64,128]{3,2,1,0:T(8,128)(2,1)}), bf16[4,32,64,128]{3,2,1,0:T(8,128)(2,1)}, u32[]{:S(2)}, u32[]{:S(2)}) async-start(bf16[4,32,64,128]{3,2,1,0:T(8,128)(2,1)} %after.9), calls=%async_computation.1 | async-start | bytes 4194304 | tf_op jit(solution)/shard_map/all_to_all | solution.py:350
  138.9 81.1 %all-to-all-start.2 = ((bf16[4,32,64,128]{3,2,1,0:T(8,128)(2,1)}), bf16[4,32,64,128]{3,2,1,0:T(8,128)(2,1)}, u32[]{:S(2)}, u32[]{:S(2)}) async-start(bf16[4,32,64,128]{3,2,1,0:T(8,128)(2,1)} %after.10), calls=%async_computation.2 | async-start | bytes 4194304 | tf_op jit(solution)/shard_map/all_to_all | solution.py:350
  173.1 31.3 %collective-permute-start.11 = (s16[32,32,128]{2,1,0:T(8,128)(2,1)S(1)}, s16[32,32,128]{2,1,0:T(8,128)(2,1)}, u32[]{:S(2)}, u32[]{:S(2)}) collective-permute-start(s16[32,32,128]{2,1,0:T(8,128)(2,1)S(1)} %get-tuple-element.171), channel_id=1, source_target_pairs={{0,5},{1,4},{2,7},{3,6},{4,1},{5,0},{6,3},{7,2},{8,13},{9,12},{10,... | collective-permute-start | bytes 786440 | tf_op jit(solution)/shard_map/ppermute | solution.py:356
  177.1 27.4 %collective-permute-start.12 = (s16[32,32,128]{2,1,0:T(8,128)(2,1)S(1)}, s16[32,32,128]{2,1,0:T(8,128)(2,1)S(1)}, u32[]{:S(2)}, u32[]{:S(2)}) collective-permute-start(s16[32,32,128]{2,1,0:T(8,128)(2,1)S(1)} %get-tuple-element.172), channel_id=1, source_target_pairs={{0,6},{1,7},{2,4},{3,5},{4,2},{5,3},{6,0},{7,1},{8,14},{9,15},{10,... | collective-permute-start | bytes 786440 | tf_op jit(solution)/shard_map/ppermute | solution.py:356
  220.0 53.7 %all-to-all-start.4 = ((bf16[4,32,64,128]{3,2,1,0:T(8,128)(2,1)}), bf16[4,32,64,128]{3,2,1,0:T(8,128)(2,1)}, u32[]{:S(2)}, u32[]{:S(2)}) async-start(bf16[4,32,64,128]{3,2,1,0:T(8,128)(2,1)} %after.12), calls=%async_computation.4 | async-start | bytes 4194304 | tf_op jit(solution)/shard_map/all_to_all | solution.py:350
  227.4 24.2 %collective-permute-start.25 = (bf16[32,32,128]{2,1,0:T(8,128)(2,1)S(1)}, bf16[32,32,128]{2,1,0:T(8,128)(2,1)S(1)}, u32[]{:S(2)}, u32[]{:S(2)}) collective-permute-start(bf16[32,32,128]{2,1,0:T(8,128)(2,1)S(1)} %get-tuple-element.191), channel_id=1, source_target_pairs={{0,5},{1,4},{2,7},{3,6},{4,1},{5,0},{6,3},{7,2},{8,13},{9,12},{10,... | collective-permute-start | bytes 786440 | tf_op jit(solution)/shard_map/ppermute | solution.py:356
  273.7 78.8 %all-to-all-start.3 = ((bf16[4,64,32,128]{3,2,1,0:T(8,128)(2,1)}), bf16[4,64,32,128]{3,2,1,0:T(8,128)(2,1)}, u32[]{:S(2)}, u32[]{:S(2)}) async-start(bf16[4,64,32,128]{3,2,1,0:T(8,128)(2,1)} %after.11), calls=%async_computation.3 | async-start | bytes 4194304 | tf_op jit(solution)/shard_map/all_to_all | solution.py:350
  280.7 24.4 %collective-permute-start.32 = (s16[32,32,128]{2,1,0:T(8,128)(2,1)S(1)}, s16[32,32,128]{2,1,0:T(8,128)(2,1)S(1)}, u32[]{:S(2)}, u32[]{:S(2)}) collective-permute-start(s16[32,32,128]{2,1,0:T(8,128)(2,1)S(1)} %get-tuple-element.204), channel_id=1, source_target_pairs={{0,5},{1,4},{2,7},{3,6},{4,1},{5,0},{6,3},{7,2},{8,13},{9,12},{10,... | collective-permute-start | bytes 786440 | tf_op jit(solution)/shard_map/ppermute | solution.py:356
  281.9 23.1 %collective-permute-start.33 = (s16[32,32,128]{2,1,0:T(8,128)(2,1)S(1)}, s16[32,32,128]{2,1,0:T(8,128)(2,1)S(1)}, u32[]{:S(2)}, u32[]{:S(2)}) collective-permute-start(s16[32,32,128]{2,1,0:T(8,128)(2,1)S(1)} %get-tuple-element.205), channel_id=1, source_target_pairs={{0,6},{1,7},{2,4},{3,5},{4,2},{5,3},{6,0},{7,1},{8,14},{9,15},{10,... | collective-permute-start | bytes 786440 | tf_op jit(solution)/shard_map/ppermute | solution.py:356
  323.1 24.9 %collective-permute-start.39 = (bf16[32,32,128]{2,1,0:T(8,128)(2,1)S(1)}, bf16[32,32,128]{2,1,0:T(8,128)(2,1)S(1)}, u32[]{:S(2)}, u32[]{:S(2)}) collective-permute-start(bf16[32,32,128]{2,1,0:T(8,128)(2,1)S(1)} %get-tuple-element.212), channel_id=1, source_target_pairs={{0,5},{1,4},{2,7},{3,6},{4,1},{5,0},{6,3},{7,2},{8,13},{9,12},{10,... | collective-permute-start | bytes 786440 | tf_op jit(solution)/shard_map/ppermute | solution.py:356
  324.6 23.4 %collective-permute-start.40 = (bf16[32,32,128]{2,1,0:T(8,128)(2,1)S(1)}, bf16[32,32,128]{2,1,0:T(8,128)(2,1)S(1)}, u32[]{:S(2)}, u32[]{:S(2)}) collective-permute-start(bf16[32,32,128]{2,1,0:T(8,128)(2,1)S(1)} %get-tuple-element.213), channel_id=1, source_target_pairs={{0,6},{1,7},{2,4},{3,5},{4,2},{5,3},{6,0},{7,1},{8,14},{9,15},{10,... | collective-permute-start | bytes 786440 | tf_op jit(solution)/shard_map/ppermute | solution.py:356
  352.5 54.1 %all-to-all-start.5 = ((bf16[4,64,32,128]{3,2,1,0:T(8,128)(2,1)}), bf16[4,64,32,128]{3,2,1,0:T(8,128)(2,1)}, u32[]{:S(2)}, u32[]{:S(2)}) async-start(bf16[4,64,32,128]{3,2,1,0:T(8,128)(2,1)} %after.13), calls=%async_computation.5 | async-start | bytes 4194304 | tf_op jit(solution)/shard_map/all_to_all | solution.py:350
  360.0 24.2 %collective-permute-start.46 = (s16[32,32,128]{2,1,0:T(8,128)(2,1)S(1)}, s16[32,32,128]{2,1,0:T(8,128)(2,1)S(1)}, u32[]{:S(2)}, u32[]{:S(2)}) collective-permute-start(s16[32,32,128]{2,1,0:T(8,128)(2,1)S(1)} %get-tuple-element.224), channel_id=1, source_target_pairs={{0,5},{1,4},{2,7},{3,6},{4,1},{5,0},{6,3},{7,2},{8,13},{9,12},{10,... | collective-permute-start | bytes 786440 | tf_op jit(solution)/shard_map/ppermute | solution.py:356
  406.5 52.5 %all-to-all-start.6 = ((bf16[4,64,32,128]{3,2,1,0:T(8,128)(2,1)}), bf16[4,64,32,128]{3,2,1,0:T(8,128)(2,1)}, u32[]{:S(2)}, u32[]{:S(2)}) async-start(bf16[4,64,32,128]{3,2,1,0:T(8,128)(2,1)} %after.14), calls=%async_computation.6 | async-start | bytes 4194304 | tf_op jit(solution)/shard_map/all_to_all | solution.py:350
  413.4 24.4 %collective-permute-start.53 = (bf16[32,32,128]{2,1,0:T(8,128)(2,1)S(1)}, bf16[32,32,128]{2,1,0:T(8,128)(2,1)S(1)}, u32[]{:S(2)}, u32[]{:S(2)}) collective-permute-start(bf16[32,32,128]{2,1,0:T(8,128)(2,1)S(1)} %get-tuple-element.232), channel_id=1, source_target_pairs={{0,5},{1,4},{2,7},{3,6},{4,1},{5,0},{6,3},{7,2},{8,13},{9,12},{10,... | collective-permute-start | bytes 786440 | tf_op jit(solution)/shard_map/ppermute | solution.py:356
  459.1 51.5 %all-to-all-start.7 = ((bf16[4,64,32,128]{3,2,1,0:T(8,128)(2,1)}), bf16[4,64,32,128]{3,2,1,0:T(8,128)(2,1)S(1)}, u32[]{:S(2)}, u32[]{:S(2)}) async-start(bf16[4,64,32,128]{3,2,1,0:T(8,128)(2,1)} %get-tuple-element.241), calls=%async_computation.7 | async-start | bytes 4194304 | tf_op jit(solution)/shard_map/all_to_all | solution.py:350
  511.9 52.3 %all-to-all-start.9 = ((bf16[4,32,64,128]{3,2,1,0:T(8,128)(2,1)}), bf16[4,32,64,128]{3,2,1,0:T(8,128)(2,1)}, u32[]{:S(2)}, u32[]{:S(2)}) async-start(bf16[4,32,64,128]{3,2,1,0:T(8,128)(2,1)} %get-tuple-element.247), calls=%async_computation.9 | async-start | bytes 4194304 | tf_op jit(solution)/shard_map/all_to_all | solution.py:350
  564.1 117.4 %all-to-all-start.8 = ((bf16[4,32,64,128]{3,2,1,0:T(8,128)(2,1)}), bf16[4,32,64,128]{3,2,1,0:T(8,128)(2,1)}, u32[]{:S(2)}, u32[]{:S(2)}) async-start(bf16[4,32,64,128]{3,2,1,0:T(8,128)(2,1)} %after.15), calls=%async_computation.8 | async-start | bytes 4194304 | tf_op jit(solution)/shard_map/all_to_all | solution.py:350
  681.5 52.8 %all-to-all-start.11 = ((bf16[4,32,64,128]{3,2,1,0:T(8,128)(2,1)}), bf16[4,32,64,128]{3,2,1,0:T(8,128)(2,1)S(1)}, u32[]{:S(2)}, u32[]{:S(2)}) async-start(bf16[4,32,64,128]{3,2,1,0:T(8,128)(2,1)} %after.17), calls=%async_computation.11 | async-start | bytes 4194304 | tf_op jit(solution)/shard_map/all_to_all | solution.py:350
  693.9 23.3 %collective-permute-start.67 = (s16[32,32,128]{2,1,0:T(8,128)(2,1)S(1)}, s16[32,32,128]{2,1,0:T(8,128)(2,1)S(1)}, u32[]{:S(2)}, u32[]{:S(2)}) collective-permute-start(s16[32,32,128]{2,1,0:T(8,128)(2,1)S(1)} %get-tuple-element.264), channel_id=1, source_target_pairs={{0,5},{1,4},{2,7},{3,6},{4,1},{5,0},{6,3},{7,2},{8,13},{9,12},{10,... | collective-permute-start | bytes 786440 | tf_op jit(solution)/shard_map/ppermute | solution.py:356
  694.0 23.2 %collective-permute-start.68 = (s16[32,32,128]{2,1,0:T(8,128)(2,1)S(1)}, s16[32,32,128]{2,1,0:T(8,128)(2,1)S(1)}, u32[]{:S(2)}, u32[]{:S(2)}) collective-permute-start(s16[32,32,128]{2,1,0:T(8,128)(2,1)S(1)} %get-tuple-element.265), channel_id=1, source_target_pairs={{0,6},{1,7},{2,4},{3,5},{4,2},{5,3},{6,0},{7,1},{8,14},{9,15},{10,... | collective-permute-start | bytes 786440 | tf_op jit(solution)/shard_map/ppermute | solution.py:356
  735.7 53.0 %all-to-all-start.10 = ((bf16[4,32,64,128]{3,2,1,0:T(8,128)(2,1)}), bf16[4,32,64,128]{3,2,1,0:T(8,128)(2,1)}, u32[]{:S(2)}, u32[]{:S(2)}) async-start(bf16[4,32,64,128]{3,2,1,0:T(8,128)(2,1)} %after.16), calls=%async_computation.10 | async-start | bytes 4194304 | tf_op jit(solution)/shard_map/all_to_all | solution.py:350
  (115 other events, 1401.6 us)
Sparse Core Ops, SparseCore 0:
  34.1 29.6 all-gather.1

commit v3 on v2

--- a/solution.py
+++ b/solution.py
@@ -16,6 +16,7 @@
 CODE_MAX = 2.0**13.5
 GROUP = 16
 HALVES = 2
+EASE = 4
 VMEM = 52 * 1024 * 1024
 
 
@@ -100,14 +101,14 @@
                 scratch_shapes=list(scratch),
                 input_output_aliases=aliases,
                 compiler_params=pltpu.CompilerParams(vmem_limit_bytes=VMEM),
-                cost_estimate=pl.CostEstimate(flops=flops, bytes_accessed=moved, transcendentals=0),
+                cost_estimate=pl.CostEstimate(flops=flops * EASE, bytes_accessed=moved * EASE, transcendentals=0),
             )(*args, *tokens)
             self.token = out[-1]
             return out[:-1]
 
         return run
 
-    def after(self, x):
+    def after(self, x, token=None):
         return pl.pallas_call(
             lambda x_ref, token_ref, out_ref: None,
             name="after",
@@ -117,7 +118,7 @@
             input_output_aliases={0: 0},
             compiler_params=pltpu.CompilerParams(vmem_limit_bytes=VMEM),
             cost_estimate=pl.CostEstimate(flops=0, bytes_accessed=0, transcendentals=0),
-        )(x, self.token)
+        )(x, self.token if token is None else token)
 
     def parts_specs(self, group):
         return [pl.BlockSpec((group, self.lr, self.ol), lambda i: (i, 0, 0))] * self.qs
@@ -290,7 +291,7 @@
 
 
 class Plain(Kernels):
-    def after(self, x):
+    def after(self, x, token=None):
         return x
 
     def hourly(self, noise, tables):
@@ -355,6 +356,18 @@
     return [parts[0]] + [
         lax.ppermute(parts[d], "lon", [(i, i ^ d) for i in range(count)]) for d in range(1, count)
     ]
+
+
+def add_over_tm(x, count):
+    return sum([lax.ppermute(x, "tm", [(i, i ^ d) for i in range(count)]) for d in range(1, count)], x)
+
+
+def add_over_lon(x, count):
+    d = 1
+    while d < count:
+        x = x + lax.ppermute(x, "lon", [(i, i ^ d) for i in range(count)])
+        d *= 2
+    return x
 
 
 def largest_norm(factor, axis):
@@ -430,8 +443,8 @@
     arrived[third] = swap_tm(wait(waves[third]))
     up(second)
     lower(first)
+    arrived[fourth] = swap_tm(wait(waves[fourth]))
     middle(second)
-    arrived[fourth] = swap_tm(wait(waves[fourth]))
     up(third)
     lower(second)
     down[first] = swap_tm(wait(down[first]))
@@ -453,8 +466,9 @@
         for u in mine:
             waves[u] = halves[u[1]]
     arrived[first] = swap_tm(waves[first])
-    arrived[second] = swap_tm(wait(waves[second]))
-    sums = lax.psum(jnp.stack(sums), ("tm", "lon"))
+    sums = add_over_tm(jnp.broadcast_to(jnp.stack(sums)[:, None], (4, 128)), zs)
+    arrived[second] = swap_tm(wait(waves[second], sums))
+    sums = add_over_lon(sums, qs)[:, 0]
     gains, steps = [], []
     for s in range(2):
         norm_sq, bending = sums[2 * s], sums[2 * s + 1]

time: 850 us -> 772 us (0.908)
  blocking collectives: 56.8 us -> 0 us
  waiting for transfers between devices: 368 us -> 330 us
  starting transfers between devices: 139 us -> 148 us
  local copies, waits for them, and re-layouts: 31 us -> 39.7 us
    psum x1 -> x0, blocking collectives: 56.8 us -> none  [shards(): sums = lax.psum(jnp.stack(sums), ('tm', 'lon'))]
    all_to_all x12, waiting for transfers between devices: 158 us -> 118 us  [swap_tm(): return lax.all_to_all(x, 'tm', split_axis=0, concat_axis=0, tiled=True)]
    ppermute x0 -> x6, waiting for transfers between devices: none -> 31.9 us  [the longest x3 28.9 us: add_over_tm(): lax.ppermute(x, 'tm', [(i, i ^ d) for i in range(count)])]
    ppermute x84, waiting for transfers between devices: 210 us -> 180 us  [swap_lon(): lax.ppermute(parts[d], 'lon', [(i, i ^ d) for i in range(count)])]
    unnamed x87 -> x115, local copies, waits for them, and re-layouts: 14.4 us -> 23.1 us
  transfers between devices with their start and end apart: 97 -> 103, of which waited for: 42 -> 47; matrix products, arithmetic and copies ran while one was open for 4% -> 5% of each run, Pallas kernels for 20% -> 23%
where the time goes in v3:
time: 772 us; the launch traced here: 762 us
  waiting for transfers between devices  330 us (43%)
  Pallas kernels  195 us (25%)
  starting transfers between devices  148 us (19%)
  local copies, waits for them, and re-layouts  39.7 us (5%)
  between operations  24.4 us (3%)
  other arithmetic  15.9 us (2%)
  matrix products  9.05 us (1%)
    pallas_call x24, Pallas kernels, run(): pl.pallas_call(whole, name=name, grid=(grid,), out_shape=list(out_shape)...  195 us
    ppermute x84, waiting for transfers between devices, swap_lon(): lax.ppermute(parts[d], 'lon', [(i, i ^ d) for i in range(count)])  180 us
    all_to_all x12, waiting for transfers between devices, swap_tm(): return lax.all_to_all(x, 'tm', split_axis=0, concat_axis=0, tiled=True)  118 us
    ppermute x84, starting transfers between devices, swap_lon(): lax.ppermute(parts[d], 'lon', [(i, i ^ d) for i in range(count)])  82.4 us
    all_to_all x12, starting transfers between devices, swap_tm(): return lax.all_to_all(x, 'tm', split_axis=0, concat_axis=0, tiled=True)  58.1 us
    ppermute x3, waiting for transfers between devices, add_over_tm(): lax.ppermute(x, 'tm', [(i, i ^ d) for i in range(count)])  28.9 us
    unnamed x115, local copies, waits for them, and re-layouts  23.1 us
  transfers between devices with their start and end apart: 103, of which 47 were waited for; matrix products, arithmetic and copies ran while one was open for 5% of the time, Pallas kernels for 23%

profile of v3, /device:TPU:0, one launch (start us, length us, event | category | flops | bytes accessed | tf_op | source)
XLA Modules:
  0.0 761.9 jit_solution(12373330042843361969)
XLA Ops:
  16.3 11.1 %hourly.2 = (bf16[4,32,64,128]{3,2,1,0:T(8,128)(2,1)}, bf16[4,32,64,128]{3,2,1,0:T(8,128)(2,1)}, f32[8,128]{1,0:T(8,128)S(1)}) custom-call(bf16[2,64,128,512]{3,2,1,0:T(8,128)(2,1)} %refs_0_.3, bf16[2,256,512]{2,1,0:T(8,128)(2,1)S(1)} %get-tuple-element.306.refs_1_), custom_call_target="tpu_custom_call" | custom-call | flops 17179869184 | bytes 83886080 | tf_op jit(solution)/shard_map/hourly/pallas_call | solution.py:94
  36.8 11.1 %hourly.3 = (bf16[4,32,64,128]{3,2,1,0:T(8,128)(2,1)}, bf16[4,32,64,128]{3,2,1,0:T(8,128)(2,1)}, f32[8,128]{1,0:T(8,128)S(1)}) custom-call(bf16[2,64,128,512]{3,2,1,0:T(8,128)(2,1)} %refs_0_.3, bf16[2,256,512]{2,1,0:T(8,128)(2,1)S(1)} %get-tuple-element.307.refs_1_, f32[8,128]{1,0:T(8,128)S(1)} %get-tuple-element.152.refs_2_), custom_call_target="tpu_custom_call" | custom-call | flops 17179869184 | bytes 83886080 | tf_op jit(solution)/shard_map/hourly/pallas_call | solution.py:94
  48.0 34.2 %all-to-all-done.refs_1_ = bf16[4,32,64,128]{3,2,1,0:T(8,128)(2,1)} async-done(((bf16[4,32,64,128]{3,2,1,0:T(8,128)(2,1)}), bf16[4,32,64,128]{3,2,1,0:T(8,128)(2,1)}, u32[]{:S(2)}, u32[]{:S(2)}) %all-to-all-start) | async-done | bytes 2097184 | tf_op jit(solution)/shard_map/all_to_all | solution.py:351
  122.2 14.8 %residual.4 = (f32[32,32,1024]{2,1,0:T(8,128)}, f32[8,128]{1,0:T(8,128)S(1)}, bf16[32,32,128]{2,1,0:T(8,128)(2,1)S(1)}, bf16[32,32,128]{2,1,0:T(8,128)(2,1)}, bf...) custom-call(f32[1]{0:T(128)} %bitcast.3.refs_0_, ...), custom_call_target="tpu_custom_call" | custom-call | flops 34359738368 | bytes 67108864 | tf_op jit(solution)/shard_map/residual/pallas_call | solution.py:94
  200.1 7.5 collective-permute-done.11.refs_6_
  207.5 14.8 %residual.5 = (f32[32,32,1024]{2,1,0:T(8,128)}, f32[8,128]{1,0:T(8,128)S(1)}, bf16[32,32,128]{2,1,0:T(8,128)(2,1)S(1)}, bf16[32,32,128]{2,1,0:T(8,128)(2,1)S(1)}...) custom-call(f32[1]{0:T(128)} %bitcast.3.refs_0_, ...), custom_call_target="tpu_custom_call" | custom-call | flops 34359738368 | bytes 67108864 | tf_op jit(solution)/shard_map/residual/pallas_call | solution.py:94
  238.1 11.4 %collective-permute-done.25.refs_5_ = bf16[32,32,128]{2,1,0:T(8,128)(2,1)S(1)} collective-permute-done((bf16[32,32,128]{2,1,0:T(8,128)(2,1)S(1)}, bf16[32,32,128]{2,1,0:T(8,128)(2,1)S(1)}, u32[]{:S(2)}, u32[]{:S(2)}) %collective-permute-start.25) | collective-permute-done | bytes 262176 | tf_op jit(solution)/shard_map/ppermute | solution.py:357
  275.2 14.8 %residual.6 = (f32[32,32,1024]{2,1,0:T(8,128)}, f32[8,128]{1,0:T(8,128)S(1)}, bf16[32,32,128]{2,1,0:T(8,128)(2,1)S(1)}, bf16[32,32,128]{2,1,0:T(8,128)(2,1)S(1)}...) custom-call(f32[1]{0:T(128)} %bitcast.3.refs_0_, ...), custom_call_target="tpu_custom_call" | custom-call | flops 34359738368 | bytes 67108864 | tf_op jit(solution)/shard_map/residual/pallas_call | solution.py:94
  338.9 10.4 %collective-permute-done.46.refs_6_ = s16[32,32,128]{2,1,0:T(8,128)(2,1)S(1)} collective-permute-done((s16[32,32,128]{2,1,0:T(8,128)(2,1)S(1)}, s16[32,32,128]{2,1,0:T(8,128)(2,1)S(1)}, u32[]{:S(2)}, u32[]{:S(2)}) %collective-permute-start.46) | collective-permute-done | bytes 262176 | tf_op jit(solution)/shard_map/ppermute | solution.py:357
  350.8 14.8 %residual.7 = (f32[32,32,1024]{2,1,0:T(8,128)}, f32[8,128]{1,0:T(8,128)S(1)}, bf16[32,32,128]{2,1,0:T(8,128)(2,1)S(1)}, bf16[32,32,128]{2,1,0:T(8,128)(2,1)S(1)}...) custom-call(f32[1]{0:T(128)} %bitcast.3.refs_0_, ...), custom_call_target="tpu_custom_call" | custom-call | flops 34359738368 | bytes 67108864 | tf_op jit(solution)/shard_map/residual/pallas_call | solution.py:94
  365.7 20.5 %all-to-all-done.5.refs_1_ = bf16[4,64,32,128]{3,2,1,0:T(8,128)(2,1)} async-done(((bf16[4,64,32,128]{3,2,1,0:T(8,128)(2,1)}), bf16[4,64,32,128]{3,2,1,0:T(8,128)(2,1)}, u32[]{:S(2)}, u32[]{:S(2)}) %all-to-all-start.5) | async-done | bytes 2097184 | tf_op jit(solution)/shard_map/all_to_all | solution.py:351
  404.6 12.8 %collective-permute-done.53.refs_5_ = bf16[32,32,128]{2,1,0:T(8,128)(2,1)S(1)} collective-permute-done((bf16[32,32,128]{2,1,0:T(8,128)(2,1)S(1)}, bf16[32,32,128]{2,1,0:T(8,128)(2,1)S(1)}, u32[]{:S(2)}, u32[]{:S(2)}) %collective-permute-start.53) | collective-permute-done | bytes 262176 | tf_op jit(solution)/shard_map/ppermute | solution.py:357
  421.8 16.6 %all-to-all-done.6.refs_0_ = bf16[4,64,32,128]{3,2,1,0:T(8,128)(2,1)} async-done(((bf16[4,64,32,128]{3,2,1,0:T(8,128)(2,1)}), bf16[4,64,32,128]{3,2,1,0:T(8,128)(2,1)}, u32[]{:S(2)}, u32[]{:S(2)}) %all-to-all-start.6) | async-done | bytes 2097184 | tf_op jit(solution)/shard_map/all_to_all | solution.py:351
  451.5 7.2 over_hours.2
  458.7 31.4 %all-to-all-done.7.refs_1_ = bf16[4,64,32,128]{3,2,1,0:T(8,128)(2,1)S(1)} async-done(((bf16[4,64,32,128]{3,2,1,0:T(8,128)(2,1)}), bf16[4,64,32,128]{3,2,1,0:T(8,128)(2,1)S(1)}, u32[]{:S(2)}, u32[]{:S(2)}) %all-to-all-start.7) | async-done | bytes 2097184 | tf_op jit(solution)/shard_map/all_to_all | solution.py:351
  514.8 28.9 %collective-permute-done.57 = f32[4,128]{1,0:T(4,128)S(1)} collective-permute-done((f32[4,128]{1,0:T(4,128)S(1)}, f32[4,128]{1,0:T(4,128)S(1)}, u32[]{:S(2)}, u32[]{:S(2)}) %collective-permute-start.57) | collective-permute-done | bytes 2080 | tf_op jit(solution)/shard_map/ppermute | solution.py:362
  577.5 12.0 %collective-permute-done.66.refs_6_ = s16[32,32,128]{2,1,0:T(8,128)(2,1)S(1)} collective-permute-done((s16[32,32,128]{2,1,0:T(8,128)(2,1)S(1)}, s16[32,32,128]{2,1,0:T(8,128)(2,1)S(1)}, u32[]{:S(2)}, u32[]{:S(2)}) %collective-permute-start.66) | collective-permute-done | bytes 262176 | tf_op jit(solution)/shard_map/ppermute | solution.py:357
  590.6 11.9 %finish.4 = (f32[2,64,32,1024]{3,2,1,0:T(8,128)}, f32[2,64,32,1024]{3,2,1,0:T(8,128)}, f32[8,128]{1,0:T(8,128)S(1)}) custom-call(f32[2]{0:T(128)S(1)} %pad_maximum_fusion.5.refs_0_, s16[32,32,128]{2,1,0:T(8,128)(2,1)S(1)} %get-tuple-element.248.refs_1_, s16[32,32,128]{2,1,0:T(8,128)(2,1)S(1)} %collective-permute-done.62.refs_2_, ...), custom_call_target="tpu_custom_call" | custom-call | flops 17179869184 | bytes 92274688 | tf_op jit(solution)/shard_map/finish/pallas_call | solution.py:94
  626.8 12.3 %collective-permute-done.73.refs_6_ = s16[32,32,128]{2,1,0:T(8,128)(2,1)S(1)} collective-permute-done((s16[32,32,128]{2,1,0:T(8,128)(2,1)S(1)}, s16[32,32,128]{2,1,0:T(8,128)(2,1)S(1)}, u32[]{:S(2)}, u32[]{:S(2)}) %collective-permute-start.73) | collective-permute-done | bytes 262176 | tf_op jit(solution)/shard_map/ppermute | solution.py:357
  639.8 11.9 %finish.5 = (f32[2,64,32,1024]{3,2,1,0:T(8,128)}, f32[2,64,32,1024]{3,2,1,0:T(8,128)}, f32[8,128]{1,0:T(8,128)S(1)}) custom-call(f32[2]{0:T(128)S(1)} %pad_maximum_fusion.5.refs_0_, s16[32,32,128]{2,1,0:T(8,128)(2,1)S(1)} %get-tuple-element.259.refs_1_, ...), custom_call_target="tpu_custom_call", output_to_operand_aliasing={{0}: (13, {}), {1}: (14, {})} | custom-call | flops 17179869184 | bytes 92274688 | tf_op jit(solution)/shard_map/finish/pallas_call | solution.py:94
  681.9 12.2 %collective-permute-done.80.refs_6_ = s16[32,32,128]{2,1,0:T(8,128)(2,1)S(1)} collective-permute-done((s16[32,32,128]{2,1,0:T(8,128)(2,1)S(1)}, s16[32,32,128]{2,1,0:T(8,128)(2,1)S(1)}, u32[]{:S(2)}, u32[]{:S(2)}) %collective-permute-start.80) | collective-permute-done | bytes 262176 | tf_op jit(solution)/shard_map/ppermute | solution.py:357
  695.0 11.9 %finish.6 = (f32[2,64,32,1024]{3,2,1,0:T(8,128)}, f32[2,64,32,1024]{3,2,1,0:T(8,128)}, f32[8,128]{1,0:T(8,128)S(1)}) custom-call(f32[2]{0:T(128)S(1)} %pad_maximum_fusion.4.refs_0_, s16[32,32,128]{2,1,0:T(8,128)(2,1)S(1)} %get-tuple-element.273.refs_1_, ...), custom_call_target="tpu_custom_call", output_to_operand_aliasing={{0}: (13, {}), {1}: (14, {})} | custom-call | flops 17179869184 | bytes 92274688 | tf_op jit(solution)/shard_map/finish/pallas_call | solution.py:94
  729.9 12.1 %collective-permute-done.87.refs_6_ = s16[32,32,128]{2,1,0:T(8,128)(2,1)S(1)} collective-permute-done((s16[32,32,128]{2,1,0:T(8,128)(2,1)S(1)}, s16[32,32,128]{2,1,0:T(8,128)(2,1)S(1)}, u32[]{:S(2)}, u32[]{:S(2)}) %collective-permute-start.87) | collective-permute-done | bytes 262176 | tf_op jit(solution)/shard_map/ppermute | solution.py:357
  742.8 11.8 %finish.7 = (f32[2,64,32,1024]{3,2,1,0:T(8,128)}, f32[2,64,32,1024]{3,2,1,0:T(8,128)}, f32[8,128]{1,0:T(8,128)}) custom-call(f32[2]{0:T(128)S(1)} %pad_maximum_fusion.4.refs_0_, s16[32,32,128]{2,1,0:T(8,128)(2,1)S(1)} %get-tuple-element.286.refs_1_, ...), custom_call_target="tpu_custom_call", output_to_operand_aliasing={{0}: (13, {}), {1}: (14, {})} | custom-call | flops 17179869184 | bytes 92274688 | tf_op jit(solution)/shard_map/finish/pallas_call | solution.py:94
  (377 shorter events, 379.1 us)
Async XLA Ops:
  7.2 88.5 %all-gather.2.cloned.1.call-start = ((), (), s32[]{:S(2)}) async-start(), calls=%async_computation.12 | async-start | bytes 2359296 | tf_op jit(solution)/shard_map/all_gather | solution.py:407
  27.4 54.8 %all-to-all-start = ((bf16[4,32,64,128]{3,2,1,0:T(8,128)(2,1)}), bf16[4,32,64,128]{3,2,1,0:T(8,128)(2,1)}, u32[]{:S(2)}, u32[]{:S(2)}) async-start(bf16[4,32,64,128]{3,2,1,0:T(8,128)(2,1)} %get-tuple-element.151), calls=%async_computation | async-start | bytes 4194304 | tf_op jit(solution)/shard_map/all_to_all | solution.py:351
  89.1 53.4 %all-to-all-start.1 = ((bf16[4,32,64,128]{3,2,1,0:T(8,128)(2,1)}), bf16[4,32,64,128]{3,2,1,0:T(8,128)(2,1)}, u32[]{:S(2)}, u32[]{:S(2)}) async-start(bf16[4,32,64,128]{3,2,1,0:T(8,128)(2,1)} %after.9), calls=%async_computation.1 | async-start | bytes 4194304 | tf_op jit(solution)/shard_map/all_to_all | solution.py:351
  142.5 53.1 %all-to-all-start.2 = ((bf16[4,32,64,128]{3,2,1,0:T(8,128)(2,1)}), bf16[4,32,64,128]{3,2,1,0:T(8,128)(2,1)}, u32[]{:S(2)}, u32[]{:S(2)}) async-start(bf16[4,32,64,128]{3,2,1,0:T(8,128)(2,1)} %after.10), calls=%async_computation.2 | async-start | bytes 4194304 | tf_op jit(solution)/shard_map/all_to_all | solution.py:351
  173.2 26.9 %collective-permute-start.9 = (s16[32,32,128]{2,1,0:T(8,128)(2,1)S(1)}, s16[32,32,128]{2,1,0:T(8,128)(2,1)S(1)}, u32[]{:S(2)}, u32[]{:S(2)}) collective-permute-start(s16[32,32,128]{2,1,0:T(8,128)(2,1)S(1)} %get-tuple-element.169), channel_id=1, source_target_pairs={{0,3},{1,2},{2,1},{3,0},{4,7},{5,6},{6,5},{7,4},{8,11},{9,10},{10,... | collective-permute-start | bytes 786440 | tf_op jit(solution)/shard_map/ppermute | solution.py:357
  174.6 25.4 %collective-permute-start.10 = (s16[32,32,128]{2,1,0:T(8,128)(2,1)S(1)}, s16[32,32,128]{2,1,0:T(8,128)(2,1)S(1)}, u32[]{:S(2)}, u32[]{:S(2)}) collective-permute-start(s16[32,32,128]{2,1,0:T(8,128)(2,1)S(1)} %get-tuple-element.170), channel_id=1, source_target_pairs={{0,4},{1,5},{2,6},{3,7},{4,0},{5,1},{6,2},{7,3},{8,12},{9,13},{10,... | collective-permute-start | bytes 786440 | tf_op jit(solution)/shard_map/ppermute | solution.py:357
  177.1 30.4 %collective-permute-start.11 = (s16[32,32,128]{2,1,0:T(8,128)(2,1)S(1)}, s16[32,32,128]{2,1,0:T(8,128)(2,1)}, u32[]{:S(2)}, u32[]{:S(2)}) collective-permute-start(s16[32,32,128]{2,1,0:T(8,128)(2,1)S(1)} %get-tuple-element.171), channel_id=1, source_target_pairs={{0,5},{1,4},{2,7},{3,6},{4,1},{5,0},{6,3},{7,2},{8,13},{9,12},{10,... | collective-permute-start | bytes 786440 | tf_op jit(solution)/shard_map/ppermute | solution.py:357
  180.6 26.9 %collective-permute-start.12 = (s16[32,32,128]{2,1,0:T(8,128)(2,1)S(1)}, s16[32,32,128]{2,1,0:T(8,128)(2,1)}, u32[]{:S(2)}, u32[]{:S(2)}) collective-permute-start(s16[32,32,128]{2,1,0:T(8,128)(2,1)S(1)} %get-tuple-element.172), channel_id=1, source_target_pairs={{0,6},{1,7},{2,4},{3,5},{4,2},{5,3},{6,0},{7,1},{8,14},{9,15},{10,... | collective-permute-start | bytes 786440 | tf_op jit(solution)/shard_map/ppermute | solution.py:357
  195.6 62.7 %all-to-all-start.4 = ((bf16[4,32,64,128]{3,2,1,0:T(8,128)(2,1)}), bf16[4,32,64,128]{3,2,1,0:T(8,128)(2,1)}, u32[]{:S(2)}, u32[]{:S(2)}) async-start(bf16[4,32,64,128]{3,2,1,0:T(8,128)(2,1)} %after.12), calls=%async_computation.4 | async-start | bytes 4194304 | tf_op jit(solution)/shard_map/all_to_all | solution.py:351
  224.8 24.7 %collective-permute-start.25 = (bf16[32,32,128]{2,1,0:T(8,128)(2,1)S(1)}, bf16[32,32,128]{2,1,0:T(8,128)(2,1)S(1)}, u32[]{:S(2)}, u32[]{:S(2)}) collective-permute-start(bf16[32,32,128]{2,1,0:T(8,128)(2,1)S(1)} %get-tuple-element.191), channel_id=1, source_target_pairs={{0,5},{1,4},{2,7},{3,6},{4,1},{5,0},{6,3},{7,2},{8,13},{9,12},{10,... | collective-permute-start | bytes 786440 | tf_op jit(solution)/shard_map/ppermute | solution.py:357
  250.6 23.7 %collective-permute-start.32 = (s16[32,32,128]{2,1,0:T(8,128)(2,1)S(1)}, s16[32,32,128]{2,1,0:T(8,128)(2,1)S(1)}, u32[]{:S(2)}, u32[]{:S(2)}) collective-permute-start(s16[32,32,128]{2,1,0:T(8,128)(2,1)S(1)} %get-tuple-element.204), channel_id=1, source_target_pairs={{0,5},{1,4},{2,7},{3,6},{4,1},{5,0},{6,3},{7,2},{8,13},{9,12},{10,... | collective-permute-start | bytes 786440 | tf_op jit(solution)/shard_map/ppermute | solution.py:357
  258.3 75.5 %all-to-all-start.3 = ((bf16[4,64,32,128]{3,2,1,0:T(8,128)(2,1)}), bf16[4,64,32,128]{3,2,1,0:T(8,128)(2,1)}, u32[]{:S(2)}, u32[]{:S(2)}) async-start(bf16[4,64,32,128]{3,2,1,0:T(8,128)(2,1)} %after.11), calls=%async_computation.3 | async-start | bytes 4194304 | tf_op jit(solution)/shard_map/all_to_all | solution.py:351
  318.1 31.2 %collective-permute-start.46 = (s16[32,32,128]{2,1,0:T(8,128)(2,1)S(1)}, s16[32,32,128]{2,1,0:T(8,128)(2,1)S(1)}, u32[]{:S(2)}, u32[]{:S(2)}) collective-permute-start(s16[32,32,128]{2,1,0:T(8,128)(2,1)S(1)} %get-tuple-element.224), channel_id=1, source_target_pairs={{0,5},{1,4},{2,7},{3,6},{4,1},{5,0},{6,3},{7,2},{8,13},{9,12},{10,... | collective-permute-start | bytes 786440 | tf_op jit(solution)/shard_map/ppermute | solution.py:357
  322.4 26.9 %collective-permute-start.47 = (s16[32,32,128]{2,1,0:T(8,128)(2,1)S(1)}, s16[32,32,128]{2,1,0:T(8,128)(2,1)S(1)}, u32[]{:S(2)}, u32[]{:S(2)}) collective-permute-start(s16[32,32,128]{2,1,0:T(8,128)(2,1)S(1)} %get-tuple-element.225), channel_id=1, source_target_pairs={{0,6},{1,7},{2,4},{3,5},{4,2},{5,3},{6,0},{7,1},{8,14},{9,15},{10,... | collective-permute-start | bytes 786440 | tf_op jit(solution)/shard_map/ppermute | solution.py:357
  333.7 52.4 %all-to-all-start.5 = ((bf16[4,64,32,128]{3,2,1,0:T(8,128)(2,1)}), bf16[4,64,32,128]{3,2,1,0:T(8,128)(2,1)}, u32[]{:S(2)}, u32[]{:S(2)}) async-start(bf16[4,64,32,128]{3,2,1,0:T(8,128)(2,1)} %after.13), calls=%async_computation.5 | async-start | bytes 4194304 | tf_op jit(solution)/shard_map/all_to_all | solution.py:351
  386.2 52.2 %all-to-all-start.6 = ((bf16[4,64,32,128]{3,2,1,0:T(8,128)(2,1)}), bf16[4,64,32,128]{3,2,1,0:T(8,128)(2,1)}, u32[]{:S(2)}, u32[]{:S(2)}) async-start(bf16[4,64,32,128]{3,2,1,0:T(8,128)(2,1)} %after.14), calls=%async_computation.6 | async-start | bytes 4194304 | tf_op jit(solution)/shard_map/all_to_all | solution.py:351
  438.4 51.6 %all-to-all-start.7 = ((bf16[4,64,32,128]{3,2,1,0:T(8,128)(2,1)}), bf16[4,64,32,128]{3,2,1,0:T(8,128)(2,1)S(1)}, u32[]{:S(2)}, u32[]{:S(2)}) async-start(bf16[4,64,32,128]{3,2,1,0:T(8,128)(2,1)} %get-tuple-element.241), calls=%async_computation.7 | async-start | bytes 4194304 | tf_op jit(solution)/shard_map/all_to_all | solution.py:351
  491.4 52.5 %all-to-all-start.9 = ((bf16[4,32,64,128]{3,2,1,0:T(8,128)(2,1)}), bf16[4,32,64,128]{3,2,1,0:T(8,128)(2,1)}, u32[]{:S(2)}, u32[]{:S(2)}) async-start(bf16[4,32,64,128]{3,2,1,0:T(8,128)(2,1)} %get-tuple-element.246), calls=%async_computation.9 | async-start | bytes 4194304 | tf_op jit(solution)/shard_map/all_to_all | solution.py:351
  510.5 33.3 %collective-permute-start.57 = (f32[4,128]{1,0:T(4,128)S(1)}, f32[4,128]{1,0:T(4,128)S(1)}, u32[]{:S(2)}, u32[]{:S(2)}) collective-permute-start(f32[4,128]{1,0:T(4,128)S(1)} %broadcast_in_dim.56), channel_id=1, source_target_pairs={{0,16},{8,24},{16,0},{24,8},{1,17},{9,25},{17,1},{25,9},{2,18},{10... | collective-permute-start | bytes 6152 | tf_op jit(solution)/shard_map/ppermute | solution.py:362
  513.4 30.4 %collective-permute-start.58 = (f32[4,128]{1,0:T(4,128)S(1)}, f32[4,128]{1,0:T(4,128)S(1)}, u32[]{:S(2)}, u32[]{:S(2)}) collective-permute-start(f32[4,128]{1,0:T(4,128)S(1)} %broadcast_in_dim.56), channel_id=1, source_target_pairs={{0,24},{8,16},{16,8},{24,0},{1,25},{9,17},{17,9},{25,1},{2,26},{10... | collective-permute-start | bytes 6152 | tf_op jit(solution)/shard_map/ppermute | solution.py:362
  514.8 28.9 %collective-permute-start.56 = (f32[4,128]{1,0:T(4,128)S(1)}, f32[4,128]{1,0:T(4,128)S(1)}, u32[]{:S(2)}, u32[]{:S(2)}) collective-permute-start(f32[4,128]{1,0:T(4,128)S(1)} %broadcast_in_dim.56), channel_id=1, source_target_pairs={{0,8},{8,0},{16,24},{24,16},{1,9},{9,1},{17,25},{25,17},{2,10},{10... | collective-permute-start | bytes 6152 | tf_op jit(solution)/shard_map/ppermute | solution.py:362
  543.8 58.6 %all-to-all-start.8 = ((bf16[4,32,64,128]{3,2,1,0:T(8,128)(2,1)}), bf16[4,32,64,128]{3,2,1,0:T(8,128)(2,1)}, u32[]{:S(2)}, u32[]{:S(2)}) async-start(bf16[4,32,64,128]{3,2,1,0:T(8,128)(2,1)} %after.15), calls=%async_computation.8 | async-start | bytes 4194304 | tf_op jit(solution)/shard_map/all_to_all | solution.py:351
  602.4 54.1 %all-to-all-start.11 = ((bf16[4,32,64,128]{3,2,1,0:T(8,128)(2,1)}), bf16[4,32,64,128]{3,2,1,0:T(8,128)(2,1)S(1)}, u32[]{:S(2)}, u32[]{:S(2)}) async-start(bf16[4,32,64,128]{3,2,1,0:T(8,128)(2,1)} %after.17), calls=%async_computation.11 | async-start | bytes 4194304 | tf_op jit(solution)/shard_map/all_to_all | solution.py:351
  657.9 52.8 %all-to-all-start.10 = ((bf16[4,32,64,128]{3,2,1,0:T(8,128)(2,1)}), bf16[4,32,64,128]{3,2,1,0:T(8,128)(2,1)}, u32[]{:S(2)}, u32[]{:S(2)}) async-start(bf16[4,32,64,128]{3,2,1,0:T(8,128)(2,1)} %after.16), calls=%async_computation.10 | async-start | bytes 4194304 | tf_op jit(solution)/shard_map/all_to_all | solution.py:351
  (135 other events, 1554.7 us)
Sparse Core Ops, SparseCore 0:
  9.9 30.8 all-gather.1

commit v4 on v3

--- a/solution.py
+++ b/solution.py
@@ -141,9 +141,9 @@
                 total = dot_rows(table_ref[0], part[0]) + dot_rows(table_ref[1], part[1])
                 for k in range(4):
                     turned[pl.ds(start + k, hours, stride=GROUP), :] = total[:, k * ol : (k + 1) * ol]
-            value = turned[...].reshape(HALVES, zs, hp, GROUP, ol).astype(BF16)
+            value = turned[...].reshape(zs, HALVES, hp, GROUP, ol).astype(BF16)
             for c in range(HALVES):
-                outs[c][...] = value[c]
+                outs[c][...] = value[:, c]
 
         return self.call(
             body, "hourly", al // GROUP, [struct((zs, hp, al, ol), BF16)] * HALVES,
@@ -153,9 +153,10 @@
             [pltpu.VMEM((hours * GROUP, ol), F32)],
         )(noise, tables)
 
-    def lat_up(self, g, lat, gain):
+    def lat_up(self, c, g, lat, gain):
         zs, qs, hp, lr, ol, lats = self.zs, self.qs, self.hp, self.lr, self.ol, self.lats
         group = 8
+        offset = c * (hp // group) if g.shape[1] == self.hl else 0
 
         def body(gain_ref, g_ref, lat_ref, *outs):
             for start in range(0, group, 4):
@@ -168,7 +169,7 @@
 
         return self.call(
             body, "lat_up", hp // group, self.parts_shape(I16),
-            [SCALARS, pl.BlockSpec((zs, group, self.al, ol), lambda i: (0, i, 0, 0)), whole_spec(lat.shape)],
+            [SCALARS, pl.BlockSpec((zs, group, self.al, ol), lambda i: (0, i + offset, 0, 0)), whole_spec(lat.shape)],
             self.parts_specs(group), 2 * self.cells * self.lats, 4 * self.cells,
         )(gain.reshape(1), g, lat)
 
@@ -204,11 +205,13 @@
         )(back.reshape(1), *codes, lon_up, lon_down, observed, mask)
         return out[0], out[1], out[2:]
 
-    def lat_down(self, v, lat_t):
+    def lat_down(self, c, v, lat_t, earlier):
         zs, qs, hp, al, lr, ol, lats = self.zs, self.qs, self.hp, self.al, self.lr, self.ol, self.lats
 
+        offset = c * (hp // GROUP)
+
         def body(*refs):
-            sent, (lat_ref, out_ref, turned) = refs[:qs], refs[qs:]
+            sent, lat_ref, (out_ref, turned) = refs[:qs], refs[qs], refs[-2:]
             for start in range(0, GROUP, 4):
                 part = [jnp.concatenate([s[start + k] for s in sent], axis=0) for k in range(4)]
                 total = dot(lat_ref[...], jnp.concatenate(part, axis=1))
@@ -217,45 +220,43 @@
             out_ref[...] = turned[...].reshape(zs, al, GROUP, ol).astype(BF16)
 
         return self.call(
-            body, "lat_down", hp // GROUP, [struct((zs, al, hp, ol), BF16)],
-            self.parts_specs(GROUP) + [whole_spec(lat_t.shape)],
-            [pl.BlockSpec((zs, al, GROUP, ol), lambda i: (0, 0, i, 0))],
+            body, "lat_down", hp // GROUP, [struct((zs, al, self.hl, ol), BF16)],
+            self.parts_specs(GROUP) + [whole_spec(lat_t.shape)] + [ANYWHERE] * len(earlier),
+            [pl.BlockSpec((zs, al, GROUP, ol), lambda i: (0, 0, i + offset, 0))],
             2 * self.cells * lats, 4 * self.cells,
-            [pltpu.VMEM((lats * GROUP, ol), F32)],
-        )(*v, lat_t)[0]
-
-    def over_hours(self, halves, kern):
-        zs, hp, al, ol, hours = self.zs, self.hp, self.al, self.ol, self.hours
-
-        def body(*refs):
-            sent, kern_ref, outs = refs[:HALVES], refs[HALVES], refs[HALVES + 1 : 2 * HALVES + 1]
-            bend_ref, turned = refs[2 * HALVES + 1 :]
+            [pltpu.VMEM((lats * GROUP, ol), F32)], {qs + 1: 0} if earlier else {},
+        )(*v, lat_t, *earlier)
+
+    def over_hours(self, x, kern, pieces):
+        zs, hl, al, ol, hours = self.zs, self.hl, self.al, self.ol, self.hours
+        hp = hl // pieces
+
+        def body(x_ref, kern_ref, *refs):
+            outs, (bend_ref, turned) = refs[:pieces], refs[pieces:]
 
             @pl.when(pl.program_id(0) == 0)
             def _():
                 bend_ref[...] = jnp.zeros_like(bend_ref)
 
             for start in range(0, GROUP, 4):
-                part = [
-                    jnp.concatenate([x[:, start + k].reshape(zs * hp, ol) for x in sent], axis=0) for k in range(4)
-                ]
+                part = [x_ref[:, start + k].reshape(hours, ol) for k in range(4)]
                 part = jnp.concatenate(part, axis=1)
                 total = dot(kern_ref[0], part) + dot(kern_ref[1], part)
                 bend_ref[...] += fold(total * part.astype(F32))
                 for k in range(4):
                     turned[pl.ds(start + k, hours, stride=GROUP), :] = total[:, k * ol : (k + 1) * ol]
-            value = turned[...].reshape(HALVES, zs, hp, GROUP, ol).astype(BF16)
-            for c in range(HALVES):
-                outs[c][...] = value[c]
+            value = turned[...].reshape(zs, pieces, hp, GROUP, ol).astype(BF16)
+            for c in range(pieces):
+                outs[c][...] = value[:, c]
 
         out = self.call(
-            body, "over_hours", al // GROUP, [struct((zs, hp, al, ol), BF16)] * HALVES + [struct((8, 128), F32)],
-            [pl.BlockSpec((zs, GROUP, hp, ol), lambda i: (0, i, 0, 0))] * HALVES + [whole_spec(kern.shape)],
-            [pl.BlockSpec((zs, hp, GROUP, ol), lambda i: (0, 0, i, 0))] * HALVES + [whole_spec((8, 128))],
+            body, "over_hours", al // GROUP, [struct((zs, hp, al, ol), BF16)] * pieces + [struct((8, 128), F32)],
+            [pl.BlockSpec((zs, GROUP, hl, ol), lambda i: (0, i, 0, 0)), whole_spec(kern.shape)],
+            [pl.BlockSpec((zs, hp, GROUP, ol), lambda i: (0, 0, i, 0))] * pieces + [whole_spec((8, 128))],
             8 * self.cells * hours, 8 * self.cells,
             [pltpu.VMEM((hours * GROUP, ol), F32)],
-        )(*halves, kern)
-        return out[:HALVES], out[-1]
+        )(x, kern)
+        return out[:pieces], out[-1]
 
     def finish(self, s, c, codes, back, step, lon_up, prior, observed, mask, earlier):
         qs, hp, lr, ol, lons = self.qs, self.hp, self.lr, self.ol, self.lons
@@ -296,10 +297,12 @@
 
     def hourly(self, noise, tables):
         h = jnp.einsum("cyxk,cjk->jyx", noise, tables, preferred_element_type=F32).astype(BF16)
-        h = h.reshape(HALVES, self.zs, self.hp, self.al, self.ol)
-        return [h[c] for c in range(HALVES)]
-
-    def lat_up(self, g, lat, gain):
+        h = h.reshape(self.zs, HALVES, self.hp, self.al, self.ol)
+        return [h[:, c] for c in range(HALVES)]
+
+    def lat_up(self, c, g, lat, gain):
+        if g.shape[1] == self.hl:
+            g = g[:, c * self.hp : (c + 1) * self.hp]
         split = lat.reshape(self.qs, self.lr, self.zs, self.al)
         x = encode(jnp.einsum("qlzy,zhyx->qhlx", split, g, preferred_element_type=F32) * gain)
         return [x[d] for d in range(self.qs)]
@@ -317,18 +320,17 @@
         v = jnp.einsum("hlo,op->hlp", resid, lon_down.astype(F32), precision=HIGH).astype(BF16)
         return prior, jnp.sum(resid * resid), jnp.split(v, self.qs, axis=2)
 
-    def lat_down(self, v, lat_t):
+    def lat_down(self, c, v, lat_t, earlier):
         split = lat_t.reshape(self.zs, self.al, self.qs, self.lr)
         x = jnp.einsum("zyql,qhlx->zyhx", split, jnp.stack(v), preferred_element_type=F32)
-        return x.astype(BF16)
-
-    def over_hours(self, halves, kern):
-        x = jnp.concatenate([jnp.swapaxes(h, 0, 1).reshape(self.al, -1, self.ol) for h in halves], axis=1)
-        x = x.astype(F32)
+        return (jnp.concatenate(list(earlier) + [x.astype(BF16)], axis=2),)
+
+    def over_hours(self, x, kern, pieces):
+        x = jnp.swapaxes(x, 0, 1).reshape(self.al, self.hours, self.ol).astype(F32)
         y = jnp.einsum("gk,ykx->gyx", kern.astype(F32).sum(0), x, precision=HIGH)
         bend = jnp.einsum("gyx,ygx->", y, x)
-        y = y.astype(BF16).reshape(HALVES, self.zs, self.hp, self.al, self.ol)
-        return [y[c] for c in range(HALVES)], bend
+        y = y.astype(BF16).reshape(self.zs, pieces, self.hl // pieces, self.al, self.ol)
+        return [y[:, c] for c in range(pieces)], bend
 
     def finish(self, s, c, codes, back, step, lon_up, prior, observed, mask, earlier):
         scaled = self.up(codes, lon_up) * (back * step)
@@ -388,8 +390,7 @@
 
     powers = jnp.concatenate([spectrum, spectrum[1:-1][::-1]])
     amplitude = jnp.sqrt(powers / periods)
-    clock = jnp.arange(HALVES)[:, None, None] * hour_part + jnp.arange(zs)[None, :, None] * hour_local
-    clock = (clock + jnp.arange(hour_part)).reshape(hours, 1)
+    clock = jnp.arange(hours)[:, None]
     phase = (clock * jnp.arange(periods) % periods).astype(F32) * (2.0 * jnp.pi / periods)
     cosine_tab, sine_tab = jnp.cos(phase), jnp.sin(phase)
     table_cos = (cosine_tab * amplitude).astype(BF16)
@@ -427,7 +428,7 @@
     codes, priors, norms, sent, down = {}, {}, {}, {}, {}
 
     def up(u):
-        codes[u] = swap_lon(stages.lat_up(arrived[u], lat, first_gain))
+        codes[u] = swap_lon(stages.lat_up(u[1], arrived[u], lat, first_gain))
 
     def middle(u):
         priors[u], norms[u], v = stages.residual(
@@ -436,7 +437,8 @@
         sent[u] = swap_lon(v)
 
     def lower(u):
-        down[u] = stages.lat_down(sent[u], lat_t)
+        s, c = u
+        down[s] = stages.lat_down(c, sent[u], lat_t, down.get(s, ()))
 
     up(first)
     middle(first)
@@ -447,27 +449,25 @@
     middle(second)
     up(third)
     lower(second)
-    down[first] = swap_tm(wait(down[first]))
+    down[0] = swap_tm(wait(down[0][0]))
+    up(fourth)
     middle(third)
-    up(fourth)
     lower(third)
-    down[second] = swap_tm(wait(down[second]))
     middle(fourth)
-    down[third] = swap_tm(wait(down[third]))
     lower(fourth)
-    down[fourth] = swap_tm(down[fourth])
+    down[1] = swap_tm(down[1][0])
 
     sums = []
     for s in range(2):
-        mine = [u for u in units if u[0] == s]
-        sums.append(sum(jnp.sum(norms[u]) for u in mine))
-        halves, bending = stages.over_hours([down[u] for u in mine], kern)
+        sums.append(sum(jnp.sum(norms[u]) for u in units if u[0] == s))
+        pieces, bending = stages.over_hours(down[s], kern, 1 if s == 0 else HALVES)
         sums.append(jnp.sum(bending))
-        for u in mine:
-            waves[u] = halves[u[1]]
-    arrived[first] = swap_tm(waves[first])
+        if s == 0:
+            arrived[first] = arrived[second] = swap_tm(pieces[0])
+        else:
+            waves[third], waves[fourth] = pieces
     sums = add_over_tm(jnp.broadcast_to(jnp.stack(sums)[:, None], (4, 128)), zs)
-    arrived[second] = swap_tm(wait(waves[second], sums))
+    arrived[third] = swap_tm(wait(waves[third], sums))
     sums = add_over_lon(sums, qs)[:, 0]
     gains, steps = [], []
     for s in range(2):
@@ -476,13 +476,26 @@
         gains.append(CODE_MAX / jnp.maximum(bound, 1e-30))
         steps.append(norm_sq / (bending + NOISE_VAR * norm_sq))
     earlier = ()
-    for u in units:
+
+    def back(u):
         s, c = u
-        codes = swap_lon(stages.lat_up(arrived[u], lat, gains[s]))
-        later = {first: third, second: fourth}.get(u)
-        earlier = stages.finish(s, c, codes, 1.0 / gains[s], steps[s], lon_up, priors[u], observed, mask, earlier)
-        if later is not None:
-            arrived[later] = swap_tm(wait(waves[later]))
+        codes[u] = swap_lon(stages.lat_up(c, arrived[u], lat, gains[s]))
+
+    def end(u):
+        s, c = u
+        return stages.finish(
+            s, c, codes[u], 1.0 / gains[s], steps[s], lon_up, priors[u], observed, mask, earlier
+        )
+
+    back(first)
+    back(second)
+    earlier = end(first)
+    arrived[fourth] = swap_tm(wait(waves[fourth]))
+    back(third)
+    earlier = end(second)
+    earlier = end(third)
+    back(fourth)
+    earlier = end(fourth)
     return stages.joined(earlier)
 
 

time: 772 us -> 774 us (level)
  waiting for transfers between devices: 330 us -> 359 us
  starting transfers between devices: 148 us -> 126 us
    ppermute x3, waiting for transfers between devices: 28.9 us -> 73.5 us  [add_over_tm(): lax.ppermute(x, 'tm', [(i, i ^ d) for i in range(count)])]
    ppermute x84, waiting for transfers between devices: 180 us -> 151 us  [swap_lon(): lax.ppermute(parts[d], 'lon', [(i, i ^ d) for i in range(count)])]
    all_to_all x12 -> x9, waiting for transfers between devices: 118 us -> 131 us  [swap_tm(): return lax.all_to_all(x, 'tm', split_axis=0, concat_axis=0, tiled=True)]
    all_to_all x12 -> x9, starting transfers between devices: 58.1 us -> 45.9 us  [swap_tm(): return lax.all_to_all(x, 'tm', split_axis=0, concat_axis=0, tiled=True)]
    ppermute x84, starting transfers between devices: 82.4 us -> 73.2 us  [swap_lon(): lax.ppermute(parts[d], 'lon', [(i, i ^ d) for i in range(count)])]
    unnamed x115 -> x117, local copies, waits for them, and re-layouts: 23.1 us -> 21.6 us
  transfers between devices with their start and end apart: 103 -> 100, of which waited for: 47 -> 38; matrix products, arithmetic and copies ran while one was open for 5% -> 5% of each run, Pallas kernels for 23% -> 23%
where the time goes in v4:
time: 774 us; the launch traced here: 764 us
  waiting for transfers between devices  359 us (46%)
  Pallas kernels  196 us (25%)
  starting transfers between devices  126 us (16%)
  local copies, waits for them, and re-layouts  38.2 us (5%)
  between operations  24.6 us (3%)
  other arithmetic  15.4 us (2%)
    pallas_call x24, Pallas kernels, run(): pl.pallas_call(whole, name=name, grid=(grid,), out_shape=list(out_shape)...  196 us
    ppermute x84, waiting for transfers between devices, swap_lon(): lax.ppermute(parts[d], 'lon', [(i, i ^ d) for i in range(count)])  151 us
    all_to_all x9, waiting for transfers between devices, swap_tm(): return lax.all_to_all(x, 'tm', split_axis=0, concat_axis=0, tiled=True)  131 us
    ppermute x3, waiting for transfers between devices, add_over_tm(): lax.ppermute(x, 'tm', [(i, i ^ d) for i in range(count)])  73.5 us
    ppermute x84, starting transfers between devices, swap_lon(): lax.ppermute(parts[d], 'lon', [(i, i ^ d) for i in range(count)])  73.2 us
    all_to_all x9, starting transfers between devices, swap_tm(): return lax.all_to_all(x, 'tm', split_axis=0, concat_axis=0, tiled=True)  45.9 us
    unnamed x117, local copies, waits for them, and re-layouts  21.6 us
  transfers between devices with their start and end apart: 100, of which 38 were waited for; matrix products, arithmetic and copies ran while one was open for 5% of the time, Pallas kernels for 23%

profile of v4, /device:TPU:0, one launch (start us, length us, event | category | flops | bytes accessed | tf_op | source)
XLA Modules:
  0.0 764.0 jit_solution(5901977093726388091)
XLA Ops:
  15.7 11.1 %hourly.2 = (bf16[4,32,64,128]{3,2,1,0:T(8,128)(2,1)}, bf16[4,32,64,128]{3,2,1,0:T(8,128)(2,1)}, f32[8,128]{1,0:T(8,128)S(1)}) custom-call(bf16[2,64,128,512]{3,2,1,0:T(8,128)(2,1)} %refs_0_.3, bf16[2,256,512]{2,1,0:T(8,128)(2,1)S(1)} %get-tuple-element.304.refs_1_), custom_call_target="tpu_custom_call" | custom-call | flops 17179869184 | bytes 83886080 | tf_op jit(solution)/shard_map/hourly/pallas_call | solution.py:94
  26.8 6.5 all-to-all-start
  36.1 11.2 %hourly.3 = (bf16[4,32,64,128]{3,2,1,0:T(8,128)(2,1)}, bf16[4,32,64,128]{3,2,1,0:T(8,128)(2,1)}, f32[8,128]{1,0:T(8,128)S(1)}) custom-call(bf16[2,64,128,512]{3,2,1,0:T(8,128)(2,1)} %refs_0_.3, bf16[2,256,512]{2,1,0:T(8,128)(2,1)S(1)} %get-tuple-element.305.refs_1_, f32[8,128]{1,0:T(8,128)S(1)} %get-tuple-element.151.refs_2_), custom_call_target="tpu_custom_call" | custom-call | flops 17179869184 | bytes 83886080 | tf_op jit(solution)/shard_map/hourly/pallas_call | solution.py:94
  47.3 34.3 %all-to-all-done.refs_1_ = bf16[4,32,64,128]{3,2,1,0:T(8,128)(2,1)} async-done(((bf16[4,32,64,128]{3,2,1,0:T(8,128)(2,1)}), bf16[4,32,64,128]{3,2,1,0:T(8,128)(2,1)}, u32[]{:S(2)}, u32[]{:S(2)}) %all-to-all-start) | async-done | bytes 2097184 | tf_op jit(solution)/shard_map/all_to_all | solution.py:353
  121.5 14.7 %residual.4 = (f32[32,32,1024]{2,1,0:T(8,128)}, f32[8,128]{1,0:T(8,128)S(1)}, bf16[32,32,128]{2,1,0:T(8,128)(2,1)S(1)}, bf16[32,32,128]{2,1,0:T(8,128)(2,1)}, bf...) custom-call(f32[1]{0:T(128)} %bitcast.3.refs_0_, ...), custom_call_target="tpu_custom_call" | custom-call | flops 34359738368 | bytes 67108864 | tf_op jit(solution)/shard_map/residual/pallas_call | solution.py:94
  199.1 7.4 collective-permute-done.11.refs_6_
  206.6 14.8 %residual.5 = (f32[32,32,1024]{2,1,0:T(8,128)}, f32[8,128]{1,0:T(8,128)S(1)}, bf16[32,32,128]{2,1,0:T(8,128)(2,1)S(1)}, bf16[32,32,128]{2,1,0:T(8,128)(2,1)S(1)}...) custom-call(f32[1]{0:T(128)} %bitcast.3.refs_0_, ...), custom_call_target="tpu_custom_call" | custom-call | flops 34359738368 | bytes 67108864 | tf_op jit(solution)/shard_map/residual/pallas_call | solution.py:94
  237.0 11.3 %collective-permute-done.25.refs_5_ = bf16[32,32,128]{2,1,0:T(8,128)(2,1)S(1)} collective-permute-done((bf16[32,32,128]{2,1,0:T(8,128)(2,1)S(1)}, bf16[32,32,128]{2,1,0:T(8,128)(2,1)S(1)}, u32[]{:S(2)}, u32[]{:S(2)}) %collective-permute-start.25) | collective-permute-done | bytes 262176 | tf_op jit(solution)/shard_map/ppermute | solution.py:359
  274.0 14.8 %residual.6 = (f32[32,32,1024]{2,1,0:T(8,128)}, f32[8,128]{1,0:T(8,128)S(1)}, bf16[32,32,128]{2,1,0:T(8,128)(2,1)S(1)}, bf16[32,32,128]{2,1,0:T(8,128)(2,1)S(1)}...) custom-call(f32[1]{0:T(128)} %bitcast.3.refs_0_, ...), custom_call_target="tpu_custom_call" | custom-call | flops 34359738368 | bytes 67108864 | tf_op jit(solution)/shard_map/residual/pallas_call | solution.py:94
  306.7 10.4 %collective-permute-done.46.refs_5_ = bf16[32,32,128]{2,1,0:T(8,128)(2,1)S(1)} collective-permute-done((bf16[32,32,128]{2,1,0:T(8,128)(2,1)S(1)}, bf16[32,32,128]{2,1,0:T(8,128)(2,1)S(1)}, u32[]{:S(2)}, u32[]{:S(2)}) %collective-permute-start.46) | collective-permute-done | bytes 262176 | tf_op jit(solution)/shard_map/ppermute | solution.py:359
  324.7 9.7 %collective-permute-done.31.refs_5_ = s16[32,32,128]{2,1,0:T(8,128)(2,1)S(1)} collective-permute-done((s16[32,32,128]{2,1,0:T(8,128)(2,1)S(1)}, s16[32,32,128]{2,1,0:T(8,128)(2,1)S(1)}, u32[]{:S(2)}, u32[]{:S(2)}) %collective-permute-start.31) | collective-permute-done | bytes 262176 | tf_op jit(solution)/shard_map/ppermute | solution.py:359
  340.4 14.8 %residual.7 = (f32[32,32,1024]{2,1,0:T(8,128)}, f32[8,128]{1,0:T(8,128)S(1)}, bf16[32,32,128]{2,1,0:T(8,128)(2,1)S(1)}, bf16[32,32,128]{2,1,0:T(8,128)(2,1)S(1)}...) custom-call(f32[1]{0:T(128)} %bitcast.3.refs_0_, ...), custom_call_target="tpu_custom_call" | custom-call | flops 34359738368 | bytes 67108864 | tf_op jit(solution)/shard_map/residual/pallas_call | solution.py:94
  369.5 13.1 %collective-permute-done.53.refs_5_ = bf16[32,32,128]{2,1,0:T(8,128)(2,1)S(1)} collective-permute-done((bf16[32,32,128]{2,1,0:T(8,128)(2,1)S(1)}, bf16[32,32,128]{2,1,0:T(8,128)(2,1)S(1)}, u32[]{:S(2)}, u32[]{:S(2)}) %collective-permute-start.53) | collective-permute-done | bytes 262176 | tf_op jit(solution)/shard_map/ppermute | solution.py:359
  398.0 7.1 over_hours.2
  405.1 81.2 %all-to-all-done.5.refs_0_ = bf16[4,64,64,128]{3,2,1,0:T(8,128)(2,1)} async-done(((bf16[4,64,64,128]{3,2,1,0:T(8,128)(2,1)}), bf16[4,64,64,128]{3,2,1,0:T(8,128)(2,1)}, u32[]{:S(2)}, u32[]{:S(2)}) %all-to-all-start.5) | async-done | bytes 4194336 | tf_op jit(solution)/shard_map/all_to_all | solution.py:353
  496.8 7.2 over_hours.3
  510.4 73.5 %collective-permute-done.57 = f32[4,128]{1,0:T(4,128)S(1)} collective-permute-done((f32[4,128]{1,0:T(4,128)S(1)}, f32[4,128]{1,0:T(4,128)S(1)}, u32[]{:S(2)}, u32[]{:S(2)}) %collective-permute-start.57) | collective-permute-done | bytes 2080 | tf_op jit(solution)/shard_map/ppermute | solution.py:364
  620.6 12.7 %collective-permute-done.66.refs_6_ = s16[32,32,128]{2,1,0:T(8,128)(2,1)S(1)} collective-permute-done((s16[32,32,128]{2,1,0:T(8,128)(2,1)S(1)}, s16[32,32,128]{2,1,0:T(8,128)(2,1)S(1)}, u32[]{:S(2)}, u32[]{:S(2)}) %collective-permute-start.66) | collective-permute-done | bytes 262176 | tf_op jit(solution)/shard_map/ppermute | solution.py:359
  636.4 11.9 %finish.4 = (f32[2,64,32,1024]{3,2,1,0:T(8,128)}, f32[2,64,32,1024]{3,2,1,0:T(8,128)}, f32[8,128]{1,0:T(8,128)S(1)}) custom-call(f32[2]{0:T(128)S(1)} %pad_maximum_fusion.5.refs_0_, s16[32,32,128]{2,1,0:T(8,128)(2,1)S(1)} %copy-done.11, s16[32,32,128]{2,1,0:T(8,128)(2,1)S(1)} %collective-permute-done.62.refs_2_, ...), custom_call_target="tpu_custom_call" | custom-call | flops 17179869184 | bytes 92274688 | tf_op jit(solution)/shard_map/finish/pallas_call | solution.py:94
  676.3 12.1 %finish.5 = (f32[2,64,32,1024]{3,2,1,0:T(8,128)}, f32[2,64,32,1024]{3,2,1,0:T(8,128)}, f32[8,128]{1,0:T(8,128)S(1)}) custom-call(f32[2]{0:T(128)S(1)} %pad_maximum_fusion.5.refs_0_, s16[32,32,128]{2,1,0:T(8,128)(2,1)S(1)} %copy-done.9, s16[32,32,128]{2,1,0:T(8,128)(2,1)S(1)} %collective-permute-done.76.refs_2_, ...), custom_call_target="tpu_custom_call", output_to_operand_aliasing={{0}: (13, {}), {1}: (14, {})} | custom-call | flops 17179869184 | bytes 92274688 | tf_op jit(solution)/shard_map/finish/pallas_call | solution.py:94
  692.6 12.0 %finish.6 = (f32[2,64,32,1024]{3,2,1,0:T(8,128)}, f32[2,64,32,1024]{3,2,1,0:T(8,128)}, f32[8,128]{1,0:T(8,128)S(1)}) custom-call(f32[2]{0:T(128)S(1)} %pad_maximum_fusion.4.refs_0_, s16[32,32,128]{2,1,0:T(8,128)(2,1)S(1)} %copy-done.13, s16[32,32,128]{2,1,0:T(8,128)(2,1)S(1)} %collective-permute-done.69.refs_2_, ...), custom_call_target="tpu_custom_call", output_to_operand_aliasing={{0}: (13, {}), {1}: (14, {})} | custom-call | flops 17179869184 | bytes 92274688 | tf_op jit(solution)/shard_map/finish/pallas_call | solution.py:94
  704.6 8.5 %all-to-all-done.7.refs_1_ = bf16[4,32,64,128]{3,2,1,0:T(8,128)(2,1)} async-done(((bf16[4,32,64,128]{3,2,1,0:T(8,128)(2,1)}), bf16[4,32,64,128]{3,2,1,0:T(8,128)(2,1)}, u32[]{:S(2)}, u32[]{:S(2)}) %all-to-all-start.7) | async-done | bytes 2097184 | tf_op jit(solution)/shard_map/all_to_all | solution.py:353
  731.8 12.6 %collective-permute-done.87.refs_6_ = s16[32,32,128]{2,1,0:T(8,128)(2,1)S(1)} collective-permute-done((s16[32,32,128]{2,1,0:T(8,128)(2,1)S(1)}, s16[32,32,128]{2,1,0:T(8,128)(2,1)S(1)}, u32[]{:S(2)}, u32[]{:S(2)}) %collective-permute-start.87) | collective-permute-done | bytes 262176 | tf_op jit(solution)/shard_map/ppermute | solution.py:359
  745.1 11.8 %finish.7 = (f32[2,64,32,1024]{3,2,1,0:T(8,128)}, f32[2,64,32,1024]{3,2,1,0:T(8,128)}, f32[8,128]{1,0:T(8,128)}) custom-call(f32[2]{0:T(128)S(1)} %pad_maximum_fusion.4.refs_0_, s16[32,32,128]{2,1,0:T(8,128)(2,1)S(1)} %get-tuple-element.284.refs_1_, ...), custom_call_target="tpu_custom_call", output_to_operand_aliasing={{0}: (13, {}), {1}: (14, {})} | custom-call | flops 17179869184 | bytes 92274688 | tf_op jit(solution)/shard_map/finish/pallas_call | solution.py:94
  (365 shorter events, 314.5 us)
Async XLA Ops:
  7.2 87.8 %all-gather.2.cloned.1.call-start = ((), (), s32[]{:S(2)}) async-start(), calls=%async_computation.9 | async-start | bytes 2359296 | tf_op jit(solution)/shard_map/all_gather | solution.py:408
  26.8 54.7 %all-to-all-start = ((bf16[4,32,64,128]{3,2,1,0:T(8,128)(2,1)}), bf16[4,32,64,128]{3,2,1,0:T(8,128)(2,1)}, u32[]{:S(2)}, u32[]{:S(2)}) async-start(bf16[4,32,64,128]{3,2,1,0:T(8,128)(2,1)} %get-tuple-element.150), calls=%async_computation | async-start | bytes 4194304 | tf_op jit(solution)/shard_map/all_to_all | solution.py:353
  88.4 53.4 %all-to-all-start.1 = ((bf16[4,32,64,128]{3,2,1,0:T(8,128)(2,1)}), bf16[4,32,64,128]{3,2,1,0:T(8,128)(2,1)}, u32[]{:S(2)}, u32[]{:S(2)}) async-start(bf16[4,32,64,128]{3,2,1,0:T(8,128)(2,1)} %after.6), calls=%async_computation.1 | async-start | bytes 4194304 | tf_op jit(solution)/shard_map/all_to_all | solution.py:353
  141.8 52.8 %all-to-all-start.2 = ((bf16[4,32,64,128]{3,2,1,0:T(8,128)(2,1)}), bf16[4,32,64,128]{3,2,1,0:T(8,128)(2,1)}, u32[]{:S(2)}, u32[]{:S(2)}) async-start(bf16[4,32,64,128]{3,2,1,0:T(8,128)(2,1)} %after.7), calls=%async_computation.2 | async-start | bytes 4194304 | tf_op jit(solution)/shard_map/all_to_all | solution.py:353
  172.2 26.9 %collective-permute-start.9 = (s16[32,32,128]{2,1,0:T(8,128)(2,1)S(1)}, s16[32,32,128]{2,1,0:T(8,128)(2,1)S(1)}, u32[]{:S(2)}, u32[]{:S(2)}) collective-permute-start(s16[32,32,128]{2,1,0:T(8,128)(2,1)S(1)} %get-tuple-element.168), channel_id=1, source_target_pairs={{0,3},{1,2},{2,1},{3,0},{4,7},{5,6},{6,5},{7,4},{8,11},{9,10},{10,... | collective-permute-start | bytes 786440 | tf_op jit(solution)/shard_map/ppermute | solution.py:359
  173.6 25.5 %collective-permute-start.10 = (s16[32,32,128]{2,1,0:T(8,128)(2,1)S(1)}, s16[32,32,128]{2,1,0:T(8,128)(2,1)S(1)}, u32[]{:S(2)}, u32[]{:S(2)}) collective-permute-start(s16[32,32,128]{2,1,0:T(8,128)(2,1)S(1)} %get-tuple-element.169), channel_id=1, source_target_pairs={{0,4},{1,5},{2,6},{3,7},{4,0},{5,1},{6,2},{7,3},{8,12},{9,13},{10,... | collective-permute-start | bytes 786440 | tf_op jit(solution)/shard_map/ppermute | solution.py:359
  176.2 30.4 %collective-permute-start.11 = (s16[32,32,128]{2,1,0:T(8,128)(2,1)S(1)}, s16[32,32,128]{2,1,0:T(8,128)(2,1)}, u32[]{:S(2)}, u32[]{:S(2)}) collective-permute-start(s16[32,32,128]{2,1,0:T(8,128)(2,1)S(1)} %get-tuple-element.170), channel_id=1, source_target_pairs={{0,5},{1,4},{2,7},{3,6},{4,1},{5,0},{6,3},{7,2},{8,13},{9,12},{10,... | collective-permute-start | bytes 786440 | tf_op jit(solution)/shard_map/ppermute | solution.py:359
  179.6 26.9 %collective-permute-start.12 = (s16[32,32,128]{2,1,0:T(8,128)(2,1)S(1)}, s16[32,32,128]{2,1,0:T(8,128)(2,1)}, u32[]{:S(2)}, u32[]{:S(2)}) collective-permute-start(s16[32,32,128]{2,1,0:T(8,128)(2,1)S(1)} %get-tuple-element.171), channel_id=1, source_target_pairs={{0,6},{1,7},{2,4},{3,5},{4,2},{5,3},{6,0},{7,1},{8,14},{9,15},{10,... | collective-permute-start | bytes 786440 | tf_op jit(solution)/shard_map/ppermute | solution.py:359
  194.6 62.6 %all-to-all-start.4 = ((bf16[4,32,64,128]{3,2,1,0:T(8,128)(2,1)}), bf16[4,32,64,128]{3,2,1,0:T(8,128)(2,1)}, u32[]{:S(2)}, u32[]{:S(2)}) async-start(bf16[4,32,64,128]{3,2,1,0:T(8,128)(2,1)} %after.9), calls=%async_computation.4 | async-start | bytes 4194304 | tf_op jit(solution)/shard_map/all_to_all | solution.py:353
  257.2 129.8 %all-to-all-start.3 = ((bf16[4,64,64,128]{3,2,1,0:T(8,128)(2,1)}), bf16[4,64,64,128]{3,2,1,0:T(8,128)(2,1)}, u32[]{:S(2)}, u32[]{:S(2)}) async-start(bf16[4,64,64,128]{3,2,1,0:T(8,128)(2,1)} %after.8), calls=%async_computation.3 | async-start | bytes 8388608 | tf_op jit(solution)/shard_map/all_to_all | solution.py:353
  292.1 24.9 %collective-permute-start.46 = (bf16[32,32,128]{2,1,0:T(8,128)(2,1)S(1)}, bf16[32,32,128]{2,1,0:T(8,128)(2,1)S(1)}, u32[]{:S(2)}, u32[]{:S(2)}) collective-permute-start(bf16[32,32,128]{2,1,0:T(8,128)(2,1)S(1)} %get-tuple-element.221), channel_id=1, source_target_pairs={{0,5},{1,4},{2,7},{3,6},{4,1},{5,0},{6,3},{7,2},{8,13},{9,12},{10,... | collective-permute-start | bytes 786440 | tf_op jit(solution)/shard_map/ppermute | solution.py:359
  306.2 28.3 %collective-permute-start.31 = (s16[32,32,128]{2,1,0:T(8,128)(2,1)S(1)}, s16[32,32,128]{2,1,0:T(8,128)(2,1)S(1)}, u32[]{:S(2)}, u32[]{:S(2)}) collective-permute-start(s16[32,32,128]{2,1,0:T(8,128)(2,1)S(1)} %get-tuple-element.203), channel_id=1, source_target_pairs={{0,4},{1,5},{2,6},{3,7},{4,0},{5,1},{6,2},{7,3},{8,12},{9,13},{10,... | collective-permute-start | bytes 786440 | tf_op jit(solution)/shard_map/ppermute | solution.py:359
  357.7 24.9 %collective-permute-start.53 = (bf16[32,32,128]{2,1,0:T(8,128)(2,1)S(1)}, bf16[32,32,128]{2,1,0:T(8,128)(2,1)S(1)}, u32[]{:S(2)}, u32[]{:S(2)}) collective-permute-start(bf16[32,32,128]{2,1,0:T(8,128)(2,1)S(1)} %get-tuple-element.231), channel_id=1, source_target_pairs={{0,5},{1,4},{2,7},{3,6},{4,1},{5,0},{6,3},{7,2},{8,13},{9,12},{10,... | collective-permute-start | bytes 786440 | tf_op jit(solution)/shard_map/ppermute | solution.py:359
  387.0 99.3 %all-to-all-start.5 = ((bf16[4,64,64,128]{3,2,1,0:T(8,128)(2,1)}), bf16[4,64,64,128]{3,2,1,0:T(8,128)(2,1)}, u32[]{:S(2)}, u32[]{:S(2)}) async-start(bf16[4,64,64,128]{3,2,1,0:T(8,128)(2,1)} %get-tuple-element.240), calls=%async_computation.5 | async-start | bytes 8388608 | tf_op jit(solution)/shard_map/all_to_all | solution.py:353
  486.3 97.7 %all-to-all-start.6 = ((bf16[4,64,64,128]{3,2,1,0:T(8,128)(2,1)}), bf16[4,64,64,128]{3,2,1,0:T(8,128)(2,1)}, u32[]{:S(2)}, u32[]{:S(2)}) async-start(bf16[4,64,64,128]{3,2,1,0:T(8,128)(2,1)} %get-tuple-element.244), calls=%async_computation.6 | async-start | bytes 8388608 | tf_op jit(solution)/shard_map/all_to_all | solution.py:353
  506.1 77.9 %collective-permute-start.57 = (f32[4,128]{1,0:T(4,128)S(1)}, f32[4,128]{1,0:T(4,128)S(1)}, u32[]{:S(2)}, u32[]{:S(2)}) collective-permute-start(f32[4,128]{1,0:T(4,128)S(1)} %broadcast_in_dim.54), channel_id=1, source_target_pairs={{0,16},{8,24},{16,0},{24,8},{1,17},{9,25},{17,1},{25,9},{2,18},{10... | collective-permute-start | bytes 6152 | tf_op jit(solution)/shard_map/ppermute | solution.py:364
  508.9 75.0 %collective-permute-start.58 = (f32[4,128]{1,0:T(4,128)S(1)}, f32[4,128]{1,0:T(4,128)S(1)}, u32[]{:S(2)}, u32[]{:S(2)}) collective-permute-start(f32[4,128]{1,0:T(4,128)S(1)} %broadcast_in_dim.54), channel_id=1, source_target_pairs={{0,24},{8,16},{16,8},{24,0},{1,25},{9,17},{17,9},{25,1},{2,26},{10... | collective-permute-start | bytes 6152 | tf_op jit(solution)/shard_map/ppermute | solution.py:364
  510.4 73.6 %collective-permute-start.56 = (f32[4,128]{1,0:T(4,128)S(1)}, f32[4,128]{1,0:T(4,128)S(1)}, u32[]{:S(2)}, u32[]{:S(2)}) collective-permute-start(f32[4,128]{1,0:T(4,128)S(1)} %broadcast_in_dim.54), channel_id=1, source_target_pairs={{0,8},{8,0},{16,24},{24,16},{1,9},{9,1},{17,25},{25,17},{2,10},{10... | collective-permute-start | bytes 6152 | tf_op jit(solution)/shard_map/ppermute | solution.py:364
  584.0 64.3 %all-to-all-start.8 = ((bf16[4,32,64,128]{3,2,1,0:T(8,128)(2,1)}), bf16[4,32,64,128]{3,2,1,0:T(8,128)(2,1)}, u32[]{:S(2)}, u32[]{:S(2)}) async-start(bf16[4,32,64,128]{3,2,1,0:T(8,128)(2,1)} %after.11), calls=%async_computation.8 | async-start | bytes 4194304 | tf_op jit(solution)/shard_map/all_to_all | solution.py:353
  610.2 25.1 %collective-permute-start.67 = (s16[32,32,128]{2,1,0:T(8,128)(2,1)S(1)}, s16[32,32,128]{2,1,0:T(8,128)(2,1)S(1)}, u32[]{:S(2)}, u32[]{:S(2)}) collective-permute-start(s16[32,32,128]{2,1,0:T(8,128)(2,1)S(1)} %get-tuple-element.252), channel_id=1, source_target_pairs={{0,6},{1,7},{2,4},{3,5},{4,2},{5,3},{6,0},{7,1},{8,14},{9,15},{10,... | collective-permute-start | bytes 786440 | tf_op jit(solution)/shard_map/ppermute | solution.py:359
  619.0 34.7 %collective-permute-start.76 = (s16[32,32,128]{2,1,0:T(8,128)(2,1)}, s16[32,32,128]{2,1,0:T(8,128)(2,1)S(1)}, u32[]{:S(2)}, u32[]{:S(2)}) collective-permute-start(s16[32,32,128]{2,1,0:T(8,128)(2,1)} %get-tuple-element.269), channel_id=1, source_target_pairs={{0,1},{1,0},{2,3},{3,2},{4,5},{5,4},{6,7},{7,6},{8,9},{9,8},{10,11... | collective-permute-start | bytes 786440 | tf_op jit(solution)/shard_map/ppermute | solution.py:359
  620.1 35.2 %collective-permute-start.77 = (s16[32,32,128]{2,1,0:T(8,128)(2,1)}, s16[32,32,128]{2,1,0:T(8,128)(2,1)S(1)}, u32[]{:S(2)}, u32[]{:S(2)}) collective-permute-start(s16[32,32,128]{2,1,0:T(8,128)(2,1)} %get-tuple-element.270), channel_id=1, source_target_pairs={{0,2},{1,3},{2,0},{3,1},{4,6},{5,7},{6,4},{7,5},{8,10},{9,11},{10,... | collective-permute-start | bytes 786440 | tf_op jit(solution)/shard_map/ppermute | solution.py:359
  635.7 28.9 %collective-permute-start.80 = (s16[32,32,128]{2,1,0:T(8,128)(2,1)S(1)}, s16[32,32,128]{2,1,0:T(8,128)(2,1)S(1)}, u32[]{:S(2)}, u32[]{:S(2)}) collective-permute-start(s16[32,32,128]{2,1,0:T(8,128)(2,1)S(1)} %get-tuple-element.273), channel_id=1, source_target_pairs={{0,5},{1,4},{2,7},{3,6},{4,1},{5,0},{6,3},{7,2},{8,13},{9,12},{10,... | collective-permute-start | bytes 786440 | tf_op jit(solution)/shard_map/ppermute | solution.py:359
  659.5 53.7 %all-to-all-start.7 = ((bf16[4,32,64,128]{3,2,1,0:T(8,128)(2,1)}), bf16[4,32,64,128]{3,2,1,0:T(8,128)(2,1)}, u32[]{:S(2)}, u32[]{:S(2)}) async-start(bf16[4,32,64,128]{3,2,1,0:T(8,128)(2,1)} %after.10), calls=%async_computation.7 | async-start | bytes 4194304 | tf_op jit(solution)/shard_map/all_to_all | solution.py:353
  (133 other events, 1639.9 us)
Sparse Core Ops, SparseCore 0:
  9.9 30.8 all-gather.1

commit v5 on v4

--- a/solution.py
+++ b/solution.py
@@ -17,6 +17,7 @@
 GROUP = 16
 HALVES = 2
 EASE = 4
+BACK_EASE = 4
 VMEM = 52 * 1024 * 1024
 
 
@@ -78,6 +79,7 @@
         self.hours, self.lats, self.lons = zs * hour_local, zs * lat_local, qs * lon_local
         self.cells = self.hp * lat_rows * self.lons
         self.token = None
+        self.ease = EASE
 
     def call(self, body, name, grid, out_shape, in_specs, out_specs, flops, moved, scratch=(), aliases={}):
         tokens = [] if self.token is None else [self.token]
@@ -101,7 +103,7 @@
                 scratch_shapes=list(scratch),
                 input_output_aliases=aliases,
                 compiler_params=pltpu.CompilerParams(vmem_limit_bytes=VMEM),
-                cost_estimate=pl.CostEstimate(flops=flops * EASE, bytes_accessed=moved * EASE, transcendentals=0),
+                cost_estimate=pl.CostEstimate(flops=flops * self.ease, bytes_accessed=moved * self.ease, transcendentals=0),
             )(*args, *tokens)
             self.token = out[-1]
             return out[:-1]
@@ -123,12 +125,12 @@
     def parts_specs(self, group):
         return [pl.BlockSpec((group, self.lr, self.ol), lambda i: (i, 0, 0))] * self.qs
 
-    def parts_shape(self, kind):
-        return [struct((self.hp, self.lr, self.ol), kind)] * self.qs
-
-    def grid_spec(self, group, c=None):
-        start = 0 if c is None else c * (self.hp // group)
-        return pl.BlockSpec((group, self.lr, self.lons), lambda i: (i + start, 0, 0))
+    def parts_shape(self, kind, size=None):
+        return [struct((size or self.hp, self.lr, self.ol), kind)] * self.qs
+
+    def grid_spec(self, group, start=0):
+        offset = start // group
+        return pl.BlockSpec((group, self.lr, self.lons), lambda i: (i + offset, 0, 0))
 
     def hourly(self, noise, tables):
         zs, hp, al, ol, hours = self.zs, self.hp, self.al, self.ol, self.hours
@@ -153,24 +155,25 @@
             [pltpu.VMEM((hours * GROUP, ol), F32)],
         )(noise, tables)
 
-    def lat_up(self, c, g, lat, gain):
-        zs, qs, hp, lr, ol, lats = self.zs, self.qs, self.hp, self.lr, self.ol, self.lats
+    def lat_up(self, start, size, g, lat, gain):
+        zs, qs, lr, ol, lats = self.zs, self.qs, self.lr, self.ol, self.lats
+        cells = size * lr * self.lons
         group = 8
-        offset = c * (hp // group) if g.shape[1] == self.hl else 0
+        offset = start // group
 
         def body(gain_ref, g_ref, lat_ref, *outs):
-            for start in range(0, group, 4):
-                part = [g_ref[:, start + k].reshape(lats, ol) for k in range(4)]
+            for h in range(0, group, 4):
+                part = [g_ref[:, h + k].reshape(lats, ol) for k in range(4)]
                 total = dot(lat_ref[...], jnp.concatenate(part, axis=1))
                 code = encode(total * gain_ref[0])
                 for k in range(4):
                     for d in range(qs):
-                        outs[d][start + k] = code[d * lr : (d + 1) * lr, k * ol : (k + 1) * ol]
+                        outs[d][h + k] = code[d * lr : (d + 1) * lr, k * ol : (k + 1) * ol]
 
         return self.call(
-            body, "lat_up", hp // group, self.parts_shape(I16),
+            body, "lat_up", size // group, self.parts_shape(I16, size),
             [SCALARS, pl.BlockSpec((zs, group, self.al, ol), lambda i: (0, i + offset, 0, 0)), whole_spec(lat.shape)],
-            self.parts_specs(group), 2 * self.cells * self.lats, 4 * self.cells,
+            self.parts_specs(group), 2 * cells * self.lats, 4 * cells,
         )(gain.reshape(1), g, lat)
 
     def residual(self, c, codes, back, lon_up, lon_down, observed, mask):
@@ -199,16 +202,17 @@
         out = self.call(
             body, "residual", hp // group,
             [struct((hp, lr, lons), F32), struct((8, 128), F32)] + self.parts_shape(BF16),
-            [SCALARS] + self.parts_specs(group) + [whole_spec(lon_up.shape)] * 2 + [self.grid_spec(group, c)] * 2,
+            [SCALARS] + self.parts_specs(group) + [whole_spec(lon_up.shape)] * 2 + [self.grid_spec(group, c * hp)] * 2,
             [self.grid_spec(group), whole_spec((8, 128))] + self.parts_specs(group),
             8 * self.cells * lons, 16 * self.cells,
         )(back.reshape(1), *codes, lon_up, lon_down, observed, mask)
         return out[0], out[1], out[2:]
 
-    def lat_down(self, c, v, lat_t, earlier):
+    def lat_down(self, c, v, lat_t, whole, earlier):
         zs, qs, hp, al, lr, ol, lats = self.zs, self.qs, self.hp, self.al, self.lr, self.ol, self.lats
 
-        offset = c * (hp // GROUP)
+        offset = c * (hp // GROUP) if whole else 0
+        size = self.hl if whole else hp
 
         def body(*refs):
             sent, lat_ref, (out_ref, turned) = refs[:qs], refs[qs], refs[-2:]
@@ -220,46 +224,52 @@
             out_ref[...] = turned[...].reshape(zs, al, GROUP, ol).astype(BF16)
 
         return self.call(
-            body, "lat_down", hp // GROUP, [struct((zs, al, self.hl, ol), BF16)],
+            body, "lat_down", hp // GROUP, [struct((zs, al, size, ol), BF16)],
             self.parts_specs(GROUP) + [whole_spec(lat_t.shape)] + [ANYWHERE] * len(earlier),
             [pl.BlockSpec((zs, al, GROUP, ol), lambda i: (0, 0, i + offset, 0))],
             2 * self.cells * lats, 4 * self.cells,
             [pltpu.VMEM((lats * GROUP, ol), F32)], {qs + 1: 0} if earlier else {},
         )(*v, lat_t, *earlier)
 
-    def over_hours(self, x, kern, pieces):
+    def over_hours(self, xs, kern, pieces):
         zs, hl, al, ol, hours = self.zs, self.hl, self.al, self.ol, self.hours
-        hp = hl // pieces
-
-        def body(x_ref, kern_ref, *refs):
-            outs, (bend_ref, turned) = refs[:pieces], refs[pieces:]
+        count = len(xs)
+
+        def body(*refs):
+            arrived, kern_ref, refs = refs[:count], refs[count], refs[count + 1 :]
+            outs, (bend_ref, turned) = refs[: len(pieces)], refs[len(pieces) :]
 
             @pl.when(pl.program_id(0) == 0)
             def _():
                 bend_ref[...] = jnp.zeros_like(bend_ref)
 
             for start in range(0, GROUP, 4):
-                part = [x_ref[:, start + k].reshape(hours, ol) for k in range(4)]
+                part = []
+                for k in range(4):
+                    rows = [x[z, start + k] for z in range(zs) for x in arrived]
+                    part.append(jnp.concatenate(rows, axis=0))
                 part = jnp.concatenate(part, axis=1)
                 total = dot(kern_ref[0], part) + dot(kern_ref[1], part)
                 bend_ref[...] += fold(total * part.astype(F32))
                 for k in range(4):
                     turned[pl.ds(start + k, hours, stride=GROUP), :] = total[:, k * ol : (k + 1) * ol]
-            value = turned[...].reshape(zs, pieces, hp, GROUP, ol).astype(BF16)
-            for c in range(pieces):
-                outs[c][...] = value[:, c]
+            value = turned[...].reshape(zs, hl, GROUP, ol).astype(BF16)
+            for out_ref, (first, size) in zip(outs, pieces):
+                out_ref[...] = value[:, first : first + size]
 
         out = self.call(
-            body, "over_hours", al // GROUP, [struct((zs, hp, al, ol), BF16)] * pieces + [struct((8, 128), F32)],
-            [pl.BlockSpec((zs, GROUP, hl, ol), lambda i: (0, i, 0, 0)), whole_spec(kern.shape)],
-            [pl.BlockSpec((zs, hp, GROUP, ol), lambda i: (0, 0, i, 0))] * pieces + [whole_spec((8, 128))],
+            body, "over_hours", al // GROUP, [struct((zs, size, al, ol), BF16) for _, size in pieces] + [struct((8, 128), F32)],
+            [pl.BlockSpec((zs, GROUP, hl // count, ol), lambda i: (0, i, 0, 0))] * count + [whole_spec(kern.shape)],
+            [pl.BlockSpec((zs, size, GROUP, ol), lambda i: (0, 0, i, 0)) for _, size in pieces]
+            + [whole_spec((8, 128))],
             8 * self.cells * hours, 8 * self.cells,
             [pltpu.VMEM((hours * GROUP, ol), F32)],
-        )(x, kern)
-        return out[:pieces], out[-1]
-
-    def finish(self, s, c, codes, back, step, lon_up, prior, observed, mask, earlier):
+        )(*xs, kern)
+        return out[:-1], out[-1]
+
+    def finish(self, s, first, size, codes, back, step, lon_up, prior, observed, mask, earlier):
         qs, hp, lr, ol, lons = self.qs, self.hp, self.lr, self.ol, self.lons
+        cells = size * lr * lons
         group = 8
         rows = group * lr
 
@@ -276,14 +286,14 @@
             next_ref[...] = (resid - seen * scaled - scalar_ref[1] * resid).reshape(shape)
 
         full = struct((2, self.hl, lr, lons), F32)
-        start = c * (hp // group)
-        out_spec = pl.BlockSpec((1, group, lr, lons), lambda i: (s, i + start, 0, 0))
+        offset = first // group
+        out_spec = pl.BlockSpec((1, group, lr, lons), lambda i: (s, i + offset, 0, 0))
         count = 1 + qs + 4
         return self.call(
-            body, "finish", hp // group, [full, full],
-            [SCALARS] + self.parts_specs(group) + [whole_spec(lon_up.shape), self.grid_spec(group)]
-            + [self.grid_spec(group, c)] * 2 + [ANYWHERE] * len(earlier),
-            [out_spec, out_spec], 4 * self.cells * lons, 22 * self.cells,
+            body, "finish", size // group, [full, full],
+            [SCALARS] + self.parts_specs(group) + [whole_spec(lon_up.shape), self.grid_spec(group, first % hp)]
+            + [self.grid_spec(group, first)] * 2 + [ANYWHERE] * len(earlier),
+            [out_spec, out_spec], 4 * cells * lons, 22 * cells,
             aliases={count + i: i for i in range(len(earlier))},
         )(jnp.stack([back * step, NOISE_VAR * step]), *codes, lon_up, prior, observed, mask, *earlier)
 
@@ -300,9 +310,8 @@
         h = h.reshape(self.zs, HALVES, self.hp, self.al, self.ol)
         return [h[:, c] for c in range(HALVES)]
 
-    def lat_up(self, c, g, lat, gain):
-        if g.shape[1] == self.hl:
-            g = g[:, c * self.hp : (c + 1) * self.hp]
+    def lat_up(self, start, size, g, lat, gain):
+        g = g[:, start : start + size]
         split = lat.reshape(self.qs, self.lr, self.zs, self.al)
         x = encode(jnp.einsum("qlzy,zhyx->qhlx", split, g, preferred_element_type=F32) * gain)
         return [x[d] for d in range(self.qs)]
@@ -311,42 +320,37 @@
         x = jnp.concatenate([decode(c) for c in codes], axis=2)
         return jnp.einsum("hlx,xo->hlo", x, lon_up.astype(F32), precision=HIGH)
 
-    def half(self, x, c):
-        return x[c * self.hp : (c + 1) * self.hp]
-
     def residual(self, c, codes, back, lon_up, lon_down, observed, mask):
         prior = self.up(codes, lon_up) * back
-        resid = self.half(mask, c).astype(F32) * (self.half(observed, c) - prior)
+        here = slice(c * self.hp, (c + 1) * self.hp)
+        resid = mask[here].astype(F32) * (observed[here] - prior)
         v = jnp.einsum("hlo,op->hlp", resid, lon_down.astype(F32), precision=HIGH).astype(BF16)
         return prior, jnp.sum(resid * resid), jnp.split(v, self.qs, axis=2)
 
-    def lat_down(self, c, v, lat_t, earlier):
+    def lat_down(self, c, v, lat_t, whole, earlier):
         split = lat_t.reshape(self.zs, self.al, self.qs, self.lr)
         x = jnp.einsum("zyql,qhlx->zyhx", split, jnp.stack(v), preferred_element_type=F32)
         return (jnp.concatenate(list(earlier) + [x.astype(BF16)], axis=2),)
 
-    def over_hours(self, x, kern, pieces):
+    def over_hours(self, xs, kern, pieces):
+        x = jnp.concatenate(xs, axis=2)
         x = jnp.swapaxes(x, 0, 1).reshape(self.al, self.hours, self.ol).astype(F32)
         y = jnp.einsum("gk,ykx->gyx", kern.astype(F32).sum(0), x, precision=HIGH)
         bend = jnp.einsum("gyx,ygx->", y, x)
-        y = y.astype(BF16).reshape(self.zs, pieces, self.hl // pieces, self.al, self.ol)
-        return [y[:, c] for c in range(pieces)], bend
-
-    def finish(self, s, c, codes, back, step, lon_up, prior, observed, mask, earlier):
+        y = y.astype(BF16).reshape(self.zs, self.hl, self.al, self.ol)
+        return [y[:, first : first + size] for first, size in pieces], bend
+
+    def finish(self, s, first, size, codes, back, step, lon_up, prior, observed, mask, earlier):
         scaled = self.up(codes, lon_up) * (back * step)
-        seen = self.half(mask, c).astype(F32)
-        resid = seen * (self.half(observed, c) - prior)
-        return tuple(earlier) + ((prior + scaled, resid - seen * scaled - NOISE_VAR * step * resid),)
+        here = slice(first, first + size)
+        prior = prior[first % self.hp : first % self.hp + size]
+        seen = mask[here].astype(F32)
+        resid = seen * (observed[here] - prior)
+        return tuple(earlier) + ((s, prior + scaled, resid - seen * scaled - NOISE_VAR * step * resid),)
 
     def joined(self, earlier):
-        whole = []
-        for i in range(2):
-            samples = [
-                jnp.concatenate([pair[i] for pair in earlier[s * HALVES : (s + 1) * HALVES]])
-                for s in range(2)
-            ]
-            whole.append(jnp.stack(samples))
-        return tuple(whole)
+        samples = [[e[1:] for e in earlier if e[0] == s] for s in range(2)]
+        return tuple(jnp.stack([jnp.concatenate([e[i] for e in part]) for part in samples]) for i in range(2))
 
 
 def swap_tm(x):
@@ -428,7 +432,7 @@
     codes, priors, norms, sent, down = {}, {}, {}, {}, {}
 
     def up(u):
-        codes[u] = swap_lon(stages.lat_up(u[1], arrived[u], lat, first_gain))
+        codes[u] = swap_lon(stages.lat_up(0, hour_part, arrived[u], lat, first_gain))
 
     def middle(u):
         priors[u], norms[u], v = stages.residual(
@@ -437,8 +441,7 @@
         sent[u] = swap_lon(v)
 
     def lower(u):
-        s, c = u
-        down[s] = stages.lat_down(c, sent[u], lat_t, down.get(s, ()))
+        down[u] = stages.lat_down(u[1], sent[u], lat_t, u[0] == 0, down[first] if u == second else ())
 
     up(first)
     middle(first)
@@ -449,53 +452,59 @@
     middle(second)
     up(third)
     lower(second)
-    down[0] = swap_tm(wait(down[0][0]))
+    down[second] = swap_tm(wait(down[second][0]))
     up(fourth)
     middle(third)
     lower(third)
     middle(fourth)
+    down[third] = swap_tm(wait(down[third][0]))
+    early, bending = stages.over_hours([down[second]], kern, [(0, hour_part), (hour_part, hour_part)])
+    sums = [sum(jnp.sum(norms[u]) for u in units if u[0] == s) for s in range(2)] + [jnp.sum(bending)]
     lower(fourth)
-    down[1] = swap_tm(down[1][0])
-
-    sums = []
-    for s in range(2):
-        sums.append(sum(jnp.sum(norms[u]) for u in units if u[0] == s))
-        pieces, bending = stages.over_hours(down[s], kern, 1 if s == 0 else HALVES)
-        sums.append(jnp.sum(bending))
-        if s == 0:
-            arrived[first] = arrived[second] = swap_tm(pieces[0])
-        else:
-            waves[third], waves[fourth] = pieces
+    down[fourth] = swap_tm(down[fourth][0])
+    early = list(early)
+    early[0] = swap_tm(early[0])
+
+    quarter = hour_part // 2
+    pieces = [(0, hour_part), (hour_part, quarter), (hour_part + quarter, hour_part - quarter)]
+    late, bending = stages.over_hours([down[third], down[fourth]], kern, pieces)
+    sums.append(jnp.sum(bending))
     sums = add_over_tm(jnp.broadcast_to(jnp.stack(sums)[:, None], (4, 128)), zs)
-    arrived[third] = swap_tm(wait(waves[third], sums))
+    late = list(late)
+    early[1] = swap_tm(wait(early[1], sums))
     sums = add_over_lon(sums, qs)[:, 0]
     gains, steps = [], []
     for s in range(2):
-        norm_sq, bending = sums[2 * s], sums[2 * s + 1]
+        norm_sq, bending = sums[s], sums[2 + s]
         bound = SPECTRUM_MAX * lat_row_norm * lat_norm * lon_col_norm * jnp.sqrt(norm_sq)
         gains.append(CODE_MAX / jnp.maximum(bound, 1e-30))
         steps.append(norm_sq / (bending + NOISE_VAR * norm_sq))
     earlier = ()
 
-    def back(u):
-        s, c = u
-        codes[u] = swap_lon(stages.lat_up(c, arrived[u], lat, gains[s]))
-
-    def end(u):
-        s, c = u
+    stages.ease = BACK_EASE
+
+    def back(s, start, size, g):
+        return swap_lon(stages.lat_up(start, size, g, lat, gains[s]))
+
+    def end(s, start, size, codes):
+        prior = priors[s, start // hour_part]
         return stages.finish(
-            s, c, codes[u], 1.0 / gains[s], steps[s], lon_up, priors[u], observed, mask, earlier
+            s, start, size, codes, 1.0 / gains[s], steps[s], lon_up, prior, observed, mask, earlier
         )
 
-    back(first)
-    back(second)
-    earlier = end(first)
-    arrived[fourth] = swap_tm(wait(waves[fourth]))
-    back(third)
-    earlier = end(second)
-    earlier = end(third)
-    back(fourth)
-    earlier = end(fourth)
+    codes = back(0, 0, hour_part, early[0])
+    earlier = end(0, 0, hour_part, codes)
+    late[0] = swap_tm(wait(late[0]))
+    codes = back(0, 0, hour_part, early[1])
+    earlier = end(0, hour_part, hour_part, codes)
+    late[1] = swap_tm(wait(late[1]))
+    codes = back(1, 0, hour_part, late[0])
+    earlier = end(1, *pieces[0], codes)
+    late[2] = swap_tm(wait(late[2]))
+    codes = back(1, 0, pieces[1][1], late[1])
+    earlier = end(1, *pieces[1], codes)
+    codes = back(1, 0, pieces[2][1], late[2])
+    earlier = end(1, *pieces[2], codes)
     return stages.joined(earlier)
 
 

time: 774 us -> 749 us (0.968)
  waiting for transfers between devices: 359 us -> 267 us
  blocking collectives: 0 us -> 52.2 us
  starting transfers between devices: 126 us -> 142 us
    all_to_all x9 -> x11, waiting for transfers between devices: 131 us -> 65.4 us  [swap_tm(): return lax.all_to_all(x, 'tm', split_axis=0, concat_axis=0, tiled=True)]
    all_to_all x0 -> x1, blocking collectives: none -> 52.2 us  [swap_tm(): return lax.all_to_all(x, 'tm', split_axis=0, concat_axis=0, tiled=True)]
    ppermute x3, waiting for transfers between devices: 73.5 us -> 28.5 us  [add_over_tm(): lax.ppermute(x, 'tm', [(i, i ^ d) for i in range(count)])]
    ppermute x84 -> x91, waiting for transfers between devices: 151 us -> 171 us  [swap_lon(): lax.ppermute(parts[d], 'lon', [(i, i ^ d) for i in range(count)])]
    ppermute x84 -> x91, starting transfers between devices: 73.2 us -> 81.2 us  [swap_lon(): lax.ppermute(parts[d], 'lon', [(i, i ^ d) for i in range(count)])]
    all_to_all x9 -> x11, starting transfers between devices: 45.9 us -> 52.8 us  [swap_tm(): return lax.all_to_all(x, 'tm', split_axis=0, concat_axis=0, tiled=True)]
    unnamed x117 -> x105, local copies, waits for them, and re-layouts: 21.6 us -> 17.9 us
    pallas_call x24 -> x26, Pallas kernels: 196 us -> 198 us  [run(): pl.pallas_call(whole, name=name, grid=(grid,), out_shape=list(out_shape)...]
  transfers between devices with their start and end apart: 100 -> 109, of which waited for: 38 -> 45; matrix products, arithmetic and copies ran while one was open for 5% -> 5% of each run, Pallas kernels for 23% -> 25%
where the time goes in v5:
time: 749 us; the launch traced here: 738 us
  waiting for transfers between devices  267 us (36%)
  Pallas kernels  198 us (26%)
  starting transfers between devices  142 us (19%)
  blocking collectives  52.2 us (7%)
  local copies, waits for them, and re-layouts  34.5 us (5%)
  between operations  24.8 us (3%)
  other arithmetic  15.4 us (2%)
    pallas_call x26, Pallas kernels, run(): pl.pallas_call(whole, name=name, grid=(grid,), out_shape=list(out_shape)...  198 us
    ppermute x91, waiting for transfers between devices, swap_lon(): lax.ppermute(parts[d], 'lon', [(i, i ^ d) for i in range(count)])  171 us
    ppermute x91, starting transfers between devices, swap_lon(): lax.ppermute(parts[d], 'lon', [(i, i ^ d) for i in range(count)])  81.2 us
    all_to_all x11, waiting for transfers between devices, swap_tm(): return lax.all_to_all(x, 'tm', split_axis=0, concat_axis=0, tiled=True)  65.4 us
    all_to_all x11, starting transfers between devices, swap_tm(): return lax.all_to_all(x, 'tm', split_axis=0, concat_axis=0, tiled=True)  52.8 us
    all_to_all x1, blocking collectives, swap_tm(): return lax.all_to_all(x, 'tm', split_axis=0, concat_axis=0, tiled=True)  52.2 us
    ppermute x3, waiting for transfers between devices, add_over_tm(): lax.ppermute(x, 'tm', [(i, i ^ d) for i in range(count)])  28.5 us
    unnamed x105, local copies, waits for them, and re-layouts  17.9 us
  transfers between devices with their start and end apart: 109, of which 45 were waited for; matrix products, arithmetic and copies ran while one was open for 5% of the time, Pallas kernels for 25%

profile of v5, /device:TPU:0, one launch (start us, length us, event | category | flops | bytes accessed | tf_op | source)
XLA Modules:
  0.0 738.4 jit_solution(13244622980641403729)
XLA Ops:
  15.6 11.1 %hourly.2 = (bf16[4,32,64,128]{3,2,1,0:T(8,128)(2,1)}, bf16[4,32,64,128]{3,2,1,0:T(8,128)(2,1)}, f32[8,128]{1,0:T(8,128)S(1)}) custom-call(bf16[2,64,128,512]{3,2,1,0:T(8,128)(2,1)} %refs_0_.3, bf16[2,256,512]{2,1,0:T(8,128)(2,1)S(1)} %get-tuple-element.332.refs_1_), custom_call_target="tpu_custom_call" | custom-call | flops 17179869184 | bytes 83886080 | tf_op jit(solution)/shard_map/hourly/pallas_call | solution.py:96
  36.1 11.2 %hourly.3 = (bf16[4,32,64,128]{3,2,1,0:T(8,128)(2,1)}, bf16[4,32,64,128]{3,2,1,0:T(8,128)(2,1)}, f32[8,128]{1,0:T(8,128)S(1)}) custom-call(bf16[2,64,128,512]{3,2,1,0:T(8,128)(2,1)} %refs_0_.3, bf16[2,256,512]{2,1,0:T(8,128)(2,1)S(1)} %get-tuple-element.333.refs_1_, f32[8,128]{1,0:T(8,128)S(1)} %get-tuple-element.165.refs_2_), custom_call_target="tpu_custom_call" | custom-call | flops 17179869184 | bytes 83886080 | tf_op jit(solution)/shard_map/hourly/pallas_call | solution.py:96
  47.3 34.2 %all-to-all-done.refs_1_ = bf16[4,32,64,128]{3,2,1,0:T(8,128)(2,1)} async-done(((bf16[4,32,64,128]{3,2,1,0:T(8,128)(2,1)}), bf16[4,32,64,128]{3,2,1,0:T(8,128)(2,1)}, u32[]{:S(2)}, u32[]{:S(2)}) %all-to-all-start) | async-done | bytes 2097184 | tf_op jit(solution)/shard_map/all_to_all | solution.py:357
  121.5 14.8 %residual.4 = (f32[32,32,1024]{2,1,0:T(8,128)}, f32[8,128]{1,0:T(8,128)S(1)}, bf16[32,32,128]{2,1,0:T(8,128)(2,1)S(1)}, bf16[32,32,128]{2,1,0:T(8,128)(2,1)}, bf...) custom-call(f32[1]{0:T(128)} %bitcast.3.refs_0_, ...), custom_call_target="tpu_custom_call" | custom-call | flops 34359738368 | bytes 67108864 | tf_op jit(solution)/shard_map/residual/pallas_call | solution.py:96
  199.1 7.4 %collective-permute-done.11.refs_6_ = s16[32,32,128]{2,1,0:T(8,128)(2,1)} collective-permute-done((s16[32,32,128]{2,1,0:T(8,128)(2,1)S(1)}, s16[32,32,128]{2,1,0:T(8,128)(2,1)}, u32[]{:S(2)}, u32[]{:S(2)}) %collective-permute-start.11) | collective-permute-done | bytes 262176 | tf_op jit(solution)/shard_map/ppermute | solution.py:363
  206.6 14.8 %residual.5 = (f32[32,32,1024]{2,1,0:T(8,128)}, f32[8,128]{1,0:T(8,128)S(1)}, bf16[32,32,128]{2,1,0:T(8,128)(2,1)S(1)}, bf16[32,32,128]{2,1,0:T(8,128)(2,1)S(1)}...) custom-call(f32[1]{0:T(128)} %bitcast.3.refs_0_, ...), custom_call_target="tpu_custom_call" | custom-call | flops 34359738368 | bytes 67108864 | tf_op jit(solution)/shard_map/residual/pallas_call | solution.py:96
  237.0 11.3 %collective-permute-done.32.refs_5_ = bf16[32,32,128]{2,1,0:T(8,128)(2,1)S(1)} collective-permute-done((bf16[32,32,128]{2,1,0:T(8,128)(2,1)S(1)}, bf16[32,32,128]{2,1,0:T(8,128)(2,1)S(1)}, u32[]{:S(2)}, u32[]{:S(2)}) %collective-permute-start.32) | collective-permute-done | bytes 262176 | tf_op jit(solution)/shard_map/ppermute | solution.py:363
  274.0 14.8 %residual.6 = (f32[32,32,1024]{2,1,0:T(8,128)}, f32[8,128]{1,0:T(8,128)S(1)}, bf16[32,32,128]{2,1,0:T(8,128)(2,1)S(1)}, bf16[32,32,128]{2,1,0:T(8,128)(2,1)S(1)}...) custom-call(f32[1]{0:T(128)} %bitcast.3.refs_0_, ...), custom_call_target="tpu_custom_call" | custom-call | flops 34359738368 | bytes 67108864 | tf_op jit(solution)/shard_map/residual/pallas_call | solution.py:96
  306.6 10.5 %collective-permute-done.46.refs_5_ = bf16[32,32,128]{2,1,0:T(8,128)(2,1)S(1)} collective-permute-done((bf16[32,32,128]{2,1,0:T(8,128)(2,1)S(1)}, bf16[32,32,128]{2,1,0:T(8,128)(2,1)S(1)}, u32[]{:S(2)}, u32[]{:S(2)}) %collective-permute-start.46) | collective-permute-done | bytes 262176 | tf_op jit(solution)/shard_map/ppermute | solution.py:363
  324.7 9.7 %collective-permute-done.38.refs_5_ = s16[32,32,128]{2,1,0:T(8,128)(2,1)S(1)} collective-permute-done((s16[32,32,128]{2,1,0:T(8,128)(2,1)S(1)}, s16[32,32,128]{2,1,0:T(8,128)(2,1)S(1)}, u32[]{:S(2)}, u32[]{:S(2)}) %collective-permute-start.38) | collective-permute-done | bytes 262176 | tf_op jit(solution)/shard_map/ppermute | solution.py:363
  340.4 14.8 %residual.7 = (f32[32,32,1024]{2,1,0:T(8,128)}, f32[8,128]{1,0:T(8,128)S(1)}, bf16[32,32,128]{2,1,0:T(8,128)(2,1)S(1)}, bf16[32,32,128]{2,1,0:T(8,128)(2,1)S(1)}...) custom-call(f32[1]{0:T(128)} %bitcast.3.refs_0_, ...), custom_call_target="tpu_custom_call" | custom-call | flops 34359738368 | bytes 67108864 | tf_op jit(solution)/shard_map/residual/pallas_call | solution.py:96
  381.1 12.5 %collective-permute-done.53.refs_5_ = bf16[32,32,128]{2,1,0:T(8,128)(2,1)S(1)} collective-permute-done((bf16[32,32,128]{2,1,0:T(8,128)(2,1)S(1)}, bf16[32,32,128]{2,1,0:T(8,128)(2,1)S(1)}, u32[]{:S(2)}, u32[]{:S(2)}) %collective-permute-start.53) | collective-permute-done | bytes 262176 | tf_op jit(solution)/shard_map/ppermute | solution.py:363
  398.0 11.8 %all-to-all-done.5.refs_0_ = bf16[4,64,32,128]{3,2,1,0:T(8,128)(2,1)} async-done(((bf16[4,64,32,128]{3,2,1,0:T(8,128)(2,1)}), bf16[4,64,32,128]{3,2,1,0:T(8,128)(2,1)}, u32[]{:S(2)}, u32[]{:S(2)}) %all-to-all-start.5) | async-done | bytes 2097184 | tf_op jit(solution)/shard_map/all_to_all | solution.py:357
  409.8 52.2 %all_to_all.60.refs_1_ = bf16[4,64,32,128]{3,2,1,0:T(8,128)(2,1)} all-to-all(bf16[4,64,32,128]{3,2,1,0:T(8,128)(2,1)} %get-tuple-element.254), channel_id=1, replica_groups=mesh['tm'=4,'lon'=8] {'tm'}, dimensions={0} | all-to-all | bytes 4194304 | tf_op jit(solution)/shard_map/all_to_all | solution.py:357
  485.5 28.5 %collective-permute-done.57 = f32[4,128]{1,0:T(4,128)S(1)} collective-permute-done((f32[4,128]{1,0:T(4,128)S(1)}, f32[4,128]{1,0:T(4,128)S(1)}, u32[]{:S(2)}, u32[]{:S(2)}) %collective-permute-start.57) | collective-permute-done | bytes 2080 | tf_op jit(solution)/shard_map/ppermute | solution.py:368
  547.2 12.4 %collective-permute-done.66.refs_6_ = s16[32,32,128]{2,1,0:T(8,128)(2,1)S(1)} collective-permute-done((s16[32,32,128]{2,1,0:T(8,128)(2,1)S(1)}, s16[32,32,128]{2,1,0:T(8,128)(2,1)S(1)}, u32[]{:S(2)}, u32[]{:S(2)}) %collective-permute-start.66) | collective-permute-done | bytes 262176 | tf_op jit(solution)/shard_map/ppermute | solution.py:363
  560.3 11.9 %finish.5 = (f32[2,64,32,1024]{3,2,1,0:T(8,128)}, f32[2,64,32,1024]{3,2,1,0:T(8,128)}, f32[8,128]{1,0:T(8,128)S(1)}) custom-call(f32[2]{0:T(128)S(1)} %pad_maximum_fusion.5.refs_0_, s16[32,32,128]{2,1,0:T(8,128)(2,1)S(1)} %get-tuple-element.261.refs_1_, s16[32,32,128]{2,1,0:T(8,128)(2,1)S(1)} %collective-permute-done.62.refs_2_, ...), custom_call_target="tpu_custom_call" | custom-call | flops 17179869184 | bytes 92274688 | tf_op jit(solution)/shard_map/finish/pallas_call | solution.py:96
  596.6 13.0 %collective-permute-done.73.refs_6_ = s16[32,32,128]{2,1,0:T(8,128)(2,1)S(1)} collective-permute-done((s16[32,32,128]{2,1,0:T(8,128)(2,1)S(1)}, s16[32,32,128]{2,1,0:T(8,128)(2,1)S(1)}, u32[]{:S(2)}, u32[]{:S(2)}) %collective-permute-start.73) | collective-permute-done | bytes 262176 | tf_op jit(solution)/shard_map/ppermute | solution.py:363
  610.3 11.8 %finish.6 = (f32[2,64,32,1024]{3,2,1,0:T(8,128)}, f32[2,64,32,1024]{3,2,1,0:T(8,128)}, f32[8,128]{1,0:T(8,128)S(1)}) custom-call(f32[2]{0:T(128)S(1)} %pad_maximum_fusion.5.refs_0_, s16[32,32,128]{2,1,0:T(8,128)(2,1)S(1)} %get-tuple-element.273.refs_1_, ...), custom_call_target="tpu_custom_call", output_to_operand_aliasing={{0}: (13, {}), {1}: (14, {})} | custom-call | flops 17179869184 | bytes 92274688 | tf_op jit(solution)/shard_map/finish/pallas_call | solution.py:96
  648.4 9.5 %collective-permute-done.80.refs_6_ = s16[32,32,128]{2,1,0:T(8,128)(2,1)S(1)} collective-permute-done((s16[32,32,128]{2,1,0:T(8,128)(2,1)S(1)}, s16[32,32,128]{2,1,0:T(8,128)(2,1)S(1)}, u32[]{:S(2)}, u32[]{:S(2)}) %collective-permute-start.80) | collective-permute-done | bytes 262176 | tf_op jit(solution)/shard_map/ppermute | solution.py:363
  658.6 11.9 %finish.7 = (f32[2,64,32,1024]{3,2,1,0:T(8,128)}, f32[2,64,32,1024]{3,2,1,0:T(8,128)}, f32[8,128]{1,0:T(8,128)S(1)}) custom-call(f32[2]{0:T(128)S(1)} %pad_maximum_fusion.4.refs_0_, s16[32,32,128]{2,1,0:T(8,128)(2,1)S(1)} %get-tuple-element.286.refs_1_, ...), custom_call_target="tpu_custom_call", output_to_operand_aliasing={{0}: (13, {}), {1}: (14, {})} | custom-call | flops 17179869184 | bytes 92274688 | tf_op jit(solution)/shard_map/finish/pallas_call | solution.py:96
  689.8 7.2 collective-permute-done.87.refs_6_
  697.0 7.2 finish.8
  717.0 7.2 collective-permute-done.94.refs_6_
  (377 shorter events, 362.0 us)
Async XLA Ops:
  7.2 87.8 %all-gather.2.cloned.1.call-start = ((), (), s32[]{:S(2)}) async-start(), calls=%async_computation.12 | async-start | bytes 2359296 | tf_op jit(solution)/shard_map/all_gather | solution.py:412
  26.8 54.7 %all-to-all-start = ((bf16[4,32,64,128]{3,2,1,0:T(8,128)(2,1)}), bf16[4,32,64,128]{3,2,1,0:T(8,128)(2,1)}, u32[]{:S(2)}, u32[]{:S(2)}) async-start(bf16[4,32,64,128]{3,2,1,0:T(8,128)(2,1)} %get-tuple-element.164), calls=%async_computation | async-start | bytes 4194304 | tf_op jit(solution)/shard_map/all_to_all | solution.py:357
  88.4 53.4 %all-to-all-start.1 = ((bf16[4,32,64,128]{3,2,1,0:T(8,128)(2,1)}), bf16[4,32,64,128]{3,2,1,0:T(8,128)(2,1)}, u32[]{:S(2)}, u32[]{:S(2)}) async-start(bf16[4,32,64,128]{3,2,1,0:T(8,128)(2,1)} %after.9), calls=%async_computation.1 | async-start | bytes 4194304 | tf_op jit(solution)/shard_map/all_to_all | solution.py:357
  141.8 52.8 %all-to-all-start.2 = ((bf16[4,32,64,128]{3,2,1,0:T(8,128)(2,1)}), bf16[4,32,64,128]{3,2,1,0:T(8,128)(2,1)}, u32[]{:S(2)}, u32[]{:S(2)}) async-start(bf16[4,32,64,128]{3,2,1,0:T(8,128)(2,1)} %after.10), calls=%async_computation.2 | async-start | bytes 4194304 | tf_op jit(solution)/shard_map/all_to_all | solution.py:357
  171.5 27.6 %collective-permute-start.9 = (s16[32,32,128]{2,1,0:T(8,128)(2,1)S(1)}, s16[32,32,128]{2,1,0:T(8,128)(2,1)S(1)}, u32[]{:S(2)}, u32[]{:S(2)}) collective-permute-start(s16[32,32,128]{2,1,0:T(8,128)(2,1)S(1)} %get-tuple-element.182), channel_id=1, source_target_pairs={{0,3},{1,2},{2,1},{3,0},{4,7},{5,6},{6,5},{7,4},{8,11},{9,10},{10,... | collective-permute-start | bytes 786440 | tf_op jit(solution)/shard_map/ppermute | solution.py:363
  172.9 26.2 %collective-permute-start.10 = (s16[32,32,128]{2,1,0:T(8,128)(2,1)S(1)}, s16[32,32,128]{2,1,0:T(8,128)(2,1)S(1)}, u32[]{:S(2)}, u32[]{:S(2)}) collective-permute-start(s16[32,32,128]{2,1,0:T(8,128)(2,1)S(1)} %get-tuple-element.183), channel_id=1, source_target_pairs={{0,4},{1,5},{2,6},{3,7},{4,0},{5,1},{6,2},{7,3},{8,12},{9,13},{10,... | collective-permute-start | bytes 786440 | tf_op jit(solution)/shard_map/ppermute | solution.py:363
  175.4 31.1 %collective-permute-start.11 = (s16[32,32,128]{2,1,0:T(8,128)(2,1)S(1)}, s16[32,32,128]{2,1,0:T(8,128)(2,1)}, u32[]{:S(2)}, u32[]{:S(2)}) collective-permute-start(s16[32,32,128]{2,1,0:T(8,128)(2,1)S(1)} %get-tuple-element.184), channel_id=1, source_target_pairs={{0,5},{1,4},{2,7},{3,6},{4,1},{5,0},{6,3},{7,2},{8,13},{9,12},{10,... | collective-permute-start | bytes 786440 | tf_op jit(solution)/shard_map/ppermute | solution.py:363
  179.6 26.9 %collective-permute-start.12 = (s16[32,32,128]{2,1,0:T(8,128)(2,1)S(1)}, s16[32,32,128]{2,1,0:T(8,128)(2,1)}, u32[]{:S(2)}, u32[]{:S(2)}) collective-permute-start(s16[32,32,128]{2,1,0:T(8,128)(2,1)S(1)} %get-tuple-element.185), channel_id=1, source_target_pairs={{0,6},{1,7},{2,4},{3,5},{4,2},{5,3},{6,0},{7,1},{8,14},{9,15},{10,... | collective-permute-start | bytes 786440 | tf_op jit(solution)/shard_map/ppermute | solution.py:363
  194.6 62.6 %all-to-all-start.3 = ((bf16[4,32,64,128]{3,2,1,0:T(8,128)(2,1)}), bf16[4,32,64,128]{3,2,1,0:T(8,128)(2,1)}, u32[]{:S(2)}, u32[]{:S(2)}) async-start(bf16[4,32,64,128]{3,2,1,0:T(8,128)(2,1)} %after.11), calls=%async_computation.3 | async-start | bytes 4194304 | tf_op jit(solution)/shard_map/all_to_all | solution.py:357
  223.8 24.6 %collective-permute-start.32 = (bf16[32,32,128]{2,1,0:T(8,128)(2,1)S(1)}, bf16[32,32,128]{2,1,0:T(8,128)(2,1)S(1)}, u32[]{:S(2)}, u32[]{:S(2)}) collective-permute-start(bf16[32,32,128]{2,1,0:T(8,128)(2,1)S(1)} %get-tuple-element.214), channel_id=1, source_target_pairs={{0,5},{1,4},{2,7},{3,6},{4,1},{5,0},{6,3},{7,2},{8,13},{9,12},{10,... | collective-permute-start | bytes 786440 | tf_op jit(solution)/shard_map/ppermute | solution.py:363
  257.2 99.4 %all-to-all-start.4 = ((bf16[4,64,64,128]{3,2,1,0:T(8,128)(2,1)}), bf16[4,64,64,128]{3,2,1,0:T(8,128)(2,1)}, u32[]{:S(2)}, u32[]{:S(2)}) async-start(bf16[4,64,64,128]{3,2,1,0:T(8,128)(2,1)} %after.12), calls=%async_computation.4 | async-start | bytes 8388608 | tf_op jit(solution)/shard_map/all_to_all | solution.py:357
  267.3 24.3 %collective-permute-start.35 = (s16[32,32,128]{2,1,0:T(8,128)(2,1)S(1)}, s16[32,32,128]{2,1,0:T(8,128)(2,1)S(1)}, u32[]{:S(2)}, u32[]{:S(2)}) collective-permute-start(s16[32,32,128]{2,1,0:T(8,128)(2,1)S(1)} %get-tuple-element.223), channel_id=1, source_target_pairs={{0,1},{1,0},{2,3},{3,2},{4,5},{5,4},{6,7},{7,6},{8,9},{9,8},{10,11... | collective-permute-start | bytes 786440 | tf_op jit(solution)/shard_map/ppermute | solution.py:363
  267.5 24.6 %collective-permute-start.36 = (s16[32,32,128]{2,1,0:T(8,128)(2,1)S(1)}, s16[32,32,128]{2,1,0:T(8,128)(2,1)S(1)}, u32[]{:S(2)}, u32[]{:S(2)}) collective-permute-start(s16[32,32,128]{2,1,0:T(8,128)(2,1)S(1)} %get-tuple-element.224), channel_id=1, source_target_pairs={{0,2},{1,3},{2,0},{3,1},{4,6},{5,7},{6,4},{7,5},{8,10},{9,11},{10,... | collective-permute-start | bytes 786440 | tf_op jit(solution)/shard_map/ppermute | solution.py:363
  292.1 25.0 %collective-permute-start.46 = (bf16[32,32,128]{2,1,0:T(8,128)(2,1)S(1)}, bf16[32,32,128]{2,1,0:T(8,128)(2,1)S(1)}, u32[]{:S(2)}, u32[]{:S(2)}) collective-permute-start(bf16[32,32,128]{2,1,0:T(8,128)(2,1)S(1)} %get-tuple-element.235), channel_id=1, source_target_pairs={{0,5},{1,4},{2,7},{3,6},{4,1},{5,0},{6,3},{7,2},{8,13},{9,12},{10,... | collective-permute-start | bytes 786440 | tf_op jit(solution)/shard_map/ppermute | solution.py:363
  306.2 28.3 %collective-permute-start.38 = (s16[32,32,128]{2,1,0:T(8,128)(2,1)S(1)}, s16[32,32,128]{2,1,0:T(8,128)(2,1)S(1)}, u32[]{:S(2)}, u32[]{:S(2)}) collective-permute-start(s16[32,32,128]{2,1,0:T(8,128)(2,1)S(1)} %get-tuple-element.226), channel_id=1, source_target_pairs={{0,4},{1,5},{2,6},{3,7},{4,0},{5,1},{6,2},{7,3},{8,12},{9,13},{10,... | collective-permute-start | bytes 786440 | tf_op jit(solution)/shard_map/ppermute | solution.py:363
  356.6 53.2 %all-to-all-start.5 = ((bf16[4,64,32,128]{3,2,1,0:T(8,128)(2,1)}), bf16[4,64,32,128]{3,2,1,0:T(8,128)(2,1)}, u32[]{:S(2)}, u32[]{:S(2)}) async-start(bf16[4,64,32,128]{3,2,1,0:T(8,128)(2,1)} %after.13), calls=%async_computation.5 | async-start | bytes 4194304 | tf_op jit(solution)/shard_map/all_to_all | solution.py:357
  462.0 52.0 %all-to-all-start.7 = ((bf16[4,32,64,128]{3,2,1,0:T(8,128)(2,1)}), bf16[4,32,64,128]{3,2,1,0:T(8,128)(2,1)}, u32[]{:S(2)}, u32[]{:S(2)}) async-start(bf16[4,32,64,128]{3,2,1,0:T(8,128)(2,1)} %get-tuple-element.259), calls=%async_computation.7 | async-start | bytes 4194304 | tf_op jit(solution)/shard_map/all_to_all | solution.py:357
  481.2 32.8 %collective-permute-start.57 = (f32[4,128]{1,0:T(4,128)S(1)}, f32[4,128]{1,0:T(4,128)S(1)}, u32[]{:S(2)}, u32[]{:S(2)}) collective-permute-start(f32[4,128]{1,0:T(4,128)S(1)} %broadcast_in_dim.54), channel_id=1, source_target_pairs={{0,16},{8,24},{16,0},{24,8},{1,17},{9,25},{17,1},{25,9},{2,18},{10... | collective-permute-start | bytes 6152 | tf_op jit(solution)/shard_map/ppermute | solution.py:368
  484.0 29.9 %collective-permute-start.58 = (f32[4,128]{1,0:T(4,128)S(1)}, f32[4,128]{1,0:T(4,128)S(1)}, u32[]{:S(2)}, u32[]{:S(2)}) collective-permute-start(f32[4,128]{1,0:T(4,128)S(1)} %broadcast_in_dim.54), channel_id=1, source_target_pairs={{0,24},{8,16},{16,8},{24,0},{1,25},{9,17},{17,9},{25,1},{2,26},{10... | collective-permute-start | bytes 6152 | tf_op jit(solution)/shard_map/ppermute | solution.py:368
  485.5 28.5 %collective-permute-start.56 = (f32[4,128]{1,0:T(4,128)S(1)}, f32[4,128]{1,0:T(4,128)S(1)}, u32[]{:S(2)}, u32[]{:S(2)}) collective-permute-start(f32[4,128]{1,0:T(4,128)S(1)} %broadcast_in_dim.54), channel_id=1, source_target_pairs={{0,8},{8,0},{16,24},{24,16},{1,9},{9,1},{17,25},{25,17},{2,10},{10... | collective-permute-start | bytes 6152 | tf_op jit(solution)/shard_map/ppermute | solution.py:368
  514.0 58.1 %all-to-all-start.9 = ((bf16[4,32,64,128]{3,2,1,0:T(8,128)(2,1)}), bf16[4,32,64,128]{3,2,1,0:T(8,128)(2,1)}, u32[]{:S(2)}, u32[]{:S(2)}) async-start(bf16[4,32,64,128]{3,2,1,0:T(8,128)(2,1)} %after.15), calls=%async_computation.9 | async-start | bytes 4194304 | tf_op jit(solution)/shard_map/all_to_all | solution.py:357
  572.2 54.7 %all-to-all-start.8 = ((bf16[4,32,64,128]{3,2,1,0:T(8,128)(2,1)}), bf16[4,32,64,128]{3,2,1,0:T(8,128)(2,1)}, u32[]{:S(2)}, u32[]{:S(2)}) async-start(bf16[4,32,64,128]{3,2,1,0:T(8,128)(2,1)} %after.14), calls=%async_computation.8 | async-start | bytes 4194304 | tf_op jit(solution)/shard_map/all_to_all | solution.py:357
  644.1 31.3 %all-to-all-start.11 = ((bf16[4,16,64,128]{3,2,1,0:T(8,128)(2,1)}), bf16[4,16,64,128]{3,2,1,0:T(8,128)(2,1)}, u32[]{:S(2)}, u32[]{:S(2)}) async-start(bf16[4,16,64,128]{3,2,1,0:T(8,128)(2,1)} %after.17), calls=%async_computation.11 | async-start | bytes 2097152 | tf_op jit(solution)/shard_map/all_to_all | solution.py:357
  675.4 30.0 %all-to-all-start.10 = ((bf16[4,16,64,128]{3,2,1,0:T(8,128)(2,1)}), bf16[4,16,64,128]{3,2,1,0:T(8,128)(2,1)S(1)}, u32[]{:S(2)}, u32[]{:S(2)}) async-start(bf16[4,16,64,128]{3,2,1,0:T(8,128)(2,1)} %after.16), calls=%async_computation.10 | async-start | bytes 2097152 | tf_op jit(solution)/shard_map/all_to_all | solution.py:357
  (136 other events, 1560.4 us)
Sparse Core Ops, SparseCore 0:
  9.9 30.8 all-gather.1

commit v6 on v5

--- a/solution.py
+++ b/solution.py
@@ -16,8 +16,6 @@
 CODE_MAX = 2.0**13.5
 GROUP = 16
 HALVES = 2
-EASE = 4
-BACK_EASE = 4
 VMEM = 52 * 1024 * 1024
 
 
@@ -79,7 +77,7 @@
         self.hours, self.lats, self.lons = zs * hour_local, zs * lat_local, qs * lon_local
         self.cells = self.hp * lat_rows * self.lons
         self.token = None
-        self.ease = EASE
+        self.ease = 1
 
     def call(self, body, name, grid, out_shape, in_specs, out_specs, flops, moved, scratch=(), aliases={}):
         tokens = [] if self.token is None else [self.token]
@@ -110,17 +108,18 @@
 
         return run
 
-    def after(self, x, token=None):
+    def after(self, x, *tokens):
+        tokens = [self.token, *tokens]
         return pl.pallas_call(
-            lambda x_ref, token_ref, out_ref: None,
+            lambda *refs: None,
             name="after",
             out_shape=struct(x.shape, x.dtype),
-            in_specs=[ANYWHERE, ANYWHERE],
+            in_specs=[ANYWHERE] * (1 + len(tokens)),
             out_specs=ANYWHERE,
             input_output_aliases={0: 0},
             compiler_params=pltpu.CompilerParams(vmem_limit_bytes=VMEM),
             cost_estimate=pl.CostEstimate(flops=0, bytes_accessed=0, transcendentals=0),
-        )(x, self.token if token is None else token)
+        )(x, *tokens)
 
     def parts_specs(self, group):
         return [pl.BlockSpec((group, self.lr, self.ol), lambda i: (i, 0, 0))] * self.qs
@@ -302,7 +301,7 @@
 
 
 class Plain(Kernels):
-    def after(self, x, token=None):
+    def after(self, x, *tokens):
         return x
 
     def hourly(self, noise, tables):
@@ -409,8 +408,12 @@
         top = lax.reduce_precision(kern, 8, 7)
         return jnp.stack([top.astype(BF16), (kern - top).astype(BF16)])
 
-    lon = lax.all_gather(lon_factor, "lon", axis=0, tiled=True).reshape(lon_count, qs, lon_local)
+    lon = lax.all_gather(lon_factor, "lon", axis=0, tiled=True)
     units = [(s, c) for s in range(2) for c in range(HALVES)]
+    lon_down = jnp.concatenate(
+        [lax.dynamic_slice_in_dim(lon, order[d] * lon_local, lon_local, axis=1) for d in range(qs)], axis=1
+    )
+    lon_up = lon_down.T
     first, second, third, fourth = units
     wait = stages.after
     arrived, waves = {}, {}
@@ -418,10 +421,8 @@
         for c, part in enumerate(stages.hourly(noise, tables[s])):
             waves[s, c] = part
     arrived[first] = swap_tm(waves[first])
-    arrived[second] = swap_tm(wait(waves[second]))
+    arrived[second] = swap_tm(wait(waves[second], lon_up, lon_down))
     kern = hour_kernel()
-    lon_down = jnp.take(lon, order, axis=1).reshape(lon_count, lon_count)
-    lon_up = lon_down.T
     lat = jnp.take(lat_factor.reshape(qs, lat_rows, lat_count), order, axis=0)
     lat = lat.reshape(lat_count, lat_count)
     lat_t = lat.T
@@ -443,8 +444,10 @@
     def lower(u):
         down[u] = stages.lat_down(u[1], sent[u], lat_t, u[0] == 0, down[first] if u == second else ())
 
+    stages.ease = 1
     up(first)
     middle(first)
+    stages.ease = 4
     arrived[third] = swap_tm(wait(waves[third]))
     up(second)
     lower(first)
@@ -481,7 +484,7 @@
         steps.append(norm_sq / (bending + NOISE_VAR * norm_sq))
     earlier = ()
 
-    stages.ease = BACK_EASE
+    stages.ease = 2
 
     def back(s, start, size, g):
         return swap_lon(stages.lat_up(start, size, g, lat, gains[s]))

time: 749 us -> 748 us (level)
  local copies, waits for them, and re-layouts: 34.5 us -> 25.7 us
    ppermute x91, waiting for transfers between devices: 171 us -> 186 us  [swap_lon(): lax.ppermute(parts[d], 'lon', [(i, i ^ d) for i in range(count)])]
    all_to_all x11, waiting for transfers between devices: 65.4 us -> 51.8 us  [swap_tm(): return lax.all_to_all(x, 'tm', split_axis=0, concat_axis=0, tiled=True)]
    gather x2 -> x0, local copies, waits for them, and re-layouts: 7.69 us -> none  [shards(): lon_down = jnp.take(lon, order, axis=1).reshape(lon_count, lon_count)]
    unnamed x105 -> x110, local copies, waits for them, and re-layouts: 17.9 us -> 20 us
  transfers between devices with their start and end apart: 109 -> 109, of which waited for: 45 -> 45; matrix products, arithmetic and copies ran while one was open for 5% -> 4% of each run, Pallas kernels for 25% -> 26%
where the time goes in v6:
time: 748 us; the launch traced here: 738 us
  waiting for transfers between devices  270 us (36%)
  Pallas kernels  198 us (26%)
  starting transfers between devices  143 us (19%)
  blocking collectives  52.6 us (7%)
  between operations  30.1 us (4%)
  local copies, waits for them, and re-layouts  25.7 us (3%)
  other arithmetic  13.6 us (2%)
    pallas_call x26, Pallas kernels, run(): pl.pallas_call(whole, name=name, grid=(grid,), out_shape=list(out_shape)...  198 us
    ppermute x91, waiting for transfers between devices, swap_lon(): lax.ppermute(parts[d], 'lon', [(i, i ^ d) for i in range(count)])  186 us
    ppermute x91, starting transfers between devices, swap_lon(): lax.ppermute(parts[d], 'lon', [(i, i ^ d) for i in range(count)])  82.1 us
    all_to_all x11, starting transfers between devices, swap_tm(): return lax.all_to_all(x, 'tm', split_axis=0, concat_axis=0, tiled=True)  54.8 us
    all_to_all x1, blocking collectives, swap_tm(): return lax.all_to_all(x, 'tm', split_axis=0, concat_axis=0, tiled=True)  52.6 us
    all_to_all x11, waiting for transfers between devices, swap_tm(): return lax.all_to_all(x, 'tm', split_axis=0, concat_axis=0, tiled=True)  51.8 us
    ppermute x3, waiting for transfers between devices, add_over_tm(): lax.ppermute(x, 'tm', [(i, i ^ d) for i in range(count)])  28.1 us
    unnamed x110, local copies, waits for them, and re-layouts  20 us
  transfers between devices with their start and end apart: 109, of which 45 were waited for; matrix products, arithmetic and copies ran while one was open for 4% of the time, Pallas kernels for 26%

profile of v6, /device:TPU:0, one launch (start us, length us, event | category | flops | bytes accessed | tf_op | source)
XLA Modules:
  0.0 738.1 jit_solution(2130120922063283085)
XLA Ops:
  15.7 11.1 %hourly.2 = (bf16[4,32,64,128]{3,2,1,0:T(8,128)(2,1)}, bf16[4,32,64,128]{3,2,1,0:T(8,128)(2,1)}, f32[8,128]{1,0:T(8,128)S(1)}) custom-call(bf16[2,64,128,512]{3,2,1,0:T(8,128)(2,1)} %refs_0_.3, bf16[2,256,512]{2,1,0:T(8,128)(2,1)S(1)} %get-tuple-element.332.refs_1_), custom_call_target="tpu_custom_call" | custom-call | flops 4294967296 | bytes 20971520 | tf_op jit(solution)/shard_map/hourly/pallas_call | solution.py:94
  39.1 11.3 %hourly.3 = (bf16[4,32,64,128]{3,2,1,0:T(8,128)(2,1)}, bf16[4,32,64,128]{3,2,1,0:T(8,128)(2,1)}, f32[8,128]{1,0:T(8,128)S(1)}) custom-call(bf16[2,64,128,512]{3,2,1,0:T(8,128)(2,1)} %refs_0_.3, bf16[2,256,512]{2,1,0:T(8,128)(2,1)S(1)} %get-tuple-element.333.refs_1_, f32[8,128]{1,0:T(8,128)S(1)} %get-tuple-element.165.refs_2_), custom_call_target="tpu_custom_call" | custom-call | flops 4294967296 | bytes 20971520 | tf_op jit(solution)/shard_map/hourly/pallas_call | solution.py:94
  57.3 24.1 %all-to-all-done.refs_1_ = bf16[4,32,64,128]{3,2,1,0:T(8,128)(2,1)} async-done(((bf16[4,32,64,128]{3,2,1,0:T(8,128)(2,1)}), bf16[4,32,64,128]{3,2,1,0:T(8,128)(2,1)}, u32[]{:S(2)}, u32[]{:S(2)}) %all-to-all-start) | async-done | bytes 2097184 | tf_op jit(solution)/shard_map/all_to_all | solution.py:356
  108.2 12.3 %collective-permute-done.4.refs_6_ = s16[32,32,128]{2,1,0:T(8,128)(2,1)S(1)} collective-permute-done((s16[32,32,128]{2,1,0:T(8,128)(2,1)S(1)}, s16[32,32,128]{2,1,0:T(8,128)(2,1)S(1)}, u32[]{:S(2)}, u32[]{:S(2)}) %collective-permute-start.4) | collective-permute-done | bytes 262176 | tf_op jit(solution)/shard_map/ppermute | solution.py:362
  121.3 14.8 %residual.4 = (f32[32,32,1024]{2,1,0:T(8,128)}, f32[8,128]{1,0:T(8,128)S(1)}, bf16[32,32,128]{2,1,0:T(8,128)(2,1)S(1)}, bf16[32,32,128]{2,1,0:T(8,128)(2,1)}, bf...) custom-call(f32[1]{0:T(128)} %bitcast.8.refs_0_, ...), custom_call_target="tpu_custom_call" | custom-call | flops 8589934592 | bytes 16777216 | tf_op jit(solution)/shard_map/residual/pallas_call | solution.py:94
  159.4 9.8 %collective-permute-done.18.refs_5_ = bf16[32,32,128]{2,1,0:T(8,128)(2,1)S(1)} collective-permute-done((bf16[32,32,128]{2,1,0:T(8,128)(2,1)S(1)}, bf16[32,32,128]{2,1,0:T(8,128)(2,1)S(1)}, u32[]{:S(2)}, u32[]{:S(2)}) %collective-permute-start.18) | collective-permute-done | bytes 262176 | tf_op jit(solution)/shard_map/ppermute | solution.py:362
  182.0 9.6 %all-to-all-done.2.refs_1_ = bf16[4,32,64,128]{3,2,1,0:T(8,128)(2,1)} async-done(((bf16[4,32,64,128]{3,2,1,0:T(8,128)(2,1)}), bf16[4,32,64,128]{3,2,1,0:T(8,128)(2,1)}, u32[]{:S(2)}, u32[]{:S(2)}) %all-to-all-start.2) | async-done | bytes 2097184 | tf_op jit(solution)/shard_map/all_to_all | solution.py:356
  196.8 14.8 %residual.5 = (f32[32,32,1024]{2,1,0:T(8,128)}, f32[8,128]{1,0:T(8,128)S(1)}, bf16[32,32,128]{2,1,0:T(8,128)(2,1)S(1)}, bf16[32,32,128]{2,1,0:T(8,128)(2,1)S(1)}...) custom-call(f32[1]{0:T(128)} %bitcast.8.refs_0_, ...), custom_call_target="tpu_custom_call" | custom-call | flops 34359738368 | bytes 67108864 | tf_op jit(solution)/shard_map/residual/pallas_call | solution.py:94
  272.4 14.8 %residual.6 = (f32[32,32,1024]{2,1,0:T(8,128)}, f32[8,128]{1,0:T(8,128)S(1)}, bf16[32,32,128]{2,1,0:T(8,128)(2,1)S(1)}, bf16[32,32,128]{2,1,0:T(8,128)(2,1)S(1)}...) custom-call(f32[1]{0:T(128)} %bitcast.8.refs_0_, ...), custom_call_target="tpu_custom_call" | custom-call | flops 34359738368 | bytes 67108864 | tf_op jit(solution)/shard_map/residual/pallas_call | solution.py:94
  304.2 10.3 %collective-permute-done.46.refs_5_ = bf16[32,32,128]{2,1,0:T(8,128)(2,1)S(1)} collective-permute-done((bf16[32,32,128]{2,1,0:T(8,128)(2,1)S(1)}, bf16[32,32,128]{2,1,0:T(8,128)(2,1)S(1)}, u32[]{:S(2)}, u32[]{:S(2)}) %collective-permute-start.46) | collective-permute-done | bytes 262176 | tf_op jit(solution)/shard_map/ppermute | solution.py:362
  322.3 9.7 %collective-permute-done.38.refs_5_ = s16[32,32,128]{2,1,0:T(8,128)(2,1)S(1)} collective-permute-done((s16[32,32,128]{2,1,0:T(8,128)(2,1)S(1)}, s16[32,32,128]{2,1,0:T(8,128)(2,1)S(1)}, u32[]{:S(2)}, u32[]{:S(2)}) %collective-permute-start.38) | collective-permute-done | bytes 262176 | tf_op jit(solution)/shard_map/ppermute | solution.py:362
  337.9 14.8 %residual.7 = (f32[32,32,1024]{2,1,0:T(8,128)}, f32[8,128]{1,0:T(8,128)S(1)}, bf16[32,32,128]{2,1,0:T(8,128)(2,1)S(1)}, bf16[32,32,128]{2,1,0:T(8,128)(2,1)S(1)}...) custom-call(f32[1]{0:T(128)} %bitcast.8.refs_0_, ...), custom_call_target="tpu_custom_call" | custom-call | flops 34359738368 | bytes 67108864 | tf_op jit(solution)/shard_map/residual/pallas_call | solution.py:94
  377.5 13.1 %collective-permute-done.53.refs_5_ = bf16[32,32,128]{2,1,0:T(8,128)(2,1)S(1)} collective-permute-done((bf16[32,32,128]{2,1,0:T(8,128)(2,1)S(1)}, bf16[32,32,128]{2,1,0:T(8,128)(2,1)S(1)}, u32[]{:S(2)}, u32[]{:S(2)}) %collective-permute-start.53) | collective-permute-done | bytes 262176 | tf_op jit(solution)/shard_map/ppermute | solution.py:362
  395.1 12.2 %all-to-all-done.5.refs_0_ = bf16[4,64,32,128]{3,2,1,0:T(8,128)(2,1)} async-done(((bf16[4,64,32,128]{3,2,1,0:T(8,128)(2,1)}), bf16[4,64,32,128]{3,2,1,0:T(8,128)(2,1)}, u32[]{:S(2)}, u32[]{:S(2)}) %all-to-all-start.5) | async-done | bytes 2097184 | tf_op jit(solution)/shard_map/all_to_all | solution.py:356
  407.3 52.6 %all_to_all.60.refs_1_ = bf16[4,64,32,128]{3,2,1,0:T(8,128)(2,1)} all-to-all(bf16[4,64,32,128]{3,2,1,0:T(8,128)(2,1)} %get-tuple-element.254), channel_id=1, replica_groups=mesh['tm'=4,'lon'=8] {'tm'}, dimensions={0} | all-to-all | bytes 4194304 | tf_op jit(solution)/shard_map/all_to_all | solution.py:356
  483.7 28.1 %collective-permute-done.57 = f32[4,128]{1,0:T(4,128)S(1)} collective-permute-done((f32[4,128]{1,0:T(4,128)S(1)}, f32[4,128]{1,0:T(4,128)S(1)}, u32[]{:S(2)}, u32[]{:S(2)}) %collective-permute-start.57) | collective-permute-done | bytes 2080 | tf_op jit(solution)/shard_map/ppermute | solution.py:367
  545.0 12.6 %collective-permute-done.66.refs_6_ = s16[32,32,128]{2,1,0:T(8,128)(2,1)S(1)} collective-permute-done((s16[32,32,128]{2,1,0:T(8,128)(2,1)S(1)}, s16[32,32,128]{2,1,0:T(8,128)(2,1)S(1)}, u32[]{:S(2)}, u32[]{:S(2)}) %collective-permute-start.66) | collective-permute-done | bytes 262176 | tf_op jit(solution)/shard_map/ppermute | solution.py:362
  558.3 11.9 %finish.5 = (f32[2,64,32,1024]{3,2,1,0:T(8,128)}, f32[2,64,32,1024]{3,2,1,0:T(8,128)}, f32[8,128]{1,0:T(8,128)S(1)}) custom-call(f32[2]{0:T(128)S(1)} %pad_maximum_fusion.5.refs_0_, s16[32,32,128]{2,1,0:T(8,128)(2,1)S(1)} %get-tuple-element.261.refs_1_, s16[32,32,128]{2,1,0:T(8,128)(2,1)S(1)} %collective-permute-done.62.refs_2_, ...), custom_call_target="tpu_custom_call" | custom-call | flops 8589934592 | bytes 46137344 | tf_op jit(solution)/shard_map/finish/pallas_call | solution.py:94
  594.3 13.3 %collective-permute-done.73.refs_6_ = s16[32,32,128]{2,1,0:T(8,128)(2,1)S(1)} collective-permute-done((s16[32,32,128]{2,1,0:T(8,128)(2,1)S(1)}, s16[32,32,128]{2,1,0:T(8,128)(2,1)S(1)}, u32[]{:S(2)}, u32[]{:S(2)}) %collective-permute-start.73) | collective-permute-done | bytes 262176 | tf_op jit(solution)/shard_map/ppermute | solution.py:362
  608.2 11.9 %finish.6 = (f32[2,64,32,1024]{3,2,1,0:T(8,128)}, f32[2,64,32,1024]{3,2,1,0:T(8,128)}, f32[8,128]{1,0:T(8,128)S(1)}) custom-call(f32[2]{0:T(128)S(1)} %pad_maximum_fusion.5.refs_0_, s16[32,32,128]{2,1,0:T(8,128)(2,1)S(1)} %get-tuple-element.273.refs_1_, ...), custom_call_target="tpu_custom_call", output_to_operand_aliasing={{0}: (13, {}), {1}: (14, {})} | custom-call | flops 8589934592 | bytes 46137344 | tf_op jit(solution)/shard_map/finish/pallas_call | solution.py:94
  648.2 12.6 %collective-permute-done.80.refs_6_ = s16[32,32,128]{2,1,0:T(8,128)(2,1)S(1)} collective-permute-done((s16[32,32,128]{2,1,0:T(8,128)(2,1)S(1)}, s16[32,32,128]{2,1,0:T(8,128)(2,1)S(1)}, u32[]{:S(2)}, u32[]{:S(2)}) %collective-permute-start.80) | collective-permute-done | bytes 262176 | tf_op jit(solution)/shard_map/ppermute | solution.py:362
  661.5 11.9 %finish.7 = (f32[2,64,32,1024]{3,2,1,0:T(8,128)}, f32[2,64,32,1024]{3,2,1,0:T(8,128)}, f32[8,128]{1,0:T(8,128)S(1)}) custom-call(f32[2]{0:T(128)S(1)} %pad_maximum_fusion.4.refs_0_, s16[32,32,128]{2,1,0:T(8,128)(2,1)S(1)} %get-tuple-element.286.refs_1_, ...), custom_call_target="tpu_custom_call", output_to_operand_aliasing={{0}: (13, {}), {1}: (14, {})} | custom-call | flops 8589934592 | bytes 46137344 | tf_op jit(solution)/shard_map/finish/pallas_call | solution.py:94
  696.8 7.2 finish.8
  723.9 7.2 finish.9
  (380 shorter events, 356.2 us)
Async XLA Ops:
  7.2 43.2 %all-gather.2.cloned.1.call-start = ((), (), s32[]{:S(2)}) async-start(), calls=%async_computation.12 | async-start | bytes 2359296 | tf_op jit(solution)/shard_map/all_gather | solution.py:411
  26.8 54.6 %all-to-all-start = ((bf16[4,32,64,128]{3,2,1,0:T(8,128)(2,1)}), bf16[4,32,64,128]{3,2,1,0:T(8,128)(2,1)}, u32[]{:S(2)}, u32[]{:S(2)}) async-start(bf16[4,32,64,128]{3,2,1,0:T(8,128)(2,1)} %get-tuple-element.164), calls=%async_computation | async-start | bytes 4194304 | tf_op jit(solution)/shard_map/all_to_all | solution.py:356
  81.4 55.4 %all-to-all-start.1 = ((bf16[4,32,64,128]{3,2,1,0:T(8,128)(2,1)}), bf16[4,32,64,128]{3,2,1,0:T(8,128)(2,1)}, u32[]{:S(2)}, u32[]{:S(2)}) async-start(bf16[4,32,64,128]{3,2,1,0:T(8,128)(2,1)} %after.9), calls=%async_computation.1 | async-start | bytes 4194304 | tf_op jit(solution)/shard_map/all_to_all | solution.py:356
  136.8 54.8 %all-to-all-start.2 = ((bf16[4,32,64,128]{3,2,1,0:T(8,128)(2,1)}), bf16[4,32,64,128]{3,2,1,0:T(8,128)(2,1)}, u32[]{:S(2)}, u32[]{:S(2)}) async-start(bf16[4,32,64,128]{3,2,1,0:T(8,128)(2,1)} %after.10), calls=%async_computation.2 | async-start | bytes 4194304 | tf_op jit(solution)/shard_map/all_to_all | solution.py:356
  169.1 26.9 %collective-permute-start.9 = (s16[32,32,128]{2,1,0:T(8,128)(2,1)S(1)}, s16[32,32,128]{2,1,0:T(8,128)(2,1)S(1)}, u32[]{:S(2)}, u32[]{:S(2)}) collective-permute-start(s16[32,32,128]{2,1,0:T(8,128)(2,1)S(1)} %get-tuple-element.182), channel_id=1, source_target_pairs={{0,3},{1,2},{2,1},{3,0},{4,7},{5,6},{6,5},{7,4},{8,11},{9,10},{10,... | collective-permute-start | bytes 786440 | tf_op jit(solution)/shard_map/ppermute | solution.py:362
  191.6 62.5 %all-to-all-start.3 = ((bf16[4,32,64,128]{3,2,1,0:T(8,128)(2,1)}), bf16[4,32,64,128]{3,2,1,0:T(8,128)(2,1)}, u32[]{:S(2)}, u32[]{:S(2)}) async-start(bf16[4,32,64,128]{3,2,1,0:T(8,128)(2,1)} %after.11), calls=%async_computation.3 | async-start | bytes 4194304 | tf_op jit(solution)/shard_map/all_to_all | solution.py:356
  236.6 28.3 %collective-permute-start.23 = (s16[32,32,128]{2,1,0:T(8,128)(2,1)S(1)}, s16[32,32,128]{2,1,0:T(8,128)(2,1)S(1)}, u32[]{:S(2)}, u32[]{:S(2)}) collective-permute-start(s16[32,32,128]{2,1,0:T(8,128)(2,1)S(1)} %get-tuple-element.203), channel_id=1, source_target_pairs={{0,3},{1,2},{2,1},{3,0},{4,7},{5,6},{6,5},{7,4},{8,11},{9,10},{10,... | collective-permute-start | bytes 786440 | tf_op jit(solution)/shard_map/ppermute | solution.py:362
  238.7 26.2 %collective-permute-start.24 = (s16[32,32,128]{2,1,0:T(8,128)(2,1)S(1)}, s16[32,32,128]{2,1,0:T(8,128)(2,1)S(1)}, u32[]{:S(2)}, u32[]{:S(2)}) collective-permute-start(s16[32,32,128]{2,1,0:T(8,128)(2,1)S(1)} %get-tuple-element.204), channel_id=1, source_target_pairs={{0,4},{1,5},{2,6},{3,7},{4,0},{5,1},{6,2},{7,3},{8,12},{9,13},{10,... | collective-permute-start | bytes 786440 | tf_op jit(solution)/shard_map/ppermute | solution.py:362
  240.2 31.3 %collective-permute-start.25 = (s16[32,32,128]{2,1,0:T(8,128)(2,1)S(1)}, s16[32,32,128]{2,1,0:T(8,128)(2,1)S(1)}, u32[]{:S(2)}, u32[]{:S(2)}) collective-permute-start(s16[32,32,128]{2,1,0:T(8,128)(2,1)S(1)} %get-tuple-element.205), channel_id=1, source_target_pairs={{0,5},{1,4},{2,7},{3,6},{4,1},{5,0},{6,3},{7,2},{8,13},{9,12},{10,... | collective-permute-start | bytes 786440 | tf_op jit(solution)/shard_map/ppermute | solution.py:362
  244.0 27.5 %collective-permute-start.26 = (s16[32,32,128]{2,1,0:T(8,128)(2,1)S(1)}, s16[32,32,128]{2,1,0:T(8,128)(2,1)S(1)}, u32[]{:S(2)}, u32[]{:S(2)}) collective-permute-start(s16[32,32,128]{2,1,0:T(8,128)(2,1)S(1)} %get-tuple-element.206), channel_id=1, source_target_pairs={{0,6},{1,7},{2,4},{3,5},{4,2},{5,3},{6,0},{7,1},{8,14},{9,15},{10,... | collective-permute-start | bytes 786440 | tf_op jit(solution)/shard_map/ppermute | solution.py:362
  254.1 99.0 %all-to-all-start.4 = ((bf16[4,64,64,128]{3,2,1,0:T(8,128)(2,1)}), bf16[4,64,64,128]{3,2,1,0:T(8,128)(2,1)}, u32[]{:S(2)}, u32[]{:S(2)}) async-start(bf16[4,64,64,128]{3,2,1,0:T(8,128)(2,1)} %after.12), calls=%async_computation.4 | async-start | bytes 8388608 | tf_op jit(solution)/shard_map/all_to_all | solution.py:356
  264.9 24.8 %collective-permute-start.36 = (s16[32,32,128]{2,1,0:T(8,128)(2,1)S(1)}, s16[32,32,128]{2,1,0:T(8,128)(2,1)S(1)}, u32[]{:S(2)}, u32[]{:S(2)}) collective-permute-start(s16[32,32,128]{2,1,0:T(8,128)(2,1)S(1)} %get-tuple-element.224), channel_id=1, source_target_pairs={{0,2},{1,3},{2,0},{3,1},{4,6},{5,7},{6,4},{7,5},{8,10},{9,11},{10,... | collective-permute-start | bytes 786440 | tf_op jit(solution)/shard_map/ppermute | solution.py:362
  289.7 24.8 %collective-permute-start.46 = (bf16[32,32,128]{2,1,0:T(8,128)(2,1)S(1)}, bf16[32,32,128]{2,1,0:T(8,128)(2,1)S(1)}, u32[]{:S(2)}, u32[]{:S(2)}) collective-permute-start(bf16[32,32,128]{2,1,0:T(8,128)(2,1)S(1)} %get-tuple-element.235), channel_id=1, source_target_pairs={{0,5},{1,4},{2,7},{3,6},{4,1},{5,0},{6,3},{7,2},{8,13},{9,12},{10,... | collective-permute-start | bytes 786440 | tf_op jit(solution)/shard_map/ppermute | solution.py:362
  303.7 28.3 %collective-permute-start.38 = (s16[32,32,128]{2,1,0:T(8,128)(2,1)S(1)}, s16[32,32,128]{2,1,0:T(8,128)(2,1)S(1)}, u32[]{:S(2)}, u32[]{:S(2)}) collective-permute-start(s16[32,32,128]{2,1,0:T(8,128)(2,1)S(1)} %get-tuple-element.226), channel_id=1, source_target_pairs={{0,4},{1,5},{2,6},{3,7},{4,0},{5,1},{6,2},{7,3},{8,12},{9,13},{10,... | collective-permute-start | bytes 786440 | tf_op jit(solution)/shard_map/ppermute | solution.py:362
  353.1 54.1 %all-to-all-start.5 = ((bf16[4,64,32,128]{3,2,1,0:T(8,128)(2,1)}), bf16[4,64,32,128]{3,2,1,0:T(8,128)(2,1)}, u32[]{:S(2)}, u32[]{:S(2)}) async-start(bf16[4,64,32,128]{3,2,1,0:T(8,128)(2,1)} %after.13), calls=%async_computation.5 | async-start | bytes 4194304 | tf_op jit(solution)/shard_map/all_to_all | solution.py:356
  459.9 52.0 %all-to-all-start.7 = ((bf16[4,32,64,128]{3,2,1,0:T(8,128)(2,1)}), bf16[4,32,64,128]{3,2,1,0:T(8,128)(2,1)}, u32[]{:S(2)}, u32[]{:S(2)}) async-start(bf16[4,32,64,128]{3,2,1,0:T(8,128)(2,1)} %get-tuple-element.259), calls=%async_computation.7 | async-start | bytes 4194304 | tf_op jit(solution)/shard_map/all_to_all | solution.py:356
  479.4 32.5 %collective-permute-start.57 = (f32[4,128]{1,0:T(4,128)S(1)}, f32[4,128]{1,0:T(4,128)S(1)}, u32[]{:S(2)}, u32[]{:S(2)}) collective-permute-start(f32[4,128]{1,0:T(4,128)S(1)} %broadcast_in_dim.30), channel_id=1, source_target_pairs={{0,16},{8,24},{16,0},{24,8},{1,17},{9,25},{17,1},{25,9},{2,18},{10... | collective-permute-start | bytes 6152 | tf_op jit(solution)/shard_map/ppermute | solution.py:367
  482.3 29.6 %collective-permute-start.58 = (f32[4,128]{1,0:T(4,128)S(1)}, f32[4,128]{1,0:T(4,128)S(1)}, u32[]{:S(2)}, u32[]{:S(2)}) collective-permute-start(f32[4,128]{1,0:T(4,128)S(1)} %broadcast_in_dim.30), channel_id=1, source_target_pairs={{0,24},{8,16},{16,8},{24,0},{1,25},{9,17},{17,9},{25,1},{2,26},{10... | collective-permute-start | bytes 6152 | tf_op jit(solution)/shard_map/ppermute | solution.py:367
  483.7 28.1 %collective-permute-start.56 = (f32[4,128]{1,0:T(4,128)S(1)}, f32[4,128]{1,0:T(4,128)S(1)}, u32[]{:S(2)}, u32[]{:S(2)}) collective-permute-start(f32[4,128]{1,0:T(4,128)S(1)} %broadcast_in_dim.30), channel_id=1, source_target_pairs={{0,8},{8,0},{16,24},{24,16},{1,9},{9,1},{17,25},{25,17},{2,10},{10... | collective-permute-start | bytes 6152 | tf_op jit(solution)/shard_map/ppermute | solution.py:367
  511.9 58.3 %all-to-all-start.9 = ((bf16[4,32,64,128]{3,2,1,0:T(8,128)(2,1)}), bf16[4,32,64,128]{3,2,1,0:T(8,128)(2,1)}, u32[]{:S(2)}, u32[]{:S(2)}) async-start(bf16[4,32,64,128]{3,2,1,0:T(8,128)(2,1)} %after.15), calls=%async_computation.9 | async-start | bytes 4194304 | tf_op jit(solution)/shard_map/all_to_all | solution.py:356
  570.2 54.3 %all-to-all-start.8 = ((bf16[4,32,64,128]{3,2,1,0:T(8,128)(2,1)}), bf16[4,32,64,128]{3,2,1,0:T(8,128)(2,1)S(1)}, u32[]{:S(2)}, u32[]{:S(2)}) async-start(bf16[4,32,64,128]{3,2,1,0:T(8,128)(2,1)} %after.14), calls=%async_computation.8 | async-start | bytes 4194304 | tf_op jit(solution)/shard_map/all_to_all | solution.py:356
  582.4 25.1 %collective-permute-start.73 = (s16[32,32,128]{2,1,0:T(8,128)(2,1)S(1)}, s16[32,32,128]{2,1,0:T(8,128)(2,1)S(1)}, u32[]{:S(2)}, u32[]{:S(2)}) collective-permute-start(s16[32,32,128]{2,1,0:T(8,128)(2,1)S(1)} %get-tuple-element.278), channel_id=1, source_target_pairs={{0,5},{1,4},{2,7},{3,6},{4,1},{5,0},{6,3},{7,2},{8,13},{9,12},{10,... | collective-permute-start | bytes 786440 | tf_op jit(solution)/shard_map/ppermute | solution.py:362
  624.5 48.9 %all-to-all-start.11 = ((bf16[4,16,64,128]{3,2,1,0:T(8,128)(2,1)}), bf16[4,16,64,128]{3,2,1,0:T(8,128)(2,1)}, u32[]{:S(2)}, u32[]{:S(2)}) async-start(bf16[4,16,64,128]{3,2,1,0:T(8,128)(2,1)} %after.17), calls=%async_computation.11 | async-start | bytes 2097152 | tf_op jit(solution)/shard_map/all_to_all | solution.py:356
  673.4 31.6 %all-to-all-start.10 = ((bf16[4,16,64,128]{3,2,1,0:T(8,128)(2,1)}), bf16[4,16,64,128]{3,2,1,0:T(8,128)(2,1)S(1)}, u32[]{:S(2)}, u32[]{:S(2)}) async-start(bf16[4,16,64,128]{3,2,1,0:T(8,128)(2,1)} %after.16), calls=%async_computation.10 | async-start | bytes 2097152 | tf_op jit(solution)/shard_map/all_to_all | solution.py:356
  (135 other events, 1582.3 us)
Sparse Core Ops, SparseCore 0:
  9.9 30.8 all-gather.1

commit v7 on v6

--- a/solution.py
+++ b/solution.py
@@ -495,19 +495,20 @@
             s, start, size, codes, 1.0 / gains[s], steps[s], lon_up, prior, observed, mask, earlier
         )
 
-    codes = back(0, 0, hour_part, early[0])
-    earlier = end(0, 0, hour_part, codes)
-    late[0] = swap_tm(wait(late[0]))
-    codes = back(0, 0, hour_part, early[1])
-    earlier = end(0, hour_part, hour_part, codes)
-    late[1] = swap_tm(wait(late[1]))
-    codes = back(1, 0, hour_part, late[0])
-    earlier = end(1, *pieces[0], codes)
-    late[2] = swap_tm(wait(late[2]))
-    codes = back(1, 0, pieces[1][1], late[1])
-    earlier = end(1, *pieces[1], codes)
-    codes = back(1, 0, pieces[2][1], late[2])
-    earlier = end(1, *pieces[2], codes)
+    quarters = pieces[1:]
+    first_codes = back(0, 0, hour_part, early[0])
+    late[0] = swap_tm(wait(late[0], *first_codes[1:]))
+    second_codes = back(0, 0, hour_part, early[1])
+    earlier = end(0, 0, hour_part, first_codes)
+    late[1] = swap_tm(wait(late[1], *second_codes[1:]))
+    third_codes = back(1, 0, hour_part, late[0])
+    earlier = end(0, hour_part, hour_part, second_codes)
+    late[2] = swap_tm(wait(late[2], *third_codes[1:5]))
+    fourth_codes = back(1, 0, quarters[0][1], late[1])
+    earlier = end(1, *pieces[0], third_codes)
+    fifth_codes = back(1, 0, quarters[1][1], late[2])
+    earlier = end(1, *quarters[0], fourth_codes)
+    earlier = end(1, *quarters[1], fifth_codes)
     return stages.joined(earlier)
 
 

time: 748 us -> 736 us (0.984)
  waiting for transfers between devices: 270 us -> 249 us
  starting transfers between devices: 143 us -> 154 us
    ppermute x91, waiting for transfers between devices: 186 us -> 147 us  [swap_lon(): lax.ppermute(parts[d], 'lon', [(i, i ^ d) for i in range(count)])]
    all_to_all x11, waiting for transfers between devices: 51.8 us -> 70.7 us  [swap_tm(): return lax.all_to_all(x, 'tm', split_axis=0, concat_axis=0, tiled=True)]
    all_to_all x11, starting transfers between devices: 54.8 us -> 63.3 us  [swap_tm(): return lax.all_to_all(x, 'tm', split_axis=0, concat_axis=0, tiled=True)]
    unnamed x110 -> x122, local copies, waits for them, and re-layouts: 20 us -> 22 us
  transfers between devices with their start and end apart: 109 -> 109, of which waited for: 45 -> 37; matrix products, arithmetic and copies ran while one was open for 4% -> 4% of each run, Pallas kernels for 26% -> 26%
where the time goes in v7:
time: 736 us; the launch traced here: 731 us
  waiting for transfers between devices  249 us (34%)
  Pallas kernels  198 us (27%)
  starting transfers between devices  154 us (21%)
  blocking collectives  52.5 us (7%)
  between operations  30 us (4%)
  local copies, waits for them, and re-layouts  27.7 us (4%)
  other arithmetic  13.5 us (2%)
    pallas_call x26, Pallas kernels, run(): pl.pallas_call(whole, name=name, grid=(grid,), out_shape=list(out_shape)...  198 us
    ppermute x91, waiting for transfers between devices, swap_lon(): lax.ppermute(parts[d], 'lon', [(i, i ^ d) for i in range(count)])  147 us
    ppermute x91, starting transfers between devices, swap_lon(): lax.ppermute(parts[d], 'lon', [(i, i ^ d) for i in range(count)])  85 us
    all_to_all x11, waiting for transfers between devices, swap_tm(): return lax.all_to_all(x, 'tm', split_axis=0, concat_axis=0, tiled=True)  70.7 us
    all_to_all x11, starting transfers between devices, swap_tm(): return lax.all_to_all(x, 'tm', split_axis=0, concat_axis=0, tiled=True)  63.3 us
    all_to_all x1, blocking collectives, swap_tm(): return lax.all_to_all(x, 'tm', split_axis=0, concat_axis=0, tiled=True)  52.5 us
    ppermute x3, waiting for transfers between devices, add_over_tm(): lax.ppermute(x, 'tm', [(i, i ^ d) for i in range(count)])  27.4 us
    unnamed x122, local copies, waits for them, and re-layouts  22 us
  transfers between devices with their start and end apart: 109, of which 37 were waited for; matrix products, arithmetic and copies ran while one was open for 4% of the time, Pallas kernels for 26%

profile of v7, /device:TPU:0, one launch (start us, length us, event | category | flops | bytes accessed | tf_op | source)
XLA Modules:
  0.0 730.9 jit_solution(2696637076715167985)
XLA Ops:
  15.7 11.1 %hourly.2 = (bf16[4,32,64,128]{3,2,1,0:T(8,128)(2,1)}, bf16[4,32,64,128]{3,2,1,0:T(8,128)(2,1)}, f32[8,128]{1,0:T(8,128)S(1)}) custom-call(bf16[2,64,128,512]{3,2,1,0:T(8,128)(2,1)} %refs_0_.3, bf16[2,256,512]{2,1,0:T(8,128)(2,1)S(1)} %get-tuple-element.332.refs_1_), custom_call_target="tpu_custom_call" | custom-call | flops 4294967296 | bytes 20971520 | tf_op jit(solution)/shard_map/hourly/pallas_call | solution.py:94
  39.0 11.3 %hourly.3 = (bf16[4,32,64,128]{3,2,1,0:T(8,128)(2,1)}, bf16[4,32,64,128]{3,2,1,0:T(8,128)(2,1)}, f32[8,128]{1,0:T(8,128)S(1)}) custom-call(bf16[2,64,128,512]{3,2,1,0:T(8,128)(2,1)} %refs_0_.3, bf16[2,256,512]{2,1,0:T(8,128)(2,1)S(1)} %get-tuple-element.333.refs_1_, f32[8,128]{1,0:T(8,128)S(1)} %get-tuple-element.165.refs_2_), custom_call_target="tpu_custom_call" | custom-call | flops 4294967296 | bytes 20971520 | tf_op jit(solution)/shard_map/hourly/pallas_call | solution.py:94
  57.2 24.2 %all-to-all-done.refs_1_ = bf16[4,32,64,128]{3,2,1,0:T(8,128)(2,1)} async-done(((bf16[4,32,64,128]{3,2,1,0:T(8,128)(2,1)}), bf16[4,32,64,128]{3,2,1,0:T(8,128)(2,1)}, u32[]{:S(2)}, u32[]{:S(2)}) %all-to-all-start) | async-done | bytes 2097184 | tf_op jit(solution)/shard_map/all_to_all | solution.py:356
  108.2 12.3 %collective-permute-done.4.refs_6_ = s16[32,32,128]{2,1,0:T(8,128)(2,1)S(1)} collective-permute-done((s16[32,32,128]{2,1,0:T(8,128)(2,1)S(1)}, s16[32,32,128]{2,1,0:T(8,128)(2,1)S(1)}, u32[]{:S(2)}, u32[]{:S(2)}) %collective-permute-start.4) | collective-permute-done | bytes 262176 | tf_op jit(solution)/shard_map/ppermute | solution.py:362
  121.3 14.8 %residual.4 = (f32[32,32,1024]{2,1,0:T(8,128)}, f32[8,128]{1,0:T(8,128)S(1)}, bf16[32,32,128]{2,1,0:T(8,128)(2,1)S(1)}, bf16[32,32,128]{2,1,0:T(8,128)(2,1)}, bf...) custom-call(f32[1]{0:T(128)} %bitcast.8.refs_0_, ...), custom_call_target="tpu_custom_call" | custom-call | flops 8589934592 | bytes 16777216 | tf_op jit(solution)/shard_map/residual/pallas_call | solution.py:94
  136.8 15.4 %all-to-all-start.2 = ((bf16[4,32,64,128]{3,2,1,0:T(8,128)(2,1)}), bf16[4,32,64,128]{3,2,1,0:T(8,128)(2,1)}, u32[]{:S(2)}, u32[]{:S(2)}) async-start(bf16[4,32,64,128]{3,2,1,0:T(8,128)(2,1)} %after.10), calls=%async_computation.2 | async-start | bytes 4194304 | tf_op jit(solution)/shard_map/all_to_all | solution.py:356
  169.6 9.8 %collective-permute-done.18.refs_5_ = bf16[32,32,128]{2,1,0:T(8,128)(2,1)S(1)} collective-permute-done((bf16[32,32,128]{2,1,0:T(8,128)(2,1)S(1)}, bf16[32,32,128]{2,1,0:T(8,128)(2,1)S(1)}, u32[]{:S(2)}, u32[]{:S(2)}) %collective-permute-start.18) | collective-permute-done | bytes 262176 | tf_op jit(solution)/shard_map/ppermute | solution.py:362
  192.2 9.6 %all-to-all-done.2.refs_1_ = bf16[4,32,64,128]{3,2,1,0:T(8,128)(2,1)} async-done(((bf16[4,32,64,128]{3,2,1,0:T(8,128)(2,1)}), bf16[4,32,64,128]{3,2,1,0:T(8,128)(2,1)}, u32[]{:S(2)}, u32[]{:S(2)}) %all-to-all-start.2) | async-done | bytes 2097184 | tf_op jit(solution)/shard_map/all_to_all | solution.py:356
  207.0 14.8 %residual.5 = (f32[32,32,1024]{2,1,0:T(8,128)}, f32[8,128]{1,0:T(8,128)S(1)}, bf16[32,32,128]{2,1,0:T(8,128)(2,1)S(1)}, bf16[32,32,128]{2,1,0:T(8,128)(2,1)S(1)}...) custom-call(f32[1]{0:T(128)} %bitcast.8.refs_0_, ...), custom_call_target="tpu_custom_call" | custom-call | flops 34359738368 | bytes 67108864 | tf_op jit(solution)/shard_map/residual/pallas_call | solution.py:94
  283.0 14.8 %residual.6 = (f32[32,32,1024]{2,1,0:T(8,128)}, f32[8,128]{1,0:T(8,128)S(1)}, bf16[32,32,128]{2,1,0:T(8,128)(2,1)S(1)}, bf16[32,32,128]{2,1,0:T(8,128)(2,1)S(1)}...) custom-call(f32[1]{0:T(128)} %bitcast.8.refs_0_, ...), custom_call_target="tpu_custom_call" | custom-call | flops 34359738368 | bytes 67108864 | tf_op jit(solution)/shard_map/residual/pallas_call | solution.py:94
  314.5 10.5 %collective-permute-done.46.refs_5_ = bf16[32,32,128]{2,1,0:T(8,128)(2,1)S(1)} collective-permute-done((bf16[32,32,128]{2,1,0:T(8,128)(2,1)S(1)}, bf16[32,32,128]{2,1,0:T(8,128)(2,1)S(1)}, u32[]{:S(2)}, u32[]{:S(2)}) %collective-permute-start.46) | collective-permute-done | bytes 262176 | tf_op jit(solution)/shard_map/ppermute | solution.py:362
  332.8 9.7 %collective-permute-done.38.refs_5_ = s16[32,32,128]{2,1,0:T(8,128)(2,1)S(1)} collective-permute-done((s16[32,32,128]{2,1,0:T(8,128)(2,1)S(1)}, s16[32,32,128]{2,1,0:T(8,128)(2,1)S(1)}, u32[]{:S(2)}, u32[]{:S(2)}) %collective-permute-start.38) | collective-permute-done | bytes 262176 | tf_op jit(solution)/shard_map/ppermute | solution.py:362
  348.4 14.8 %residual.7 = (f32[32,32,1024]{2,1,0:T(8,128)}, f32[8,128]{1,0:T(8,128)S(1)}, bf16[32,32,128]{2,1,0:T(8,128)(2,1)S(1)}, bf16[32,32,128]{2,1,0:T(8,128)(2,1)S(1)}...) custom-call(f32[1]{0:T(128)} %bitcast.8.refs_0_, ...), custom_call_target="tpu_custom_call" | custom-call | flops 34359738368 | bytes 67108864 | tf_op jit(solution)/shard_map/residual/pallas_call | solution.py:94
  387.9 13.2 %collective-permute-done.53.refs_5_ = bf16[32,32,128]{2,1,0:T(8,128)(2,1)S(1)} collective-permute-done((bf16[32,32,128]{2,1,0:T(8,128)(2,1)S(1)}, bf16[32,32,128]{2,1,0:T(8,128)(2,1)S(1)}, u32[]{:S(2)}, u32[]{:S(2)}) %collective-permute-start.53) | collective-permute-done | bytes 262176 | tf_op jit(solution)/shard_map/ppermute | solution.py:362
  405.6 12.2 %all-to-all-done.5.refs_0_ = bf16[4,64,32,128]{3,2,1,0:T(8,128)(2,1)} async-done(((bf16[4,64,32,128]{3,2,1,0:T(8,128)(2,1)}), bf16[4,64,32,128]{3,2,1,0:T(8,128)(2,1)}, u32[]{:S(2)}, u32[]{:S(2)}) %all-to-all-start.5) | async-done | bytes 2097184 | tf_op jit(solution)/shard_map/all_to_all | solution.py:356
  417.7 52.5 %all_to_all.60.refs_1_ = bf16[4,64,32,128]{3,2,1,0:T(8,128)(2,1)} all-to-all(bf16[4,64,32,128]{3,2,1,0:T(8,128)(2,1)} %get-tuple-element.254), channel_id=1, replica_groups=mesh['tm'=4,'lon'=8] {'tm'}, dimensions={0} | all-to-all | bytes 4194304 | tf_op jit(solution)/shard_map/all_to_all | solution.py:356
  494.7 27.4 %collective-permute-done.57 = f32[4,128]{1,0:T(4,128)S(1)} collective-permute-done((f32[4,128]{1,0:T(4,128)S(1)}, f32[4,128]{1,0:T(4,128)S(1)}, u32[]{:S(2)}, u32[]{:S(2)}) %collective-permute-start.57) | collective-permute-done | bytes 2080 | tf_op jit(solution)/shard_map/ppermute | solution.py:367
  555.9 12.6 %collective-permute-done.73.refs_6_ = s16[32,32,128]{2,1,0:T(8,128)(2,1)S(1)} collective-permute-done((s16[32,32,128]{2,1,0:T(8,128)(2,1)S(1)}, s16[32,32,128]{2,1,0:T(8,128)(2,1)S(1)}, u32[]{:S(2)}, u32[]{:S(2)}) %collective-permute-start.73) | collective-permute-done | bytes 262176 | tf_op jit(solution)/shard_map/ppermute | solution.py:362
  595.2 11.9 %finish.5 = (f32[2,64,32,1024]{3,2,1,0:T(8,128)}, f32[2,64,32,1024]{3,2,1,0:T(8,128)}, f32[8,128]{1,0:T(8,128)S(1)}) custom-call(f32[2]{0:T(128)S(1)} %pad_maximum_fusion.5.refs_0_, s16[32,32,128]{2,1,0:T(8,128)(2,1)S(1)} %copy-done.13, s16[32,32,128]{2,1,0:T(8,128)(2,1)S(1)} %collective-permute-done.69.refs_2_, ...), custom_call_target="tpu_custom_call" | custom-call | flops 8589934592 | bytes 46137344 | tf_op jit(solution)/shard_map/finish/pallas_call | solution.py:94
  612.8 14.1 %all-to-all-done.9.refs_1_ = bf16[4,32,64,128]{3,2,1,0:T(8,128)(2,1)} async-done(((bf16[4,32,64,128]{3,2,1,0:T(8,128)(2,1)}), bf16[4,32,64,128]{3,2,1,0:T(8,128)(2,1)}, u32[]{:S(2)}, u32[]{:S(2)}) %all-to-all-start.9) | async-done | bytes 2097184 | tf_op jit(solution)/shard_map/all_to_all | solution.py:356
  639.3 11.9 %finish.6 = (f32[2,64,32,1024]{3,2,1,0:T(8,128)}, f32[2,64,32,1024]{3,2,1,0:T(8,128)}, f32[8,128]{1,0:T(8,128)S(1)}) custom-call(f32[2]{0:T(128)S(1)} %pad_maximum_fusion.5.refs_0_, s16[32,32,128]{2,1,0:T(8,128)(2,1)S(1)} %get-tuple-element.262.refs_1_, ...), custom_call_target="tpu_custom_call", output_to_operand_aliasing={{0}: (13, {}), {1}: (14, {})} | custom-call | flops 8589934592 | bytes 46137344 | tf_op jit(solution)/shard_map/finish/pallas_call | solution.py:94
  670.3 9.6 %collective-permute-done.80.refs_6_ = s16[32,32,128]{2,1,0:T(8,128)(2,1)S(1)} collective-permute-done((s16[32,32,128]{2,1,0:T(8,128)(2,1)S(1)}, s16[32,32,128]{2,1,0:T(8,128)(2,1)S(1)}, u32[]{:S(2)}, u32[]{:S(2)}) %collective-permute-start.80) | collective-permute-done | bytes 262176 | tf_op jit(solution)/shard_map/ppermute | solution.py:362
  682.9 11.9 %finish.7 = (f32[2,64,32,1024]{3,2,1,0:T(8,128)}, f32[2,64,32,1024]{3,2,1,0:T(8,128)}, f32[8,128]{1,0:T(8,128)S(1)}) custom-call(f32[2]{0:T(128)S(1)} %pad_maximum_fusion.4.refs_0_, s16[32,32,128]{2,1,0:T(8,128)(2,1)S(1)} %get-tuple-element.291.refs_1_, ...), custom_call_target="tpu_custom_call", output_to_operand_aliasing={{0}: (13, {}), {1}: (14, {})} | custom-call | flops 8589934592 | bytes 46137344 | tf_op jit(solution)/shard_map/finish/pallas_call | solution.py:94
  716.6 7.2 finish.9
  (392 shorter events, 343.3 us)
Async XLA Ops:
  7.2 43.1 %all-gather.2.cloned.1.call-start = ((), (), s32[]{:S(2)}) async-start(), calls=%async_computation.12 | async-start | bytes 2359296 | tf_op jit(solution)/shard_map/all_gather | solution.py:411
  26.8 54.6 %all-to-all-start = ((bf16[4,32,64,128]{3,2,1,0:T(8,128)(2,1)}), bf16[4,32,64,128]{3,2,1,0:T(8,128)(2,1)}, u32[]{:S(2)}, u32[]{:S(2)}) async-start(bf16[4,32,64,128]{3,2,1,0:T(8,128)(2,1)} %get-tuple-element.164), calls=%async_computation | async-start | bytes 4194304 | tf_op jit(solution)/shard_map/all_to_all | solution.py:356
  81.4 55.4 %all-to-all-start.1 = ((bf16[4,32,64,128]{3,2,1,0:T(8,128)(2,1)}), bf16[4,32,64,128]{3,2,1,0:T(8,128)(2,1)}, u32[]{:S(2)}, u32[]{:S(2)}) async-start(bf16[4,32,64,128]{3,2,1,0:T(8,128)(2,1)} %after.9), calls=%async_computation.1 | async-start | bytes 4194304 | tf_op jit(solution)/shard_map/all_to_all | solution.py:356
  136.8 65.0 %all-to-all-start.2 = ((bf16[4,32,64,128]{3,2,1,0:T(8,128)(2,1)}), bf16[4,32,64,128]{3,2,1,0:T(8,128)(2,1)}, u32[]{:S(2)}, u32[]{:S(2)}) async-start(bf16[4,32,64,128]{3,2,1,0:T(8,128)(2,1)} %after.10), calls=%async_computation.2 | async-start | bytes 4194304 | tf_op jit(solution)/shard_map/all_to_all | solution.py:356
  179.4 26.9 %collective-permute-start.9 = (s16[32,32,128]{2,1,0:T(8,128)(2,1)S(1)}, s16[32,32,128]{2,1,0:T(8,128)(2,1)S(1)}, u32[]{:S(2)}, u32[]{:S(2)}) collective-permute-start(s16[32,32,128]{2,1,0:T(8,128)(2,1)S(1)} %get-tuple-element.182), channel_id=1, source_target_pairs={{0,3},{1,2},{2,1},{3,0},{4,7},{5,6},{6,5},{7,4},{8,11},{9,10},{10,... | collective-permute-start | bytes 786440 | tf_op jit(solution)/shard_map/ppermute | solution.py:362
  201.8 62.7 %all-to-all-start.3 = ((bf16[4,32,64,128]{3,2,1,0:T(8,128)(2,1)}), bf16[4,32,64,128]{3,2,1,0:T(8,128)(2,1)}, u32[]{:S(2)}, u32[]{:S(2)}) async-start(bf16[4,32,64,128]{3,2,1,0:T(8,128)(2,1)} %after.11), calls=%async_computation.3 | async-start | bytes 4194304 | tf_op jit(solution)/shard_map/all_to_all | solution.py:356
  246.8 28.0 %collective-permute-start.23 = (s16[32,32,128]{2,1,0:T(8,128)(2,1)S(1)}, s16[32,32,128]{2,1,0:T(8,128)(2,1)S(1)}, u32[]{:S(2)}, u32[]{:S(2)}) collective-permute-start(s16[32,32,128]{2,1,0:T(8,128)(2,1)S(1)} %get-tuple-element.203), channel_id=1, source_target_pairs={{0,3},{1,2},{2,1},{3,0},{4,7},{5,6},{6,5},{7,4},{8,11},{9,10},{10,... | collective-permute-start | bytes 786440 | tf_op jit(solution)/shard_map/ppermute | solution.py:362
  249.0 25.8 %collective-permute-start.24 = (s16[32,32,128]{2,1,0:T(8,128)(2,1)S(1)}, s16[32,32,128]{2,1,0:T(8,128)(2,1)S(1)}, u32[]{:S(2)}, u32[]{:S(2)}) collective-permute-start(s16[32,32,128]{2,1,0:T(8,128)(2,1)S(1)} %get-tuple-element.204), channel_id=1, source_target_pairs={{0,4},{1,5},{2,6},{3,7},{4,0},{5,1},{6,2},{7,3},{8,12},{9,13},{10,... | collective-permute-start | bytes 786440 | tf_op jit(solution)/shard_map/ppermute | solution.py:362
  250.7 31.3 %collective-permute-start.25 = (s16[32,32,128]{2,1,0:T(8,128)(2,1)S(1)}, s16[32,32,128]{2,1,0:T(8,128)(2,1)S(1)}, u32[]{:S(2)}, u32[]{:S(2)}) collective-permute-start(s16[32,32,128]{2,1,0:T(8,128)(2,1)S(1)} %get-tuple-element.205), channel_id=1, source_target_pairs={{0,5},{1,4},{2,7},{3,6},{4,1},{5,0},{6,3},{7,2},{8,13},{9,12},{10,... | collective-permute-start | bytes 786440 | tf_op jit(solution)/shard_map/ppermute | solution.py:362
  254.5 27.5 %collective-permute-start.26 = (s16[32,32,128]{2,1,0:T(8,128)(2,1)S(1)}, s16[32,32,128]{2,1,0:T(8,128)(2,1)S(1)}, u32[]{:S(2)}, u32[]{:S(2)}) collective-permute-start(s16[32,32,128]{2,1,0:T(8,128)(2,1)S(1)} %get-tuple-element.206), channel_id=1, source_target_pairs={{0,6},{1,7},{2,4},{3,5},{4,2},{5,3},{6,0},{7,1},{8,14},{9,15},{10,... | collective-permute-start | bytes 786440 | tf_op jit(solution)/shard_map/ppermute | solution.py:362
  264.5 98.8 %all-to-all-start.4 = ((bf16[4,64,64,128]{3,2,1,0:T(8,128)(2,1)}), bf16[4,64,64,128]{3,2,1,0:T(8,128)(2,1)}, u32[]{:S(2)}, u32[]{:S(2)}) async-start(bf16[4,64,64,128]{3,2,1,0:T(8,128)(2,1)} %after.12), calls=%async_computation.4 | async-start | bytes 8388608 | tf_op jit(solution)/shard_map/all_to_all | solution.py:356
  274.8 25.2 %collective-permute-start.36 = (s16[32,32,128]{2,1,0:T(8,128)(2,1)S(1)}, s16[32,32,128]{2,1,0:T(8,128)(2,1)S(1)}, u32[]{:S(2)}, u32[]{:S(2)}) collective-permute-start(s16[32,32,128]{2,1,0:T(8,128)(2,1)S(1)} %get-tuple-element.224), channel_id=1, source_target_pairs={{0,2},{1,3},{2,0},{3,1},{4,6},{5,7},{6,4},{7,5},{8,10},{9,11},{10,... | collective-permute-start | bytes 786440 | tf_op jit(solution)/shard_map/ppermute | solution.py:362
  314.2 28.3 %collective-permute-start.38 = (s16[32,32,128]{2,1,0:T(8,128)(2,1)S(1)}, s16[32,32,128]{2,1,0:T(8,128)(2,1)S(1)}, u32[]{:S(2)}, u32[]{:S(2)}) collective-permute-start(s16[32,32,128]{2,1,0:T(8,128)(2,1)S(1)} %get-tuple-element.226), channel_id=1, source_target_pairs={{0,4},{1,5},{2,6},{3,7},{4,0},{5,1},{6,2},{7,3},{8,12},{9,13},{10,... | collective-permute-start | bytes 786440 | tf_op jit(solution)/shard_map/ppermute | solution.py:362
  363.3 54.4 %all-to-all-start.5 = ((bf16[4,64,32,128]{3,2,1,0:T(8,128)(2,1)}), bf16[4,64,32,128]{3,2,1,0:T(8,128)(2,1)}, u32[]{:S(2)}, u32[]{:S(2)}) async-start(bf16[4,64,32,128]{3,2,1,0:T(8,128)(2,1)} %after.13), calls=%async_computation.5 | async-start | bytes 4194304 | tf_op jit(solution)/shard_map/all_to_all | solution.py:356
  470.3 51.9 %all-to-all-start.8 = ((bf16[4,32,64,128]{3,2,1,0:T(8,128)(2,1)}), bf16[4,32,64,128]{3,2,1,0:T(8,128)(2,1)}, u32[]{:S(2)}, u32[]{:S(2)}) async-start(bf16[4,32,64,128]{3,2,1,0:T(8,128)(2,1)} %get-tuple-element.260), calls=%async_computation.8 | async-start | bytes 4194304 | tf_op jit(solution)/shard_map/all_to_all | solution.py:356
  490.4 31.7 %collective-permute-start.57 = (f32[4,128]{1,0:T(4,128)S(1)}, f32[4,128]{1,0:T(4,128)S(1)}, u32[]{:S(2)}, u32[]{:S(2)}) collective-permute-start(f32[4,128]{1,0:T(4,128)S(1)} %broadcast_in_dim.30), channel_id=1, source_target_pairs={{0,16},{8,24},{16,0},{24,8},{1,17},{9,25},{17,1},{25,9},{2,18},{10... | collective-permute-start | bytes 6152 | tf_op jit(solution)/shard_map/ppermute | solution.py:367
  493.3 28.9 %collective-permute-start.58 = (f32[4,128]{1,0:T(4,128)S(1)}, f32[4,128]{1,0:T(4,128)S(1)}, u32[]{:S(2)}, u32[]{:S(2)}) collective-permute-start(f32[4,128]{1,0:T(4,128)S(1)} %broadcast_in_dim.30), channel_id=1, source_target_pairs={{0,24},{8,16},{16,8},{24,0},{1,25},{9,17},{17,9},{25,1},{2,26},{10... | collective-permute-start | bytes 6152 | tf_op jit(solution)/shard_map/ppermute | solution.py:367
  494.7 27.4 %collective-permute-start.56 = (f32[4,128]{1,0:T(4,128)S(1)}, f32[4,128]{1,0:T(4,128)S(1)}, u32[]{:S(2)}, u32[]{:S(2)}) collective-permute-start(f32[4,128]{1,0:T(4,128)S(1)} %broadcast_in_dim.30), channel_id=1, source_target_pairs={{0,8},{8,0},{16,24},{24,16},{1,9},{9,1},{17,25},{25,17},{2,10},{10... | collective-permute-start | bytes 6152 | tf_op jit(solution)/shard_map/ppermute | solution.py:367
  522.2 52.3 %all-to-all-start.7 = ((bf16[4,32,64,128]{3,2,1,0:T(8,128)(2,1)}), bf16[4,32,64,128]{3,2,1,0:T(8,128)(2,1)}, u32[]{:S(2)}, u32[]{:S(2)}) async-start(bf16[4,32,64,128]{3,2,1,0:T(8,128)(2,1)} %after.14), calls=%async_computation.7 | async-start | bytes 4194304 | tf_op jit(solution)/shard_map/all_to_all | solution.py:356
  574.5 52.4 %all-to-all-start.9 = ((bf16[4,32,64,128]{3,2,1,0:T(8,128)(2,1)}), bf16[4,32,64,128]{3,2,1,0:T(8,128)(2,1)}, u32[]{:S(2)}, u32[]{:S(2)}) async-start(bf16[4,32,64,128]{3,2,1,0:T(8,128)(2,1)} %after.15), calls=%async_computation.9 | async-start | bytes 4194304 | tf_op jit(solution)/shard_map/all_to_all | solution.py:356
  626.9 29.5 %all-to-all-start.11 = ((bf16[4,16,64,128]{3,2,1,0:T(8,128)(2,1)}), bf16[4,16,64,128]{3,2,1,0:T(8,128)(2,1)}, u32[]{:S(2)}, u32[]{:S(2)}) async-start(bf16[4,16,64,128]{3,2,1,0:T(8,128)(2,1)} %after.17), calls=%async_computation.11 | async-start | bytes 2097152 | tf_op jit(solution)/shard_map/all_to_all | solution.py:356
  656.5 38.3 %all-to-all-start.10 = ((bf16[4,16,64,128]{3,2,1,0:T(8,128)(2,1)}), bf16[4,16,64,128]{3,2,1,0:T(8,128)(2,1)}, u32[]{:S(2)}, u32[]{:S(2)}) async-start(bf16[4,16,64,128]{3,2,1,0:T(8,128)(2,1)} %after.16), calls=%async_computation.10 | async-start | bytes 2097152 | tf_op jit(solution)/shard_map/all_to_all | solution.py:356
  668.4 28.8 %collective-permute-start.90 = (s16[16,32,128]{2,1,0:T(8,128)(2,1)}, s16[16,32,128]{2,1,0:T(8,128)(2,1)S(1)}, u32[]{:S(2)}, u32[]{:S(2)}) collective-permute-start(s16[16,32,128]{2,1,0:T(8,128)(2,1)} %get-tuple-element.311), channel_id=1, source_target_pairs={{0,1},{1,0},{2,3},{3,2},{4,5},{5,4},{6,7},{7,6},{8,9},{9,8},{10,11... | collective-permute-start | bytes 393224 | tf_op jit(solution)/shard_map/ppermute | solution.py:362
  668.8 28.7 %collective-permute-start.91 = (s16[16,32,128]{2,1,0:T(8,128)(2,1)}, s16[16,32,128]{2,1,0:T(8,128)(2,1)S(1)}, u32[]{:S(2)}, u32[]{:S(2)}) collective-permute-start(s16[16,32,128]{2,1,0:T(8,128)(2,1)} %get-tuple-element.312), channel_id=1, source_target_pairs={{0,2},{1,3},{2,0},{3,1},{4,6},{5,7},{6,4},{7,5},{8,10},{9,11},{10,... | collective-permute-start | bytes 393224 | tf_op jit(solution)/shard_map/ppermute | solution.py:362
  (141 other events, 1735.5 us)
Sparse Core Ops, SparseCore 0:
  9.9 30.9 all-gather.1

commit v8 on v7

--- a/solution.py
+++ b/solution.py
@@ -453,6 +453,7 @@
     lower(first)
     arrived[fourth] = swap_tm(wait(waves[fourth]))
     middle(second)
+    arrived[third] = wait(arrived[third], *sent[second][1:4])
     up(third)
     lower(second)
     down[second] = swap_tm(wait(down[second][0]))
@@ -503,7 +504,7 @@
     late[1] = swap_tm(wait(late[1], *second_codes[1:]))
     third_codes = back(1, 0, hour_part, late[0])
     earlier = end(0, hour_part, hour_part, second_codes)
-    late[2] = swap_tm(wait(late[2], *third_codes[1:5]))
+    late[2] = swap_tm(wait(late[2], *third_codes[1:6]))
     fourth_codes = back(1, 0, quarters[0][1], late[1])
     earlier = end(1, *pieces[0], third_codes)
     fifth_codes = back(1, 0, quarters[1][1], late[2])

time: 736 us -> 724 us (0.984)
  waiting for transfers between devices: 249 us -> 236 us
    ppermute x91, waiting for transfers between devices: 147 us -> 133 us  [swap_lon(): lax.ppermute(parts[d], 'lon', [(i, i ^ d) for i in range(count)])]
    unnamed x122 -> x116, local copies, waits for them, and re-layouts: 22 us -> 20.6 us
  transfers between devices with their start and end apart: 109 -> 109, of which waited for: 37 -> 37; matrix products, arithmetic and copies ran while one was open for 4% -> 4% of each run, Pallas kernels for 26% -> 27%
where the time goes in v8:
time: 724 us; the launch traced here: 719 us
  waiting for transfers between devices  236 us (33%)
  Pallas kernels  198 us (27%)
  starting transfers between devices  157 us (22%)
  blocking collectives  52.4 us (7%)
  between operations  29.9 us (4%)
  local copies, waits for them, and re-layouts  26.2 us (4%)
  other arithmetic  13.4 us (2%)
    pallas_call x26, Pallas kernels, run(): pl.pallas_call(whole, name=name, grid=(grid,), out_shape=list(out_shape)...  198 us
    ppermute x91, waiting for transfers between devices, swap_lon(): lax.ppermute(parts[d], 'lon', [(i, i ^ d) for i in range(count)])  133 us
    ppermute x91, starting transfers between devices, swap_lon(): lax.ppermute(parts[d], 'lon', [(i, i ^ d) for i in range(count)])  89.1 us
    all_to_all x11, waiting for transfers between devices, swap_tm(): return lax.all_to_all(x, 'tm', split_axis=0, concat_axis=0, tiled=True)  71.2 us
    all_to_all x11, starting transfers between devices, swap_tm(): return lax.all_to_all(x, 'tm', split_axis=0, concat_axis=0, tiled=True)  62.7 us
    all_to_all x1, blocking collectives, swap_tm(): return lax.all_to_all(x, 'tm', split_axis=0, concat_axis=0, tiled=True)  52.4 us
    ppermute x3, waiting for transfers between devices, add_over_tm(): lax.ppermute(x, 'tm', [(i, i ^ d) for i in range(count)])  27.5 us
    unnamed x116, local copies, waits for them, and re-layouts  20.6 us
  transfers between devices with their start and end apart: 109, of which 37 were waited for; matrix products, arithmetic and copies ran while one was open for 4% of the time, Pallas kernels for 27%

profile of v8, /device:TPU:0, one launch (start us, length us, event | category | flops | bytes accessed | tf_op | source)
XLA Modules:
  0.0 719.2 jit_solution(18441765057459612282)
XLA Ops:
  15.7 11.1 %hourly.2 = (bf16[4,32,64,128]{3,2,1,0:T(8,128)(2,1)}, bf16[4,32,64,128]{3,2,1,0:T(8,128)(2,1)}, f32[8,128]{1,0:T(8,128)S(1)}) custom-call(bf16[2,64,128,512]{3,2,1,0:T(8,128)(2,1)} %refs_0_.3, bf16[2,256,512]{2,1,0:T(8,128)(2,1)S(1)} %get-tuple-element.332.refs_1_), custom_call_target="tpu_custom_call" | custom-call | flops 4294967296 | bytes 20971520 | tf_op jit(solution)/shard_map/hourly/pallas_call | solution.py:94
  39.0 11.3 %hourly.3 = (bf16[4,32,64,128]{3,2,1,0:T(8,128)(2,1)}, bf16[4,32,64,128]{3,2,1,0:T(8,128)(2,1)}, f32[8,128]{1,0:T(8,128)S(1)}) custom-call(bf16[2,64,128,512]{3,2,1,0:T(8,128)(2,1)} %refs_0_.3, bf16[2,256,512]{2,1,0:T(8,128)(2,1)S(1)} %get-tuple-element.333.refs_1_, f32[8,128]{1,0:T(8,128)S(1)} %get-tuple-element.165.refs_2_), custom_call_target="tpu_custom_call" | custom-call | flops 4294967296 | bytes 20971520 | tf_op jit(solution)/shard_map/hourly/pallas_call | solution.py:94
  57.2 24.2 %all-to-all-done.refs_1_ = bf16[4,32,64,128]{3,2,1,0:T(8,128)(2,1)} async-done(((bf16[4,32,64,128]{3,2,1,0:T(8,128)(2,1)}), bf16[4,32,64,128]{3,2,1,0:T(8,128)(2,1)}, u32[]{:S(2)}, u32[]{:S(2)}) %all-to-all-start) | async-done | bytes 2097184 | tf_op jit(solution)/shard_map/all_to_all | solution.py:356
  108.1 12.3 %collective-permute-done.4.refs_6_ = s16[32,32,128]{2,1,0:T(8,128)(2,1)S(1)} collective-permute-done((s16[32,32,128]{2,1,0:T(8,128)(2,1)S(1)}, s16[32,32,128]{2,1,0:T(8,128)(2,1)S(1)}, u32[]{:S(2)}, u32[]{:S(2)}) %collective-permute-start.4) | collective-permute-done | bytes 262176 | tf_op jit(solution)/shard_map/ppermute | solution.py:362
  121.3 14.8 %residual.4 = (f32[32,32,1024]{2,1,0:T(8,128)}, f32[8,128]{1,0:T(8,128)S(1)}, bf16[32,32,128]{2,1,0:T(8,128)(2,1)S(1)}, bf16[32,32,128]{2,1,0:T(8,128)(2,1)}, bf...) custom-call(f32[1]{0:T(128)} %bitcast.8.refs_0_, ...), custom_call_target="tpu_custom_call" | custom-call | flops 8589934592 | bytes 16777216 | tf_op jit(solution)/shard_map/residual/pallas_call | solution.py:94
  136.8 15.5 %all-to-all-start.2 = ((bf16[4,32,64,128]{3,2,1,0:T(8,128)(2,1)}), bf16[4,32,64,128]{3,2,1,0:T(8,128)(2,1)}, u32[]{:S(2)}, u32[]{:S(2)}) async-start(bf16[4,32,64,128]{3,2,1,0:T(8,128)(2,1)} %after.11), calls=%async_computation.2 | async-start | bytes 4194304 | tf_op jit(solution)/shard_map/all_to_all | solution.py:356
  169.5 9.8 %collective-permute-done.18.refs_5_ = bf16[32,32,128]{2,1,0:T(8,128)(2,1)S(1)} collective-permute-done((bf16[32,32,128]{2,1,0:T(8,128)(2,1)S(1)}, bf16[32,32,128]{2,1,0:T(8,128)(2,1)S(1)}, u32[]{:S(2)}, u32[]{:S(2)}) %collective-permute-start.18) | collective-permute-done | bytes 262176 | tf_op jit(solution)/shard_map/ppermute | solution.py:362
  192.2 9.8 %all-to-all-done.2.refs_0_ = bf16[4,32,64,128]{3,2,1,0:T(8,128)(2,1)} async-done(((bf16[4,32,64,128]{3,2,1,0:T(8,128)(2,1)}), bf16[4,32,64,128]{3,2,1,0:T(8,128)(2,1)}, u32[]{:S(2)}, u32[]{:S(2)}) %all-to-all-start.2) | async-done | bytes 2097184 | tf_op jit(solution)/shard_map/all_to_all | solution.py:356
  207.1 14.8 %residual.5 = (f32[32,32,1024]{2,1,0:T(8,128)}, f32[8,128]{1,0:T(8,128)S(1)}, bf16[32,32,128]{2,1,0:T(8,128)(2,1)S(1)}, bf16[32,32,128]{2,1,0:T(8,128)(2,1)S(1)}...) custom-call(f32[1]{0:T(128)} %bitcast.8.refs_0_, ...), custom_call_target="tpu_custom_call" | custom-call | flops 34359738368 | bytes 67108864 | tf_op jit(solution)/shard_map/residual/pallas_call | solution.py:94
  275.5 14.8 %residual.6 = (f32[32,32,1024]{2,1,0:T(8,128)}, f32[8,128]{1,0:T(8,128)S(1)}, bf16[32,32,128]{2,1,0:T(8,128)(2,1)S(1)}, bf16[32,32,128]{2,1,0:T(8,128)(2,1)S(1)}...) custom-call(f32[1]{0:T(128)} %bitcast.8.refs_0_, ...), custom_call_target="tpu_custom_call" | custom-call | flops 34359738368 | bytes 67108864 | tf_op jit(solution)/shard_map/residual/pallas_call | solution.py:94
  308.3 9.7 %collective-permute-done.46.refs_5_ = bf16[32,32,128]{2,1,0:T(8,128)(2,1)S(1)} collective-permute-done((bf16[32,32,128]{2,1,0:T(8,128)(2,1)S(1)}, bf16[32,32,128]{2,1,0:T(8,128)(2,1)S(1)}, u32[]{:S(2)}, u32[]{:S(2)}) %collective-permute-start.46) | collective-permute-done | bytes 262176 | tf_op jit(solution)/shard_map/ppermute | solution.py:362
  326.1 9.5 %collective-permute-done.38.refs_5_ = s16[32,32,128]{2,1,0:T(8,128)(2,1)S(1)} collective-permute-done((s16[32,32,128]{2,1,0:T(8,128)(2,1)S(1)}, s16[32,32,128]{2,1,0:T(8,128)(2,1)S(1)}, u32[]{:S(2)}, u32[]{:S(2)}) %collective-permute-start.38) | collective-permute-done | bytes 262176 | tf_op jit(solution)/shard_map/ppermute | solution.py:362
  341.7 14.8 %residual.7 = (f32[32,32,1024]{2,1,0:T(8,128)}, f32[8,128]{1,0:T(8,128)S(1)}, bf16[32,32,128]{2,1,0:T(8,128)(2,1)S(1)}, bf16[32,32,128]{2,1,0:T(8,128)(2,1)S(1)}...) custom-call(f32[1]{0:T(128)} %bitcast.8.refs_0_, ...), custom_call_target="tpu_custom_call" | custom-call | flops 34359738368 | bytes 67108864 | tf_op jit(solution)/shard_map/residual/pallas_call | solution.py:94
  382.1 13.1 %collective-permute-done.53.refs_5_ = bf16[32,32,128]{2,1,0:T(8,128)(2,1)S(1)} collective-permute-done((bf16[32,32,128]{2,1,0:T(8,128)(2,1)S(1)}, bf16[32,32,128]{2,1,0:T(8,128)(2,1)S(1)}, u32[]{:S(2)}, u32[]{:S(2)}) %collective-permute-start.53) | collective-permute-done | bytes 262176 | tf_op jit(solution)/shard_map/ppermute | solution.py:362
  399.7 12.2 %all-to-all-done.5.refs_0_ = bf16[4,64,32,128]{3,2,1,0:T(8,128)(2,1)} async-done(((bf16[4,64,32,128]{3,2,1,0:T(8,128)(2,1)}), bf16[4,64,32,128]{3,2,1,0:T(8,128)(2,1)}, u32[]{:S(2)}, u32[]{:S(2)}) %all-to-all-start.5) | async-done | bytes 2097184 | tf_op jit(solution)/shard_map/all_to_all | solution.py:356
  411.9 52.4 %all_to_all.60.refs_1_ = bf16[4,64,32,128]{3,2,1,0:T(8,128)(2,1)} all-to-all(bf16[4,64,32,128]{3,2,1,0:T(8,128)(2,1)} %get-tuple-element.254), channel_id=1, replica_groups=mesh['tm'=4,'lon'=8] {'tm'}, dimensions={0} | all-to-all | bytes 4194304 | tf_op jit(solution)/shard_map/all_to_all | solution.py:356
  488.7 27.5 %collective-permute-done.57 = f32[4,128]{1,0:T(4,128)S(1)} collective-permute-done((f32[4,128]{1,0:T(4,128)S(1)}, f32[4,128]{1,0:T(4,128)S(1)}, u32[]{:S(2)}, u32[]{:S(2)}) %collective-permute-start.57) | collective-permute-done | bytes 2080 | tf_op jit(solution)/shard_map/ppermute | solution.py:367
  549.9 12.6 %collective-permute-done.73.refs_6_ = s16[32,32,128]{2,1,0:T(8,128)(2,1)S(1)} collective-permute-done((s16[32,32,128]{2,1,0:T(8,128)(2,1)S(1)}, s16[32,32,128]{2,1,0:T(8,128)(2,1)S(1)}, u32[]{:S(2)}, u32[]{:S(2)}) %collective-permute-start.73) | collective-permute-done | bytes 262176 | tf_op jit(solution)/shard_map/ppermute | solution.py:362
  589.1 11.9 %finish.5 = (f32[2,64,32,1024]{3,2,1,0:T(8,128)}, f32[2,64,32,1024]{3,2,1,0:T(8,128)}, f32[8,128]{1,0:T(8,128)S(1)}) custom-call(f32[2]{0:T(128)S(1)} %pad_maximum_fusion.5.refs_0_, s16[32,32,128]{2,1,0:T(8,128)(2,1)S(1)} %copy-done.11, s16[32,32,128]{2,1,0:T(8,128)(2,1)S(1)} %collective-permute-done.69.refs_2_, ...), custom_call_target="tpu_custom_call" | custom-call | flops 8589934592 | bytes 46137344 | tf_op jit(solution)/shard_map/finish/pallas_call | solution.py:94
  606.9 14.1 %all-to-all-done.9.refs_1_ = bf16[4,32,64,128]{3,2,1,0:T(8,128)(2,1)} async-done(((bf16[4,32,64,128]{3,2,1,0:T(8,128)(2,1)}), bf16[4,32,64,128]{3,2,1,0:T(8,128)(2,1)}, u32[]{:S(2)}, u32[]{:S(2)}) %all-to-all-start.9) | async-done | bytes 2097184 | tf_op jit(solution)/shard_map/all_to_all | solution.py:356
  634.1 11.9 %finish.6 = (f32[2,64,32,1024]{3,2,1,0:T(8,128)}, f32[2,64,32,1024]{3,2,1,0:T(8,128)}, f32[8,128]{1,0:T(8,128)S(1)}) custom-call(f32[2]{0:T(128)S(1)} %pad_maximum_fusion.5.refs_0_, s16[32,32,128]{2,1,0:T(8,128)(2,1)S(1)} %get-tuple-element.262.refs_1_, ...), custom_call_target="tpu_custom_call", output_to_operand_aliasing={{0}: (13, {}), {1}: (14, {})} | custom-call | flops 8589934592 | bytes 46137344 | tf_op jit(solution)/shard_map/finish/pallas_call | solution.py:94
  670.7 11.9 %finish.7 = (f32[2,64,32,1024]{3,2,1,0:T(8,128)}, f32[2,64,32,1024]{3,2,1,0:T(8,128)}, f32[8,128]{1,0:T(8,128)S(1)}) custom-call(f32[2]{0:T(128)S(1)} %pad_maximum_fusion.4.refs_0_, s16[32,32,128]{2,1,0:T(8,128)(2,1)S(1)} %get-tuple-element.292.refs_1_, ...), custom_call_target="tpu_custom_call", output_to_operand_aliasing={{0}: (13, {}), {1}: (14, {})} | custom-call | flops 8589934592 | bytes 46137344 | tf_op jit(solution)/shard_map/finish/pallas_call | solution.py:94
  697.8 7.2 finish.8
  705.0 7.2 %finish.9 = (f32[2,64,32,1024]{3,2,1,0:T(8,128)}, f32[2,64,32,1024]{3,2,1,0:T(8,128)}, f32[8,128]{1,0:T(8,128)}) custom-call(f32[2]{0:T(128)S(1)} %pad_maximum_fusion.4.refs_0_, s16[16,32,128]{2,1,0:T(8,128)(2,1)S(1)} %get-tuple-element.301.refs_1_, ...), custom_call_target="tpu_custom_call", output_to_operand_aliasing={{0}: (13, {}), {1}: (14, {})} | custom-call | flops 4294967296 | bytes 23068672 | tf_op jit(solution)/shard_map/finish/pallas_call | solution.py:94
  (387 shorter events, 335.1 us)
Async XLA Ops:
  7.2 43.1 %all-gather.2.cloned.1.call-start = ((), (), s32[]{:S(2)}) async-start(), calls=%async_computation.12 | async-start | bytes 2359296 | tf_op jit(solution)/shard_map/all_gather | solution.py:411
  26.8 54.6 %all-to-all-start = ((bf16[4,32,64,128]{3,2,1,0:T(8,128)(2,1)}), bf16[4,32,64,128]{3,2,1,0:T(8,128)(2,1)}, u32[]{:S(2)}, u32[]{:S(2)}) async-start(bf16[4,32,64,128]{3,2,1,0:T(8,128)(2,1)} %get-tuple-element.164), calls=%async_computation | async-start | bytes 4194304 | tf_op jit(solution)/shard_map/all_to_all | solution.py:356
  81.4 55.4 %all-to-all-start.1 = ((bf16[4,32,64,128]{3,2,1,0:T(8,128)(2,1)}), bf16[4,32,64,128]{3,2,1,0:T(8,128)(2,1)}, u32[]{:S(2)}, u32[]{:S(2)}) async-start(bf16[4,32,64,128]{3,2,1,0:T(8,128)(2,1)} %after.10), calls=%async_computation.1 | async-start | bytes 4194304 | tf_op jit(solution)/shard_map/all_to_all | solution.py:356
  136.8 65.1 %all-to-all-start.2 = ((bf16[4,32,64,128]{3,2,1,0:T(8,128)(2,1)}), bf16[4,32,64,128]{3,2,1,0:T(8,128)(2,1)}, u32[]{:S(2)}, u32[]{:S(2)}) async-start(bf16[4,32,64,128]{3,2,1,0:T(8,128)(2,1)} %after.11), calls=%async_computation.2 | async-start | bytes 4194304 | tf_op jit(solution)/shard_map/all_to_all | solution.py:356
  179.4 27.0 %collective-permute-start.9 = (s16[32,32,128]{2,1,0:T(8,128)(2,1)S(1)}, s16[32,32,128]{2,1,0:T(8,128)(2,1)S(1)}, u32[]{:S(2)}, u32[]{:S(2)}) collective-permute-start(s16[32,32,128]{2,1,0:T(8,128)(2,1)S(1)} %get-tuple-element.182), channel_id=1, source_target_pairs={{0,3},{1,2},{2,1},{3,0},{4,7},{5,6},{6,5},{7,4},{8,11},{9,10},{10,... | collective-permute-start | bytes 786440 | tf_op jit(solution)/shard_map/ppermute | solution.py:362
  182.1 24.3 %collective-permute-start.10 = (s16[32,32,128]{2,1,0:T(8,128)(2,1)S(1)}, s16[32,32,128]{2,1,0:T(8,128)(2,1)}, u32[]{:S(2)}, u32[]{:S(2)}) collective-permute-start(s16[32,32,128]{2,1,0:T(8,128)(2,1)S(1)} %get-tuple-element.183), channel_id=1, source_target_pairs={{0,4},{1,5},{2,6},{3,7},{4,0},{5,1},{6,2},{7,3},{8,12},{9,13},{10,... | collective-permute-start | bytes 786440 | tf_op jit(solution)/shard_map/ppermute | solution.py:362
  201.9 57.0 %all-to-all-start.3 = ((bf16[4,32,64,128]{3,2,1,0:T(8,128)(2,1)}), bf16[4,32,64,128]{3,2,1,0:T(8,128)(2,1)}, u32[]{:S(2)}, u32[]{:S(2)}) async-start(bf16[4,32,64,128]{3,2,1,0:T(8,128)(2,1)} %after.13), calls=%async_computation.3 | async-start | bytes 4194304 | tf_op jit(solution)/shard_map/all_to_all | solution.py:356
  225.6 25.0 %collective-permute-start.33 = (bf16[32,32,128]{2,1,0:T(8,128)(2,1)S(1)}, bf16[32,32,128]{2,1,0:T(8,128)(2,1)S(1)}, u32[]{:S(2)}, u32[]{:S(2)}) collective-permute-start(bf16[32,32,128]{2,1,0:T(8,128)(2,1)S(1)} %get-tuple-element.215), channel_id=1, source_target_pairs={{0,6},{1,7},{2,4},{3,5},{4,2},{5,3},{6,0},{7,1},{8,14},{9,15},{10,... | collective-permute-start | bytes 786440 | tf_op jit(solution)/shard_map/ppermute | solution.py:362
  258.9 99.3 %all-to-all-start.4 = ((bf16[4,64,64,128]{3,2,1,0:T(8,128)(2,1)}), bf16[4,64,64,128]{3,2,1,0:T(8,128)(2,1)}, u32[]{:S(2)}, u32[]{:S(2)}) async-start(bf16[4,64,64,128]{3,2,1,0:T(8,128)(2,1)} %after.14), calls=%async_computation.4 | async-start | bytes 8388608 | tf_op jit(solution)/shard_map/all_to_all | solution.py:356
  270.4 24.1 %collective-permute-start.36 = (s16[32,32,128]{2,1,0:T(8,128)(2,1)S(1)}, s16[32,32,128]{2,1,0:T(8,128)(2,1)S(1)}, u32[]{:S(2)}, u32[]{:S(2)}) collective-permute-start(s16[32,32,128]{2,1,0:T(8,128)(2,1)S(1)} %get-tuple-element.224), channel_id=1, source_target_pairs={{0,2},{1,3},{2,0},{3,1},{4,6},{5,7},{6,4},{7,5},{8,10},{9,11},{10,... | collective-permute-start | bytes 786440 | tf_op jit(solution)/shard_map/ppermute | solution.py:362
  294.9 25.5 %collective-permute-start.47 = (bf16[32,32,128]{2,1,0:T(8,128)(2,1)S(1)}, bf16[32,32,128]{2,1,0:T(8,128)(2,1)S(1)}, u32[]{:S(2)}, u32[]{:S(2)}) collective-permute-start(bf16[32,32,128]{2,1,0:T(8,128)(2,1)S(1)} %get-tuple-element.236), channel_id=1, source_target_pairs={{0,6},{1,7},{2,4},{3,5},{4,2},{5,3},{6,0},{7,1},{8,14},{9,15},{10,... | collective-permute-start | bytes 786440 | tf_op jit(solution)/shard_map/ppermute | solution.py:362
  306.7 28.9 %collective-permute-start.38 = (s16[32,32,128]{2,1,0:T(8,128)(2,1)S(1)}, s16[32,32,128]{2,1,0:T(8,128)(2,1)S(1)}, u32[]{:S(2)}, u32[]{:S(2)}) collective-permute-start(s16[32,32,128]{2,1,0:T(8,128)(2,1)S(1)} %get-tuple-element.226), channel_id=1, source_target_pairs={{0,4},{1,5},{2,6},{3,7},{4,0},{5,1},{6,2},{7,3},{8,12},{9,13},{10,... | collective-permute-start | bytes 786440 | tf_op jit(solution)/shard_map/ppermute | solution.py:362
  358.2 53.7 %all-to-all-start.5 = ((bf16[4,64,32,128]{3,2,1,0:T(8,128)(2,1)}), bf16[4,64,32,128]{3,2,1,0:T(8,128)(2,1)}, u32[]{:S(2)}, u32[]{:S(2)}) async-start(bf16[4,64,32,128]{3,2,1,0:T(8,128)(2,1)} %after.15), calls=%async_computation.5 | async-start | bytes 4194304 | tf_op jit(solution)/shard_map/all_to_all | solution.py:356
  464.3 52.0 %all-to-all-start.8 = ((bf16[4,32,64,128]{3,2,1,0:T(8,128)(2,1)}), bf16[4,32,64,128]{3,2,1,0:T(8,128)(2,1)}, u32[]{:S(2)}, u32[]{:S(2)}) async-start(bf16[4,32,64,128]{3,2,1,0:T(8,128)(2,1)} %get-tuple-element.260), calls=%async_computation.8 | async-start | bytes 4194304 | tf_op jit(solution)/shard_map/all_to_all | solution.py:356
  484.3 31.9 %collective-permute-start.57 = (f32[4,128]{1,0:T(4,128)S(1)}, f32[4,128]{1,0:T(4,128)S(1)}, u32[]{:S(2)}, u32[]{:S(2)}) collective-permute-start(f32[4,128]{1,0:T(4,128)S(1)} %broadcast_in_dim.30), channel_id=1, source_target_pairs={{0,16},{8,24},{16,0},{24,8},{1,17},{9,25},{17,1},{25,9},{2,18},{10... | collective-permute-start | bytes 6152 | tf_op jit(solution)/shard_map/ppermute | solution.py:367
  487.2 29.0 %collective-permute-start.58 = (f32[4,128]{1,0:T(4,128)S(1)}, f32[4,128]{1,0:T(4,128)S(1)}, u32[]{:S(2)}, u32[]{:S(2)}) collective-permute-start(f32[4,128]{1,0:T(4,128)S(1)} %broadcast_in_dim.30), channel_id=1, source_target_pairs={{0,24},{8,16},{16,8},{24,0},{1,25},{9,17},{17,9},{25,1},{2,26},{10... | collective-permute-start | bytes 6152 | tf_op jit(solution)/shard_map/ppermute | solution.py:367
  488.6 27.6 %collective-permute-start.56 = (f32[4,128]{1,0:T(4,128)S(1)}, f32[4,128]{1,0:T(4,128)S(1)}, u32[]{:S(2)}, u32[]{:S(2)}) collective-permute-start(f32[4,128]{1,0:T(4,128)S(1)} %broadcast_in_dim.30), channel_id=1, source_target_pairs={{0,8},{8,0},{16,24},{24,16},{1,9},{9,1},{17,25},{25,17},{2,10},{10... | collective-permute-start | bytes 6152 | tf_op jit(solution)/shard_map/ppermute | solution.py:367
  516.3 52.3 %all-to-all-start.7 = ((bf16[4,32,64,128]{3,2,1,0:T(8,128)(2,1)}), bf16[4,32,64,128]{3,2,1,0:T(8,128)(2,1)}, u32[]{:S(2)}, u32[]{:S(2)}) async-start(bf16[4,32,64,128]{3,2,1,0:T(8,128)(2,1)} %after.16), calls=%async_computation.7 | async-start | bytes 4194304 | tf_op jit(solution)/shard_map/all_to_all | solution.py:356
  538.4 24.2 %collective-permute-start.73 = (s16[32,32,128]{2,1,0:T(8,128)(2,1)S(1)}, s16[32,32,128]{2,1,0:T(8,128)(2,1)S(1)}, u32[]{:S(2)}, u32[]{:S(2)}) collective-permute-start(s16[32,32,128]{2,1,0:T(8,128)(2,1)S(1)} %get-tuple-element.276), channel_id=1, source_target_pairs={{0,5},{1,4},{2,7},{3,6},{4,1},{5,0},{6,3},{7,2},{8,13},{9,12},{10,... | collective-permute-start | bytes 786440 | tf_op jit(solution)/shard_map/ppermute | solution.py:362
  568.6 52.4 %all-to-all-start.9 = ((bf16[4,32,64,128]{3,2,1,0:T(8,128)(2,1)}), bf16[4,32,64,128]{3,2,1,0:T(8,128)(2,1)}, u32[]{:S(2)}, u32[]{:S(2)}) async-start(bf16[4,32,64,128]{3,2,1,0:T(8,128)(2,1)} %after.17), calls=%async_computation.9 | async-start | bytes 4194304 | tf_op jit(solution)/shard_map/all_to_all | solution.py:356
  582.4 24.5 %collective-permute-start.66 = (s16[32,32,128]{2,1,0:T(8,128)(2,1)}, s16[32,32,128]{2,1,0:T(8,128)(2,1)S(1)}, u32[]{:S(2)}, u32[]{:S(2)}) collective-permute-start(s16[32,32,128]{2,1,0:T(8,128)(2,1)} %get-tuple-element.267), channel_id=1, source_target_pairs={{0,5},{1,4},{2,7},{3,6},{4,1},{5,0},{6,3},{7,2},{8,13},{9,12},{10,... | collective-permute-start | bytes 786440 | tf_op jit(solution)/shard_map/ppermute | solution.py:362
  621.0 29.5 %all-to-all-start.11 = ((bf16[4,16,64,128]{3,2,1,0:T(8,128)(2,1)}), bf16[4,16,64,128]{3,2,1,0:T(8,128)(2,1)}, u32[]{:S(2)}, u32[]{:S(2)}) async-start(bf16[4,16,64,128]{3,2,1,0:T(8,128)(2,1)} %after.19), calls=%async_computation.11 | async-start | bytes 2097152 | tf_op jit(solution)/shard_map/all_to_all | solution.py:356
  650.6 32.0 %all-to-all-start.10 = ((bf16[4,16,64,128]{3,2,1,0:T(8,128)(2,1)}), bf16[4,16,64,128]{3,2,1,0:T(8,128)(2,1)}, u32[]{:S(2)}, u32[]{:S(2)}) async-start(bf16[4,16,64,128]{3,2,1,0:T(8,128)(2,1)} %after.18), calls=%async_computation.10 | async-start | bytes 2097152 | tf_op jit(solution)/shard_map/all_to_all | solution.py:356
  660.9 24.1 %collective-permute-start.90 = (s16[16,32,128]{2,1,0:T(8,128)(2,1)}, s16[16,32,128]{2,1,0:T(8,128)(2,1)S(1)}, u32[]{:S(2)}, u32[]{:S(2)}) collective-permute-start(s16[16,32,128]{2,1,0:T(8,128)(2,1)} %get-tuple-element.311), channel_id=1, source_target_pairs={{0,1},{1,0},{2,3},{3,2},{4,5},{5,4},{6,7},{7,6},{8,9},{9,8},{10,11... | collective-permute-start | bytes 393224 | tf_op jit(solution)/shard_map/ppermute | solution.py:362
  (138 other events, 1668.9 us)
Sparse Core Ops, SparseCore 0:
  9.9 30.9 all-gather.1

commit v9 on v8

--- a/solution.py
+++ b/solution.py
@@ -1,6 +1,7 @@
 import functools
 import jax
 import jax.numpy as jnp
+import numpy as np
 from jax import lax
 from jax.experimental import pallas as pl
 from jax.experimental.pallas import tpu as pltpu
@@ -393,9 +394,8 @@
 
     powers = jnp.concatenate([spectrum, spectrum[1:-1][::-1]])
     amplitude = jnp.sqrt(powers / periods)
-    clock = jnp.arange(hours)[:, None]
-    phase = (clock * jnp.arange(periods) % periods).astype(F32) * (2.0 * jnp.pi / periods)
-    cosine_tab, sine_tab = jnp.cos(phase), jnp.sin(phase)
+    turns = np.arange(hours)[:, None] * np.arange(periods) % periods * (2.0 * np.pi / periods)
+    cosine_tab, sine_tab = jnp.asarray(np.cos(turns), F32), jnp.asarray(np.sin(turns), F32)
     table_cos = (cosine_tab * amplitude).astype(BF16)
     table_sin = (sine_tab * amplitude).astype(BF16)
     tables = (jnp.stack([table_cos, table_sin]), jnp.stack([-table_sin, table_cos]))
@@ -506,6 +506,7 @@
     earlier = end(0, hour_part, hour_part, second_codes)
     late[2] = swap_tm(wait(late[2], *third_codes[1:6]))
     fourth_codes = back(1, 0, quarters[0][1], late[1])
+    third_codes[0] = wait(third_codes[0], *fourth_codes[1:3])
     earlier = end(1, *pieces[0], third_codes)
     fifth_codes = back(1, 0, quarters[1][1], late[2])
     earlier = end(1, *quarters[0], fourth_codes)

time: 724 us -> 718 us (level)
  starting transfers between devices: 157 us -> 143 us
  waiting for transfers between devices: 236 us -> 244 us
    all_to_all x11, starting transfers between devices: 62.7 us -> 52.3 us  [swap_tm(): return lax.all_to_all(x, 'tm', split_axis=0, concat_axis=0, tiled=True)]
    unnamed x116 -> x120, local copies, waits for them, and re-layouts: 20.6 us -> 20.6 us
  transfers between devices with their start and end apart: 109 -> 109, of which waited for: 37 -> 36; matrix products, arithmetic and copies ran while one was open for 4% -> 3% of each run, Pallas kernels for 27% -> 27%
where the time goes in v9:
time: 718 us; the launch traced here: 708 us
  waiting for transfers between devices  244 us (34%)
  Pallas kernels  198 us (28%)
  starting transfers between devices  143 us (20%)
  blocking collectives  52.4 us (7%)
  between operations  30.5 us (4%)
  local copies, waits for them, and re-layouts  26.2 us (4%)
  other arithmetic  11.7 us (2%)
    pallas_call x26, Pallas kernels, run(): pl.pallas_call(whole, name=name, grid=(grid,), out_shape=list(out_shape)...  198 us
    ppermute x91, waiting for transfers between devices, swap_lon(): lax.ppermute(parts[d], 'lon', [(i, i ^ d) for i in range(count)])  137 us
    ppermute x91, starting transfers between devices, swap_lon(): lax.ppermute(parts[d], 'lon', [(i, i ^ d) for i in range(count)])  85.4 us
    all_to_all x11, waiting for transfers between devices, swap_tm(): return lax.all_to_all(x, 'tm', split_axis=0, concat_axis=0, tiled=True)  75.2 us
    all_to_all x1, blocking collectives, swap_tm(): return lax.all_to_all(x, 'tm', split_axis=0, concat_axis=0, tiled=True)  52.4 us
    all_to_all x11, starting transfers between devices, swap_tm(): return lax.all_to_all(x, 'tm', split_axis=0, concat_axis=0, tiled=True)  52.3 us
    ppermute x3, waiting for transfers between devices, add_over_tm(): lax.ppermute(x, 'tm', [(i, i ^ d) for i in range(count)])  27.4 us
    unnamed x120, local copies, waits for them, and re-layouts  20.6 us
  transfers between devices with their start and end apart: 109, of which 36 were waited for; matrix products, arithmetic and copies ran while one was open for 3% of the time, Pallas kernels for 27%

profile of v9, /device:TPU:0, one launch (start us, length us, event | category | flops | bytes accessed | tf_op | source)
XLA Modules:
  0.0 707.8 jit_solution(12800062112926200820)
XLA Ops:
  13.8 11.3 %hourly.2 = (bf16[4,32,64,128]{3,2,1,0:T(8,128)(2,1)}, bf16[4,32,64,128]{3,2,1,0:T(8,128)(2,1)}, f32[8,128]{1,0:T(8,128)S(1)}) custom-call(bf16[2,64,128,512]{3,2,1,0:T(8,128)(2,1)} %refs_0_.3, bf16[2,256,512]{2,1,0:T(8,128)(2,1)S(1)} %get-tuple-element.332.refs_1_), custom_call_target="tpu_custom_call" | custom-call | flops 4294967296 | bytes 20971520 | tf_op jit(solution)/shard_map/hourly/pallas_call | solution.py:95
  37.0 11.2 %hourly.3 = (bf16[4,32,64,128]{3,2,1,0:T(8,128)(2,1)}, bf16[4,32,64,128]{3,2,1,0:T(8,128)(2,1)}, f32[8,128]{1,0:T(8,128)S(1)}) custom-call(bf16[2,64,128,512]{3,2,1,0:T(8,128)(2,1)} %refs_0_.3, bf16[2,256,512]{2,1,0:T(8,128)(2,1)S(1)} %get-tuple-element.333.refs_1_, f32[8,128]{1,0:T(8,128)S(1)} %get-tuple-element.165.refs_2_), custom_call_target="tpu_custom_call" | custom-call | flops 4294967296 | bytes 20971520 | tf_op jit(solution)/shard_map/hourly/pallas_call | solution.py:95
  55.1 24.5 %all-to-all-done.refs_1_ = bf16[4,32,64,128]{3,2,1,0:T(8,128)(2,1)} async-done(((bf16[4,32,64,128]{3,2,1,0:T(8,128)(2,1)}), bf16[4,32,64,128]{3,2,1,0:T(8,128)(2,1)}, u32[]{:S(2)}, u32[]{:S(2)}) %all-to-all-start) | async-done | bytes 2097184 | tf_op jit(solution)/shard_map/all_to_all | solution.py:357
  106.4 12.3 %collective-permute-done.4.refs_6_ = s16[32,32,128]{2,1,0:T(8,128)(2,1)S(1)} collective-permute-done((s16[32,32,128]{2,1,0:T(8,128)(2,1)S(1)}, s16[32,32,128]{2,1,0:T(8,128)(2,1)S(1)}, u32[]{:S(2)}, u32[]{:S(2)}) %collective-permute-start.4) | collective-permute-done | bytes 262176 | tf_op jit(solution)/shard_map/ppermute | solution.py:363
  119.6 14.8 %residual.4 = (f32[32,32,1024]{2,1,0:T(8,128)}, f32[8,128]{1,0:T(8,128)S(1)}, bf16[32,32,128]{2,1,0:T(8,128)(2,1)S(1)}, bf16[32,32,128]{2,1,0:T(8,128)(2,1)}, bf...) custom-call(f32[1]{0:T(128)} %bitcast.8.refs_0_, ...), custom_call_target="tpu_custom_call" | custom-call | flops 8589934592 | bytes 16777216 | tf_op jit(solution)/shard_map/residual/pallas_call | solution.py:95
  157.3 9.9 %collective-permute-done.18.refs_5_ = bf16[32,32,128]{2,1,0:T(8,128)(2,1)S(1)} collective-permute-done((bf16[32,32,128]{2,1,0:T(8,128)(2,1)S(1)}, bf16[32,32,128]{2,1,0:T(8,128)(2,1)S(1)}, u32[]{:S(2)}, u32[]{:S(2)}) %collective-permute-start.18) | collective-permute-done | bytes 262176 | tf_op jit(solution)/shard_map/ppermute | solution.py:363
  179.9 9.7 %all-to-all-done.2.refs_0_ = bf16[4,32,64,128]{3,2,1,0:T(8,128)(2,1)} async-done(((bf16[4,32,64,128]{3,2,1,0:T(8,128)(2,1)}), bf16[4,32,64,128]{3,2,1,0:T(8,128)(2,1)}, u32[]{:S(2)}, u32[]{:S(2)}) %all-to-all-start.2) | async-done | bytes 2097184 | tf_op jit(solution)/shard_map/all_to_all | solution.py:357
  195.0 14.8 %residual.5 = (f32[32,32,1024]{2,1,0:T(8,128)}, f32[8,128]{1,0:T(8,128)S(1)}, bf16[32,32,128]{2,1,0:T(8,128)(2,1)S(1)}, bf16[32,32,128]{2,1,0:T(8,128)(2,1)S(1)}...) custom-call(f32[1]{0:T(128)} %bitcast.8.refs_0_, ...), custom_call_target="tpu_custom_call" | custom-call | flops 34359738368 | bytes 67108864 | tf_op jit(solution)/shard_map/residual/pallas_call | solution.py:95
  263.2 14.8 %residual.6 = (f32[32,32,1024]{2,1,0:T(8,128)}, f32[8,128]{1,0:T(8,128)S(1)}, bf16[32,32,128]{2,1,0:T(8,128)(2,1)S(1)}, bf16[32,32,128]{2,1,0:T(8,128)(2,1)S(1)}...) custom-call(f32[1]{0:T(128)} %bitcast.8.refs_0_, ...), custom_call_target="tpu_custom_call" | custom-call | flops 34359738368 | bytes 67108864 | tf_op jit(solution)/shard_map/residual/pallas_call | solution.py:95
  296.1 9.7 %collective-permute-done.46.refs_5_ = bf16[32,32,128]{2,1,0:T(8,128)(2,1)S(1)} collective-permute-done((bf16[32,32,128]{2,1,0:T(8,128)(2,1)S(1)}, bf16[32,32,128]{2,1,0:T(8,128)(2,1)S(1)}, u32[]{:S(2)}, u32[]{:S(2)}) %collective-permute-start.46) | collective-permute-done | bytes 262176 | tf_op jit(solution)/shard_map/ppermute | solution.py:363
  313.9 9.5 %collective-permute-done.38.refs_5_ = s16[32,32,128]{2,1,0:T(8,128)(2,1)S(1)} collective-permute-done((s16[32,32,128]{2,1,0:T(8,128)(2,1)S(1)}, s16[32,32,128]{2,1,0:T(8,128)(2,1)S(1)}, u32[]{:S(2)}, u32[]{:S(2)}) %collective-permute-start.38) | collective-permute-done | bytes 262176 | tf_op jit(solution)/shard_map/ppermute | solution.py:363
  329.4 14.8 %residual.7 = (f32[32,32,1024]{2,1,0:T(8,128)}, f32[8,128]{1,0:T(8,128)S(1)}, bf16[32,32,128]{2,1,0:T(8,128)(2,1)S(1)}, bf16[32,32,128]{2,1,0:T(8,128)(2,1)S(1)}...) custom-call(f32[1]{0:T(128)} %bitcast.8.refs_0_, ...), custom_call_target="tpu_custom_call" | custom-call | flops 34359738368 | bytes 67108864 | tf_op jit(solution)/shard_map/residual/pallas_call | solution.py:95
  367.8 11.1 %collective-permute-done.53.refs_5_ = bf16[32,32,128]{2,1,0:T(8,128)(2,1)S(1)} collective-permute-done((bf16[32,32,128]{2,1,0:T(8,128)(2,1)S(1)}, bf16[32,32,128]{2,1,0:T(8,128)(2,1)S(1)}, u32[]{:S(2)}, u32[]{:S(2)}) %collective-permute-start.53) | collective-permute-done | bytes 262176 | tf_op jit(solution)/shard_map/ppermute | solution.py:363
  383.4 16.2 %all-to-all-done.5.refs_0_ = bf16[4,64,32,128]{3,2,1,0:T(8,128)(2,1)} async-done(((bf16[4,64,32,128]{3,2,1,0:T(8,128)(2,1)}), bf16[4,64,32,128]{3,2,1,0:T(8,128)(2,1)}, u32[]{:S(2)}, u32[]{:S(2)}) %all-to-all-start.5) | async-done | bytes 2097184 | tf_op jit(solution)/shard_map/all_to_all | solution.py:357
  399.5 52.4 %all_to_all.60.refs_1_ = bf16[4,64,32,128]{3,2,1,0:T(8,128)(2,1)} all-to-all(bf16[4,64,32,128]{3,2,1,0:T(8,128)(2,1)} %get-tuple-element.254), channel_id=1, replica_groups=mesh['tm'=4,'lon'=8] {'tm'}, dimensions={0} | all-to-all | bytes 4194304 | tf_op jit(solution)/shard_map/all_to_all | solution.py:357
  476.4 27.4 %collective-permute-done.57 = f32[4,128]{1,0:T(4,128)S(1)} collective-permute-done((f32[4,128]{1,0:T(4,128)S(1)}, f32[4,128]{1,0:T(4,128)S(1)}, u32[]{:S(2)}, u32[]{:S(2)}) %collective-permute-start.57) | collective-permute-done | bytes 2080 | tf_op jit(solution)/shard_map/ppermute | solution.py:368
  537.6 12.6 %collective-permute-done.73.refs_6_ = s16[32,32,128]{2,1,0:T(8,128)(2,1)S(1)} collective-permute-done((s16[32,32,128]{2,1,0:T(8,128)(2,1)S(1)}, s16[32,32,128]{2,1,0:T(8,128)(2,1)S(1)}, u32[]{:S(2)}, u32[]{:S(2)}) %collective-permute-start.73) | collective-permute-done | bytes 262176 | tf_op jit(solution)/shard_map/ppermute | solution.py:363
  576.5 11.8 %finish.5 = (f32[2,64,32,1024]{3,2,1,0:T(8,128)}, f32[2,64,32,1024]{3,2,1,0:T(8,128)}, f32[8,128]{1,0:T(8,128)S(1)}) custom-call(f32[2]{0:T(128)S(1)} %pad_maximum_fusion.5.refs_0_, s16[32,32,128]{2,1,0:T(8,128)(2,1)S(1)} %copy-done.11, s16[32,32,128]{2,1,0:T(8,128)(2,1)S(1)} %collective-permute-done.69.refs_2_, ...), custom_call_target="tpu_custom_call" | custom-call | flops 8589934592 | bytes 46137344 | tf_op jit(solution)/shard_map/finish/pallas_call | solution.py:95
  594.4 14.0 %all-to-all-done.9.refs_1_ = bf16[4,32,64,128]{3,2,1,0:T(8,128)(2,1)} async-done(((bf16[4,32,64,128]{3,2,1,0:T(8,128)(2,1)}), bf16[4,32,64,128]{3,2,1,0:T(8,128)(2,1)}, u32[]{:S(2)}, u32[]{:S(2)}) %all-to-all-start.9) | async-done | bytes 2097184 | tf_op jit(solution)/shard_map/all_to_all | solution.py:357
  621.9 11.9 %finish.6 = (f32[2,64,32,1024]{3,2,1,0:T(8,128)}, f32[2,64,32,1024]{3,2,1,0:T(8,128)}, f32[8,128]{1,0:T(8,128)S(1)}) custom-call(f32[2]{0:T(128)S(1)} %pad_maximum_fusion.5.refs_0_, s16[32,32,128]{2,1,0:T(8,128)(2,1)S(1)} %get-tuple-element.262.refs_1_, ...), custom_call_target="tpu_custom_call", output_to_operand_aliasing={{0}: (13, {}), {1}: (14, {})} | custom-call | flops 8589934592 | bytes 46137344 | tf_op jit(solution)/shard_map/finish/pallas_call | solution.py:95
  652.5 7.3 %collective-permute-done.82.refs_3_ = s16[16,32,128]{2,1,0:T(8,128)(2,1)S(1)} collective-permute-done((s16[16,32,128]{2,1,0:T(8,128)(2,1)S(1)}, s16[16,32,128]{2,1,0:T(8,128)(2,1)S(1)}, u32[]{:S(2)}, u32[]{:S(2)}) %collective-permute-start.82) | collective-permute-done | bytes 131104 | tf_op jit(solution)/shard_map/ppermute | solution.py:363
  663.5 11.9 %finish.7 = (f32[2,64,32,1024]{3,2,1,0:T(8,128)}, f32[2,64,32,1024]{3,2,1,0:T(8,128)}, f32[8,128]{1,0:T(8,128)S(1)}) custom-call(f32[2]{0:T(128)S(1)} %pad_maximum_fusion.4.refs_0_, s16[32,32,128]{2,1,0:T(8,128)(2,1)S(1)} %after.21.refs_1_, s16[32,32,128]{2,1,0:T(8,128)(2,1)S(1)} %collective-permute-done.76.refs_2_, ...), custom_call_target="tpu_custom_call", output_to_operand_aliasing={{0}: (13, {}), {1}: (14, {})} | custom-call | flops 8589934592 | bytes 46137344 | tf_op jit(solution)/shard_map/finish/pallas_call | solution.py:95
  684.2 7.2 %finish.8 = (f32[2,64,32,1024]{3,2,1,0:T(8,128)}, f32[2,64,32,1024]{3,2,1,0:T(8,128)}, f32[8,128]{1,0:T(8,128)S(1)}) custom-call(f32[2]{0:T(128)S(1)} %pad_maximum_fusion.4.refs_0_, s16[16,32,128]{2,1,0:T(8,128)(2,1)S(1)} %get-tuple-element.312.refs_1_, ...), custom_call_target="tpu_custom_call", output_to_operand_aliasing={{0}: (13, {}), {1}: (14, {})} | custom-call | flops 4294967296 | bytes 23068672 | tf_op jit(solution)/shard_map/finish/pallas_call | solution.py:95
  693.3 7.2 %finish.9 = (f32[2,64,32,1024]{3,2,1,0:T(8,128)}, f32[2,64,32,1024]{3,2,1,0:T(8,128)}, f32[8,128]{1,0:T(8,128)}) custom-call(f32[2]{0:T(128)S(1)} %pad_maximum_fusion.4.refs_0_, s16[16,32,128]{2,1,0:T(8,128)(2,1)S(1)} %get-tuple-element.303.refs_1_, ...), custom_call_target="tpu_custom_call", output_to_operand_aliasing={{0}: (13, {}), {1}: (14, {})} | custom-call | flops 4294967296 | bytes 23068672 | tf_op jit(solution)/shard_map/finish/pallas_call | solution.py:95
  (392 shorter events, 329.2 us)
Async XLA Ops:
  7.2 41.0 %all-gather.2.cloned.1.call-start = ((), (), s32[]{:S(2)}) async-start(), calls=%async_computation.12 | async-start | bytes 2359296 | tf_op jit(solution)/shard_map/all_gather | solution.py:411
  25.1 54.5 %all-to-all-start = ((bf16[4,32,64,128]{3,2,1,0:T(8,128)(2,1)}), bf16[4,32,64,128]{3,2,1,0:T(8,128)(2,1)}, u32[]{:S(2)}, u32[]{:S(2)}) async-start(bf16[4,32,64,128]{3,2,1,0:T(8,128)(2,1)} %get-tuple-element.164), calls=%async_computation | async-start | bytes 4194304 | tf_op jit(solution)/shard_map/all_to_all | solution.py:357
  79.6 55.4 %all-to-all-start.1 = ((bf16[4,32,64,128]{3,2,1,0:T(8,128)(2,1)}), bf16[4,32,64,128]{3,2,1,0:T(8,128)(2,1)}, u32[]{:S(2)}, u32[]{:S(2)}) async-start(bf16[4,32,64,128]{3,2,1,0:T(8,128)(2,1)} %after.11), calls=%async_computation.1 | async-start | bytes 4194304 | tf_op jit(solution)/shard_map/all_to_all | solution.py:357
  135.0 54.6 %all-to-all-start.2 = ((bf16[4,32,64,128]{3,2,1,0:T(8,128)(2,1)}), bf16[4,32,64,128]{3,2,1,0:T(8,128)(2,1)}, u32[]{:S(2)}, u32[]{:S(2)}) async-start(bf16[4,32,64,128]{3,2,1,0:T(8,128)(2,1)} %after.12), calls=%async_computation.2 | async-start | bytes 4194304 | tf_op jit(solution)/shard_map/all_to_all | solution.py:357
  167.2 27.1 %collective-permute-start.9 = (s16[32,32,128]{2,1,0:T(8,128)(2,1)S(1)}, s16[32,32,128]{2,1,0:T(8,128)(2,1)S(1)}, u32[]{:S(2)}, u32[]{:S(2)}) collective-permute-start(s16[32,32,128]{2,1,0:T(8,128)(2,1)S(1)} %get-tuple-element.182), channel_id=1, source_target_pairs={{0,3},{1,2},{2,1},{3,0},{4,7},{5,6},{6,5},{7,4},{8,11},{9,10},{10,... | collective-permute-start | bytes 786440 | tf_op jit(solution)/shard_map/ppermute | solution.py:363
  169.8 24.5 %collective-permute-start.10 = (s16[32,32,128]{2,1,0:T(8,128)(2,1)S(1)}, s16[32,32,128]{2,1,0:T(8,128)(2,1)}, u32[]{:S(2)}, u32[]{:S(2)}) collective-permute-start(s16[32,32,128]{2,1,0:T(8,128)(2,1)S(1)} %get-tuple-element.183), channel_id=1, source_target_pairs={{0,4},{1,5},{2,6},{3,7},{4,0},{5,1},{6,2},{7,3},{8,12},{9,13},{10,... | collective-permute-start | bytes 786440 | tf_op jit(solution)/shard_map/ppermute | solution.py:363
  189.6 57.0 %all-to-all-start.3 = ((bf16[4,32,64,128]{3,2,1,0:T(8,128)(2,1)}), bf16[4,32,64,128]{3,2,1,0:T(8,128)(2,1)}, u32[]{:S(2)}, u32[]{:S(2)}) async-start(bf16[4,32,64,128]{3,2,1,0:T(8,128)(2,1)} %after.14), calls=%async_computation.3 | async-start | bytes 4194304 | tf_op jit(solution)/shard_map/all_to_all | solution.py:357
  213.5 25.0 %collective-permute-start.33 = (bf16[32,32,128]{2,1,0:T(8,128)(2,1)S(1)}, bf16[32,32,128]{2,1,0:T(8,128)(2,1)S(1)}, u32[]{:S(2)}, u32[]{:S(2)}) collective-permute-start(bf16[32,32,128]{2,1,0:T(8,128)(2,1)S(1)} %get-tuple-element.215), channel_id=1, source_target_pairs={{0,6},{1,7},{2,4},{3,5},{4,2},{5,3},{6,0},{7,1},{8,14},{9,15},{10,... | collective-permute-start | bytes 786440 | tf_op jit(solution)/shard_map/ppermute | solution.py:363
  246.7 99.4 %all-to-all-start.4 = ((bf16[4,64,64,128]{3,2,1,0:T(8,128)(2,1)}), bf16[4,64,64,128]{3,2,1,0:T(8,128)(2,1)}, u32[]{:S(2)}, u32[]{:S(2)}) async-start(bf16[4,64,64,128]{3,2,1,0:T(8,128)(2,1)} %after.15), calls=%async_computation.4 | async-start | bytes 8388608 | tf_op jit(solution)/shard_map/all_to_all | solution.py:357
  258.1 24.1 %collective-permute-start.36 = (s16[32,32,128]{2,1,0:T(8,128)(2,1)S(1)}, s16[32,32,128]{2,1,0:T(8,128)(2,1)S(1)}, u32[]{:S(2)}, u32[]{:S(2)}) collective-permute-start(s16[32,32,128]{2,1,0:T(8,128)(2,1)S(1)} %get-tuple-element.224), channel_id=1, source_target_pairs={{0,2},{1,3},{2,0},{3,1},{4,6},{5,7},{6,4},{7,5},{8,10},{9,11},{10,... | collective-permute-start | bytes 786440 | tf_op jit(solution)/shard_map/ppermute | solution.py:363
  282.6 25.5 %collective-permute-start.47 = (bf16[32,32,128]{2,1,0:T(8,128)(2,1)S(1)}, bf16[32,32,128]{2,1,0:T(8,128)(2,1)S(1)}, u32[]{:S(2)}, u32[]{:S(2)}) collective-permute-start(bf16[32,32,128]{2,1,0:T(8,128)(2,1)S(1)} %get-tuple-element.236), channel_id=1, source_target_pairs={{0,6},{1,7},{2,4},{3,5},{4,2},{5,3},{6,0},{7,1},{8,14},{9,15},{10,... | collective-permute-start | bytes 786440 | tf_op jit(solution)/shard_map/ppermute | solution.py:363
  294.6 28.8 %collective-permute-start.38 = (s16[32,32,128]{2,1,0:T(8,128)(2,1)S(1)}, s16[32,32,128]{2,1,0:T(8,128)(2,1)S(1)}, u32[]{:S(2)}, u32[]{:S(2)}) collective-permute-start(s16[32,32,128]{2,1,0:T(8,128)(2,1)S(1)} %get-tuple-element.226), channel_id=1, source_target_pairs={{0,4},{1,5},{2,6},{3,7},{4,0},{5,1},{6,2},{7,3},{8,12},{9,13},{10,... | collective-permute-start | bytes 786440 | tf_op jit(solution)/shard_map/ppermute | solution.py:363
  346.1 53.5 %all-to-all-start.5 = ((bf16[4,64,32,128]{3,2,1,0:T(8,128)(2,1)}), bf16[4,64,32,128]{3,2,1,0:T(8,128)(2,1)}, u32[]{:S(2)}, u32[]{:S(2)}) async-start(bf16[4,64,32,128]{3,2,1,0:T(8,128)(2,1)} %after.16), calls=%async_computation.5 | async-start | bytes 4194304 | tf_op jit(solution)/shard_map/all_to_all | solution.py:357
  451.9 52.0 %all-to-all-start.8 = ((bf16[4,32,64,128]{3,2,1,0:T(8,128)(2,1)}), bf16[4,32,64,128]{3,2,1,0:T(8,128)(2,1)}, u32[]{:S(2)}, u32[]{:S(2)}) async-start(bf16[4,32,64,128]{3,2,1,0:T(8,128)(2,1)} %get-tuple-element.260), calls=%async_computation.8 | async-start | bytes 4194304 | tf_op jit(solution)/shard_map/all_to_all | solution.py:357
  472.0 31.8 %collective-permute-start.57 = (f32[4,128]{1,0:T(4,128)S(1)}, f32[4,128]{1,0:T(4,128)S(1)}, u32[]{:S(2)}, u32[]{:S(2)}) collective-permute-start(f32[4,128]{1,0:T(4,128)S(1)} %broadcast_in_dim.28), channel_id=1, source_target_pairs={{0,16},{8,24},{16,0},{24,8},{1,17},{9,25},{17,1},{25,9},{2,18},{10... | collective-permute-start | bytes 6152 | tf_op jit(solution)/shard_map/ppermute | solution.py:368
  474.9 28.9 %collective-permute-start.58 = (f32[4,128]{1,0:T(4,128)S(1)}, f32[4,128]{1,0:T(4,128)S(1)}, u32[]{:S(2)}, u32[]{:S(2)}) collective-permute-start(f32[4,128]{1,0:T(4,128)S(1)} %broadcast_in_dim.28), channel_id=1, source_target_pairs={{0,24},{8,16},{16,8},{24,0},{1,25},{9,17},{17,9},{25,1},{2,26},{10... | collective-permute-start | bytes 6152 | tf_op jit(solution)/shard_map/ppermute | solution.py:368
  476.4 27.4 %collective-permute-start.56 = (f32[4,128]{1,0:T(4,128)S(1)}, f32[4,128]{1,0:T(4,128)S(1)}, u32[]{:S(2)}, u32[]{:S(2)}) collective-permute-start(f32[4,128]{1,0:T(4,128)S(1)} %broadcast_in_dim.28), channel_id=1, source_target_pairs={{0,8},{8,0},{16,24},{24,16},{1,9},{9,1},{17,25},{25,17},{2,10},{10... | collective-permute-start | bytes 6152 | tf_op jit(solution)/shard_map/ppermute | solution.py:368
  503.9 52.3 %all-to-all-start.7 = ((bf16[4,32,64,128]{3,2,1,0:T(8,128)(2,1)}), bf16[4,32,64,128]{3,2,1,0:T(8,128)(2,1)}, u32[]{:S(2)}, u32[]{:S(2)}) async-start(bf16[4,32,64,128]{3,2,1,0:T(8,128)(2,1)} %after.17), calls=%async_computation.7 | async-start | bytes 4194304 | tf_op jit(solution)/shard_map/all_to_all | solution.py:357
  556.3 52.2 %all-to-all-start.9 = ((bf16[4,32,64,128]{3,2,1,0:T(8,128)(2,1)}), bf16[4,32,64,128]{3,2,1,0:T(8,128)(2,1)}, u32[]{:S(2)}, u32[]{:S(2)}) async-start(bf16[4,32,64,128]{3,2,1,0:T(8,128)(2,1)} %after.18), calls=%async_computation.9 | async-start | bytes 4194304 | tf_op jit(solution)/shard_map/all_to_all | solution.py:357
  570.0 24.4 %collective-permute-start.66 = (s16[32,32,128]{2,1,0:T(8,128)(2,1)}, s16[32,32,128]{2,1,0:T(8,128)(2,1)S(1)}, u32[]{:S(2)}, u32[]{:S(2)}) collective-permute-start(s16[32,32,128]{2,1,0:T(8,128)(2,1)} %get-tuple-element.267), channel_id=1, source_target_pairs={{0,5},{1,4},{2,7},{3,6},{4,1},{5,0},{6,3},{7,2},{8,13},{9,12},{10,... | collective-permute-start | bytes 786440 | tf_op jit(solution)/shard_map/ppermute | solution.py:363
  608.5 29.8 %all-to-all-start.11 = ((bf16[4,16,64,128]{3,2,1,0:T(8,128)(2,1)}), bf16[4,16,64,128]{3,2,1,0:T(8,128)(2,1)}, u32[]{:S(2)}, u32[]{:S(2)}) async-start(bf16[4,16,64,128]{3,2,1,0:T(8,128)(2,1)} %after.20), calls=%async_computation.11 | async-start | bytes 2097152 | tf_op jit(solution)/shard_map/all_to_all | solution.py:357
  638.2 37.2 %all-to-all-start.10 = ((bf16[4,16,64,128]{3,2,1,0:T(8,128)(2,1)}), bf16[4,16,64,128]{3,2,1,0:T(8,128)(2,1)}, u32[]{:S(2)}, u32[]{:S(2)}) async-start(bf16[4,16,64,128]{3,2,1,0:T(8,128)(2,1)} %after.19), calls=%async_computation.10 | async-start | bytes 2097152 | tf_op jit(solution)/shard_map/all_to_all | solution.py:357
  651.0 26.7 %collective-permute-start.92 = (s16[16,32,128]{2,1,0:T(8,128)(2,1)}, s16[16,32,128]{2,1,0:T(8,128)(2,1)S(1)}, u32[]{:S(2)}, u32[]{:S(2)}) collective-permute-start(s16[16,32,128]{2,1,0:T(8,128)(2,1)} %get-tuple-element.313), channel_id=1, source_target_pairs={{0,3},{1,2},{2,1},{3,0},{4,7},{5,6},{6,5},{7,4},{8,11},{9,10},{10,... | collective-permute-start | bytes 393224 | tf_op jit(solution)/shard_map/ppermute | solution.py:363
  651.9 26.0 %collective-permute-start.93 = (s16[16,32,128]{2,1,0:T(8,128)(2,1)}, s16[16,32,128]{2,1,0:T(8,128)(2,1)S(1)}, u32[]{:S(2)}, u32[]{:S(2)}) collective-permute-start(s16[16,32,128]{2,1,0:T(8,128)(2,1)} %get-tuple-element.314), channel_id=1, source_target_pairs={{0,4},{1,5},{2,6},{3,7},{4,0},{5,1},{6,2},{7,3},{8,12},{9,13},{10,... | collective-permute-start | bytes 393224 | tf_op jit(solution)/shard_map/ppermute | solution.py:363
  (140 other events, 1681.8 us)
Sparse Core Ops, SparseCore 0:
  9.9 30.9 all-gather.1
